TPU v7x, 32 devices: a whole 2x2x4 slice. The times are simulated.
32 devices in a mesh: dp: 8 (over z, y), tensor: 4 (over x, core).
Axes of the slice: x: 2, y: 2, z: 4, core: 2. Of those that a mesh axis runs over, the one named last changes fastest.
Arguments:
- source: bfloat16 [8, 1024, 512], P('dp', 'tensor'), may hold values from -6 to 6
- target: bfloat16 [8, 1024, 512], P('dp', 'tensor'), may hold values from -6 to 6
- out_grad: bfloat16 [8, 1024, 512], P('dp', 'tensor'), may hold values from -6 to 6
- src_len: int32 [8], P('dp'), may hold values from 1 to 1024, 5120 in all
- tgt_len: int32 [8], P('dp'), may hold values from 1 to 1024, 5120 in all
- owners: int32 [4, 56], P('tensor'), may hold values from 0 to 7, as said below
- master: float32 [4, 64, 64, 512], P('tensor', 'dp'), may hold values from -4 to 4
- rotated_first_moment: float32 [4, 64, 64, 512], P('tensor', 'dp'), may hold values from -40 to 40
- rotated_second_moment: float32 [4, 64, 64, 512], P('tensor', 'dp'), may hold values from 4.096 to 16.384
- stat_left: float32 [4, 64, 64, 64], P('tensor', 'dp'), may hold values from -104857.6 to 461373.44, as said below
- stat_right: float32 [4, 64, 512, 512], P('tensor', 'dp'), may hold values from -13107.2 to 57671.68, as said below
- basis_left: float32 [4, 64, 64, 64], P('tensor', 'dp'), may hold values from -1 to 1, as said below
- basis_right: float32 [4, 64, 512, 512], P('tensor', 'dp'), may hold values from -1 to 1, as said below
- norm_params: float32 [2, 5, 512], replicated, may hold values from -0.3 to 1.4
- norm_one: float32 [2, 5, 512], replicated, may hold values from -40 to 40
- norm_two: float32 [2, 5, 512], replicated, may hold values from 4.096 to 16.384
Outputs:
- decoded: bfloat16 [8, 1024, 512], P('dp', 'tensor')
- src_grad: float32 [8, 1024, 512], P('dp', 'tensor')
- tgt_grad: float32 [8, 1024, 512], P('dp', 'tensor')
- master_new: float32 [4, 64, 64, 512], P('tensor', 'dp')
- moment_one_new: float32 [4, 64, 64, 512], P('tensor', 'dp')
- moment_two_new: float32 [4, 64, 64, 512], P('tensor', 'dp')
- stat_left_new: float32 [4, 64, 64, 64], P('tensor', 'dp')
- stat_right_new: float32 [4, 64, 512, 512], P('tensor', 'dp')
- basis_left_new: float32 [4, 64, 64, 64], P('tensor', 'dp')
- basis_right_new: float32 [4, 64, 512, 512], P('tensor', 'dp')
- copies_new: bfloat16 [4, 64, 64, 512], P('tensor', 'dp')
- norm_new: float32 [2, 5, 512], replicated
- norm_one_new: float32 [2, 5, 512], replicated
- norm_two_new: float32 [2, 5, 512], replicated
Inputs may be any that keep to these rules, and one draw needn't show every extreme that they name: `src_len`: the lengths of all 8 sources sum to 5120; some source is 1024 long. `tgt_len`: the lengths of all 8 targets sum to 5120; some target is 1024 long. `owners`: in each tensor index, no owner holds more than 8 blocks, and some owner holds exactly 8. `stat_left`: symmetric positive definite. `stat_right`: symmetric positive definite. `basis_left`: orthogonal to float32 rounding. `basis_right`: orthogonal to float32 rounding.
All inputs are finite; a program needn't handle non-finite values. No bound on the sum of `src_len` or of `tgt_len` on one device may be relied on, other than what follows from the above.
Results may differ from a plain program's by a relative error of at most 0.033.
Values may be sent and summed in bfloat16 or wider, within the bound.
No kernel may reach another device: no remote copies, remote signals or barrier semaphores. Data moves between devices by JAX's collectives and lax.ppermute only.
A program may use at most 192 MiB of HBM per device.

v0:
```python
import jax
import jax.numpy as jnp
from jax import lax
from jax.sharding import PartitionSpec as P

HEADS = 8
STEP = 10
FFB = 32


highest = lax.Precision.HIGHEST
rate_matrix = 0.3
rate_vector = 0.6


def slot_positions(owner_row, capacity):
    block_ids = jnp.arange(owner_row.shape[0], dtype=jnp.int32)
    same_owner = (owner_row[:, None] == owner_row[None, :]).astype(jnp.int32)
    earlier = (block_ids[None, :] < block_ids[:, None]).astype(jnp.int32)
    rank_of = jnp.sum(same_owner * earlier, axis=1)
    return owner_row * capacity + rank_of


def layer_norm(values, norm_gain, norm_shift):
    center = values - jnp.mean(values, axis=-1, keepdims=True)
    spread = jnp.mean(center * center, axis=-1, keepdims=True)
    return center * lax.rsqrt(spread + 1e-05) * norm_gain + norm_shift


def project(rows_b, matrix):
    return jnp.einsum("sd,kd->sk", rows_b, matrix, preferred_element_type=jnp.float32)


def gather_rows(rows_b):
    return lax.all_gather(rows_b, "tensor", axis=0, tiled=True)


def scatter_rows(term_fn, row_count):
    return lax.psum_scatter(
        term_fn(jnp.int32(0), row_count * lax.axis_size("tensor")).astype(jnp.bfloat16),
        "tensor",
        scatter_dimension=0,
        tiled=True,
    ).astype(jnp.float32)


def gather_grads(rows_b):
    return lax.all_gather(rows_b, "tensor", axis=0, tiled=True)


def scatter_grads(term_fn, row_count):
    return lax.psum_scatter(
        term_fn(jnp.int32(0), row_count * lax.axis_size("tensor")).astype(jnp.bfloat16),
        "tensor",
        scatter_dimension=0,
        tiled=True,
    ).astype(jnp.float32)


def attention_scores(query_b, key_b, allowed):
    score_scale = query_b.shape[-1] ** (-0.5)
    scores = (
        jnp.einsum("qhe,khe->hqk", query_b, key_b, preferred_element_type=jnp.float32) * score_scale
    )
    return jnp.where(allowed[None], scores, -1e30)


def attention_forward(query_rows, key_rows, weights_four, allowed, head_count, row_count):
    w_query, w_key, w_value, w_out = weights_four
    q_len = query_rows.shape[0]
    k_len = key_rows.shape[0]
    query_b = project(query_rows, w_query).astype(jnp.bfloat16).reshape(q_len, head_count, -1)
    key_b = project(key_rows, w_key).astype(jnp.bfloat16).reshape(k_len, head_count, -1)
    value_b = project(key_rows, w_value).astype(jnp.bfloat16).reshape(k_len, head_count, -1)
    scores = attention_scores(query_b, key_b, allowed)
    top_score = jnp.max(scores, axis=-1, keepdims=True)
    powers = jnp.exp(scores - top_score)
    row_sum = jnp.sum(powers, axis=-1, keepdims=True)
    chance = powers / row_sum
    log_total = top_score + jnp.log(row_sum)
    mixed = jnp.einsum(
        "hqk,khe->qhe", chance.astype(jnp.bfloat16), value_b, preferred_element_type=jnp.float32
    )
    mixed_b = mixed.astype(jnp.bfloat16).reshape(q_len, -1)

    def attention_out_term(row_start, row_total):
        return jnp.dot(mixed_b, w_out, preferred_element_type=jnp.float32)

    branch = scatter_rows(attention_out_term, row_count)
    return (branch, (query_b, key_b, value_b, log_total, mixed_b))


def attention_backward(
    grad_own, saved, weights_four, query_rows, key_rows, allowed, row_count, same_rows
):
    w_query, w_key, w_value, w_out = weights_four
    query_b, key_b, value_b, log_total, mixed_b = saved
    q_len = query_rows.shape[0]
    k_len = key_rows.shape[0]
    grad_full_b = gather_grads(grad_own.astype(jnp.bfloat16))
    grad_mixed_b = jnp.einsum("sd,kd->sk", grad_full_b, w_out, preferred_element_type=jnp.float32)
    grad_mixed_b = grad_mixed_b.astype(jnp.bfloat16).reshape(query_b.shape)
    grad_out_w = jnp.einsum("sk,sd->kd", mixed_b, grad_full_b, preferred_element_type=jnp.float32)
    scores = attention_scores(query_b, key_b, allowed)
    chance = jnp.exp(scores - log_total)
    grad_value = jnp.einsum(
        "hqk,qhe->khe",
        chance.astype(jnp.bfloat16),
        grad_mixed_b,
        preferred_element_type=jnp.float32,
    )
    grad_chance = jnp.einsum(
        "qhe,khe->hqk", grad_mixed_b, value_b, preferred_element_type=jnp.float32
    )
    inner = jnp.sum(chance * grad_chance, axis=-1, keepdims=True)
    grad_score_b = (chance * (grad_chance - inner)).astype(jnp.bfloat16)
    score_scale = query_b.shape[-1] ** (-0.5)
    grad_query = (
        jnp.einsum("hqk,khe->qhe", grad_score_b, key_b, preferred_element_type=jnp.float32)
        * score_scale
    )
    grad_key = (
        jnp.einsum("hqk,qhe->khe", grad_score_b, query_b, preferred_element_type=jnp.float32)
        * score_scale
    )
    grad_query_b = grad_query.astype(jnp.bfloat16).reshape(q_len, -1)
    grad_key_b = grad_key.astype(jnp.bfloat16).reshape(k_len, -1)
    grad_value_b = grad_value.astype(jnp.bfloat16).reshape(k_len, -1)
    grad_weights = [
        jnp.einsum("sk,sd->kd", grad_query_b, query_rows, preferred_element_type=jnp.float32),
        jnp.einsum("sk,sd->kd", grad_key_b, key_rows, preferred_element_type=jnp.float32),
        jnp.einsum("sk,sd->kd", grad_value_b, key_rows, preferred_element_type=jnp.float32),
        grad_out_w,
    ]

    def attention_input_term(row_start, row_total):
        part_query = jnp.dot(grad_query_b, w_query, preferred_element_type=jnp.float32)
        part_key = jnp.dot(grad_key_b, w_key, preferred_element_type=jnp.float32)
        part_key = part_key + jnp.dot(grad_value_b, w_value, preferred_element_type=jnp.float32)
        if same_rows:
            return part_query + part_key
        return jnp.concatenate([part_query, part_key], axis=1)

    return (grad_weights, scatter_grads(attention_input_term, row_count))


def feed_forward(input_rows, w_in, w_down, row_count):
    hidden = project(input_rows, w_in)
    active_b = jax.nn.gelu(hidden, approximate=False).astype(jnp.bfloat16)

    def feed_out_term(row_start, row_total):
        return jnp.dot(active_b, w_down, preferred_element_type=jnp.float32)

    return (scatter_rows(feed_out_term, row_count), (hidden, active_b))


def feed_backward(grad_own, saved, w_in, w_down, input_rows, row_count):
    hidden, active_b = saved
    grad_full_b = gather_grads(grad_own.astype(jnp.bfloat16))
    grad_active = jnp.einsum("sd,kd->sk", grad_full_b, w_down, preferred_element_type=jnp.float32)
    grad_hidden = jax.vjp(lambda inner_value: jax.nn.gelu(inner_value, approximate=False), hidden)[
        1
    ](grad_active)[0]
    grad_hidden_b = grad_hidden.astype(jnp.bfloat16)
    grad_down = jnp.einsum("sk,sd->kd", active_b, grad_full_b, preferred_element_type=jnp.float32)
    grad_in = jnp.einsum("sk,sd->kd", grad_hidden_b, input_rows, preferred_element_type=jnp.float32)

    def feed_input_term(row_start, row_total):
        return jnp.dot(grad_hidden_b, w_in, preferred_element_type=jnp.float32)

    return ([grad_in, grad_down], scatter_grads(feed_input_term, row_count))


def renew_basis(matrix):
    gram_matrix = jnp.dot(matrix.T, matrix, precision=highest)
    lower_factor = jnp.linalg.cholesky(gram_matrix)
    return jax.scipy.linalg.solve_triangular(lower_factor, matrix.T, lower=True).T


def update_slot(inputs):
    (
        grad_block,
        weight,
        first_moment,
        second_moment,
        left_stat,
        right_stat,
        left_basis,
        right_basis,
    ) = inputs
    fix_one = 1.0 - 0.9**STEP
    fix_two = 1.0 - 0.999**STEP
    turned = jnp.dot(
        jnp.dot(left_basis.T, grad_block, precision=highest), right_basis, precision=highest
    )
    first_new = 0.9 * first_moment + 0.1 * turned
    second_new = 0.999 * second_moment + 0.001 * turned * turned
    direction = first_new / fix_one / (jnp.sqrt(second_new / fix_two) + 1e-08)
    update = jnp.dot(
        jnp.dot(left_basis, direction, precision=highest), right_basis.T, precision=highest
    )
    weight_new = weight - rate_matrix * (update + 0.01 * weight)
    left_new = 0.95 * left_stat + 0.05 * jnp.dot(grad_block, grad_block.T, precision=highest)
    right_new = 0.95 * right_stat + 0.05 * jnp.dot(grad_block.T, grad_block, precision=highest)
    left_basis_new = renew_basis(jnp.dot(left_new, left_basis, precision=highest))
    right_basis_new = renew_basis(jnp.dot(right_new, right_basis, precision=highest))
    return (
        weight_new,
        first_new,
        second_new,
        left_new,
        right_new,
        left_basis_new,
        right_basis_new,
        weight_new.astype(jnp.bfloat16),
    )


def per_device(
    source,
    target,
    out_grad,
    src_len,
    tgt_len,
    owners,
    master,
    rotated_first_moment,
    rotated_second_moment,
    stat_left,
    stat_right,
    basis_left,
    basis_right,
    norm_params,
    norm_one,
    norm_two,
):
    tensor_count = lax.axis_size("tensor")
    head_count = HEADS // tensor_count
    col_count = FFB // tensor_count
    capacity = master.shape[1]
    slot_count = capacity * lax.axis_size("dp")
    row_count = source.shape[1]
    seq_full = row_count * tensor_count
    block_rows = master.shape[2]
    width = master.shape[3]
    gathered = lax.all_gather(master.astype(jnp.bfloat16), "dp", axis=1, tiled=True)
    slot_of = slot_positions(owners[0], capacity)
    blocks = gathered[0][slot_of]
    extents = [head_count] * 4 + [col_count] * 2 + [head_count] * 8 + [col_count] * 2
    matrices = []
    offset = 0
    for extent in extents:
        matrices.append(blocks[offset : offset + extent].reshape(extent * block_rows, width))
        offset += extent
    positions = lax.iota(jnp.int32, seq_full)
    own_positions = lax.axis_index("tensor") * row_count + lax.iota(jnp.int32, row_count)
    gains = norm_params[0]
    shifts = norm_params[1]

    def pair_step(totals, inputs):
        src_own, tgt_own, cot_own, src_size, tgt_size = inputs
        enc_allowed = jnp.broadcast_to(positions[None, :] < src_size, (seq_full, seq_full))
        dec_allowed = (positions[None, :] <= positions[:, None]) & (positions[None, :] < tgt_size)
        keep_rows = (own_positions < tgt_size).astype(jnp.float32)[:, None]
        src_full = gather_rows(src_own)
        branch_one, saved_one = attention_forward(
            src_full, src_full, matrices[0:4], enc_allowed, head_count, row_count
        )
        z_one = src_own.astype(jnp.float32) + branch_one
        h_one, pull_one = jax.vjp(layer_norm, z_one, gains[0], shifts[0])
        h_one_full = gather_rows(h_one.astype(jnp.bfloat16))
        branch_two, saved_two = feed_forward(h_one_full, matrices[4], matrices[5], row_count)
        z_two = h_one + branch_two
        encoded, pull_two = jax.vjp(layer_norm, z_two, gains[1], shifts[1])
        enc_full = gather_rows(encoded.astype(jnp.bfloat16))
        tgt_full = gather_rows(tgt_own)
        branch_three, saved_three = attention_forward(
            tgt_full, tgt_full, matrices[6:10], dec_allowed, head_count, row_count
        )
        z_three = tgt_own.astype(jnp.float32) + branch_three
        g_one, pull_three = jax.vjp(layer_norm, z_three, gains[2], shifts[2])
        g_one_full = gather_rows(g_one.astype(jnp.bfloat16))
        branch_four, saved_four = attention_forward(
            g_one_full, enc_full, matrices[10:14], enc_allowed, head_count, row_count
        )
        z_four = g_one + branch_four
        g_two, pull_four = jax.vjp(layer_norm, z_four, gains[3], shifts[3])
        g_two_full = gather_rows(g_two.astype(jnp.bfloat16))
        branch_five, saved_five = feed_forward(g_two_full, matrices[14], matrices[15], row_count)
        z_five = g_two + branch_five
        normed, pull_five = jax.vjp(layer_norm, z_five, gains[4], shifts[4])
        decoded_own = (normed * keep_rows).astype(jnp.bfloat16)
        grad_z_five, gain_five, shift_five = pull_five(cot_own.astype(jnp.float32) * keep_rows)
        weights_five, rows_five = feed_backward(
            grad_z_five, saved_five, matrices[14], matrices[15], g_two_full, row_count
        )
        grad_z_four, gain_four, shift_four = pull_four(grad_z_five + rows_five)
        weights_four, rows_four = attention_backward(
            grad_z_four,
            saved_four,
            matrices[10:14],
            g_one_full,
            enc_full,
            enc_allowed,
            row_count,
            False,
        )
        grad_g_one = grad_z_four + rows_four[:, :width]
        grad_encoded = rows_four[:, width:]
        grad_z_three, gain_three, shift_three = pull_three(grad_g_one)
        weights_three, rows_three = attention_backward(
            grad_z_three,
            saved_three,
            matrices[6:10],
            tgt_full,
            tgt_full,
            dec_allowed,
            row_count,
            True,
        )
        tgt_grad_own = grad_z_three + rows_three
        grad_z_two, gain_two, shift_two = pull_two(grad_encoded)
        weights_two, rows_two = feed_backward(
            grad_z_two, saved_two, matrices[4], matrices[5], h_one_full, row_count
        )
        grad_z_one, gain_one, shift_one = pull_one(grad_z_two + rows_two)
        weights_one, rows_one = attention_backward(
            grad_z_one, saved_one, matrices[0:4], src_full, src_full, enc_allowed, row_count, True
        )
        src_grad_own = grad_z_one + rows_one
        grad_list = weights_one + weights_two + weights_three + weights_four + weights_five
        grad_blocks = jnp.concatenate(
            [grad_item.reshape(-1, block_rows, width) for grad_item in grad_list], axis=0
        )
        grad_norms = jnp.stack(
            [
                jnp.stack([gain_one, gain_two, gain_three, gain_four, gain_five]),
                jnp.stack([shift_one, shift_two, shift_three, shift_four, shift_five]),
            ]
        )
        return (
            (totals[0] + grad_blocks, totals[1] + grad_norms),
            (decoded_own, src_grad_own, tgt_grad_own),
        )

    start_totals = (jnp.zeros(blocks.shape, jnp.float32), jnp.zeros(norm_params.shape, jnp.float32))
    totals, stacked = lax.scan(
        pair_step, start_totals, (source, target, out_grad, src_len, tgt_len)
    )
    decoded, src_grad, tgt_grad = stacked
    block_grad, norm_local = totals
    summed = lax.psum(block_grad.astype(jnp.bfloat16), "dp").astype(jnp.float32)
    buffer = jnp.zeros((slot_count, block_rows, width), jnp.float32).at[slot_of].set(summed)
    own_grad = lax.dynamic_slice_in_dim(buffer, lax.axis_index("dp") * capacity, capacity, 0)
    norm_grad = lax.psum(norm_local, ("dp", "tensor"))
    results = lax.map(
        update_slot,
        (
            own_grad,
            master[0],
            rotated_first_moment[0],
            rotated_second_moment[0],
            stat_left[0],
            stat_right[0],
            basis_left[0],
            basis_right[0],
        ),
    )
    fix_one = 1.0 - 0.9**STEP
    fix_two = 1.0 - 0.999**STEP
    norm_one_new = 0.9 * norm_one + 0.1 * norm_grad
    norm_two_new = 0.999 * norm_two + 0.001 * norm_grad * norm_grad
    norm_new = norm_params - rate_vector * (norm_one_new / fix_one) / (
        jnp.sqrt(norm_two_new / fix_two) + 1e-08
    )
    return (
        decoded,
        src_grad,
        tgt_grad,
        results[0][None],
        results[1][None],
        results[2][None],
        results[3][None],
        results[4][None],
        results[5][None],
        results[6][None],
        results[7][None],
        norm_new,
        norm_one_new,
        norm_two_new,
    )


def solution(mesh):
    in_specs = (
        P("dp", "tensor", None),
        P("dp", "tensor", None),
        P("dp", "tensor", None),
        P("dp"),
        P("dp"),
        P("tensor", None),
        P("tensor", "dp", None, None),
        P("tensor", "dp", None, None),
        P("tensor", "dp", None, None),
        P("tensor", "dp", None, None),
        P("tensor", "dp", None, None),
        P("tensor", "dp", None, None),
        P("tensor", "dp", None, None),
        P(),
        P(),
        P(),
    )
    out_specs = (
        P("dp", "tensor", None),
        P("dp", "tensor", None),
        P("dp", "tensor", None),
        P("tensor", "dp", None, None),
        P("tensor", "dp", None, None),
        P("tensor", "dp", None, None),
        P("tensor", "dp", None, None),
        P("tensor", "dp", None, None),
        P("tensor", "dp", None, None),
        P("tensor", "dp", None, None),
        P("tensor", "dp", None, None),
        P(),
        P(),
        P(),
    )
    return jax.shard_map(
        per_device, mesh=mesh, in_specs=in_specs, out_specs=out_specs, check_vma=False
    )
```

profile of v0, /device:TPU:0, one launch (start us, length us, event | category | flops | bytes accessed | tf_op | source)
XLA Modules:
  0.0 2221.2 jit_solution(6974611714285123348)
XLA Ops:
  12.4 74.4 %all-gather.15.cloned.1.call-done = bf16[1,64,64,512]{3,2,0,1:T(8,128)(2,1)} async-done(((bf16[1,8,64,512]{3,2,0,1:T(8,128)(2,1)}), bf16[1,64,64,512]{3,2,0,1:T(8,128)(2,1)}) %all-gather.15.cloned.1.call-update) | async-done | bytes 4194320 | tf_op jit(solution)/shard_map/all_gather | solution.py:246
  131.7 17.9 reduce-scatter.13.cloned.1.call-done
  180.9 17.9 reduce-scatter.11.cloned.1.call-done
  202.9 23.8 %reduce-scatter.15.cloned.1.call-done = bf16[256,512]{1,0:T(8,128)(2,1)} async-done(((bf16[1024,512]{1,0:T(8,128)(2,1)}), bf16[256,512]{1,0:T(8,128)(2,1)}) %reduce-scatter.15.cloned.1.call-update) | async-done | bytes 262160 | tf_op jit(solution)/shard_map/while/body/eval_jaxpr/reduce_scatter | solution.py:39
  229.2 16.5 all-gather.21.cloned.1.call-done
  247.4 17.3 all-gather.19.cloned.1.call-done
  275.9 24.6 %reduce-scatter.17.cloned.1.call-done = bf16[256,512]{1,0:T(8,128)(2,1)} async-done(((bf16[1024,512]{1,0:T(8,128)(2,1)}), bf16[256,512]{1,0:T(8,128)(2,1)}) %reduce-scatter.17.cloned.1.call-update) | async-done | bytes 262160 | tf_op jit(solution)/shard_map/while/body/eval_jaxpr/reduce_scatter | solution.py:39
  304.8 16.8 all-gather.23.cloned.1.call-done
  332.5 24.5 %reduce-scatter.19.cloned.1.call-done = bf16[256,512]{1,0:T(8,128)(2,1)} async-done(((bf16[1024,512]{1,0:T(8,128)(2,1)}), bf16[256,512]{1,0:T(8,128)(2,1)}) %reduce-scatter.19.cloned.1.call-update) | async-done | bytes 262160 | tf_op jit(solution)/shard_map/while/body/eval_jaxpr/reduce_scatter | solution.py:39
  363.8 16.8 all-gather.25.cloned.1.call-done
  387.4 25.0 %reduce-scatter.21.cloned.1.call-done = bf16[256,512]{1,0:T(8,128)(2,1)} async-done(((bf16[1024,512]{1,0:T(8,128)(2,1)}), bf16[256,512]{1,0:T(8,128)(2,1)}) %reduce-scatter.21.cloned.1.call-update) | async-done | bytes 262160 | tf_op jit(solution)/shard_map/while/body/eval_jaxpr/reduce_scatter | solution.py:52
  419.2 15.9 all-gather.27.cloned.1.call-done
  454.5 31.5 %reduce-scatter.23.cloned.1.call-done = bf16[256,1024]{1,0:T(8,128)(2,1)} async-done(((bf16[1024,1024]{1,0:T(8,128)(2,1)}), bf16[256,1024]{1,0:T(8,128)(2,1)}) %reduce-scatter.23.cloned.1.call-update) | async-done | bytes 524304 | tf_op jit(solution)/shard_map/while/body/eval_jaxpr/reduce_scatter | solution.py:52
  492.2 16.8 all-gather.29.cloned.1.call-done
  516.5 24.3 %reduce-scatter.25.cloned.1.call-done = bf16[256,512]{1,0:T(8,128)(2,1)} async-done(((bf16[1024,512]{1,0:T(8,128)(2,1)}), bf16[256,512]{1,0:T(8,128)(2,1)}) %reduce-scatter.25.cloned.1.call-update) | async-done | bytes 262160 | tf_op jit(solution)/shard_map/while/body/eval_jaxpr/reduce_scatter | solution.py:52
  621.6 40.2 %psum.15 = f32[2,5,512]{2,1,0:T(8,128)S(1)} all-reduce(f32[2,5,512]{2,1,0:T(8,128)S(1)} %pad_maximum_fusion.1), channel_id=1, replica_groups=mesh['dp'=8,'tensor'=4] {'dp','tensor'}, use_global_device_ids=true, to_apply=%region_64.65 | all-reduce | flops 5120 | bytes 40960 | tf_op jit(solution)/shard_map/psum | solution.py:355
  667.5 117.8 %all-reduce.3.cloned.1.call-done = bf16[56,64,512]{2,1,0:T(8,128)(2,1)} async-done(((bf16[56,64,512]{2,1,0:T(8,128)(2,1)}), bf16[56,64,512]{2,1,0:T(8,128)(2,1)}) %all-reduce.3.cloned.1.call-update) | async-done | bytes 3670032 | tf_op jit(solution)/shard_map/psum | solution.py:352
  795.7 15.5 scatter_fusion
  812.5 1401.6 %while.8 = (s32[]{:T(128)}, f32[8,64,512]{2,1,0:T(8,128)}, f32[8,64,512]{2,1,0:T(8,128)}, f32[8,64,512]{2,1,0:T(8,128)}, f32[8,64,64]{2,1,0:T(8,128)}, /*index=5...) while((s32[]{:T(128)}, f32[8,64,512]{2,1,0:T(8,128)}, ...), condition=%wide.region_53.54_spmd, body=%wide.region_42.53_spmd.sunk | while | flops 5324489216 | bytes 50588708 | solution.py:356
  846.5 11.9 cholesky.484
  870.9 11.7 cholesky.487
  894.0 12.1 cholesky.489
  917.4 11.7 cholesky.490
  941.3 39.3 %custom-call.62 = f32[4,128,128]{1,2,0:T(8,128)S(1)} custom-call(f32[4,128,128]{2,1,0:T(8,128)S(1)} %get-tuple-element.661), custom_call_target="InvertDiagBlocksLowerTriangular" | custom-call | tf_op jit(solution)/shard_map/while/body/eval_jaxpr/jit(_solve_triangular)/triangular_solve | solution.py:177
  1021.5 12.1 cholesky.484
  1046.1 11.7 cholesky.487
  1069.2 11.9 cholesky.489
  1092.4 11.7 cholesky.490
  1116.4 39.3 %custom-call.62 = f32[4,128,128]{1,2,0:T(8,128)S(1)} custom-call(f32[4,128,128]{2,1,0:T(8,128)S(1)} %get-tuple-element.661), custom_call_target="InvertDiagBlocksLowerTriangular" | custom-call | tf_op jit(solution)/shard_map/while/body/eval_jaxpr/jit(_solve_triangular)/triangular_solve | solution.py:177
  1196.7 11.9 cholesky.484
  1221.1 11.7 cholesky.487
  1244.2 11.9 cholesky.489
  1291.6 39.3 %custom-call.62 = f32[4,128,128]{1,2,0:T(8,128)S(1)} custom-call(f32[4,128,128]{2,1,0:T(8,128)S(1)} %get-tuple-element.661), custom_call_target="InvertDiagBlocksLowerTriangular" | custom-call | tf_op jit(solution)/shard_map/while/body/eval_jaxpr/jit(_solve_triangular)/triangular_solve | solution.py:177
  1371.7 11.9 cholesky.484
  1419.3 12.1 cholesky.489
  1466.6 39.3 %custom-call.62 = f32[4,128,128]{1,2,0:T(8,128)S(1)} custom-call(f32[4,128,128]{2,1,0:T(8,128)S(1)} %get-tuple-element.661), custom_call_target="InvertDiagBlocksLowerTriangular" | custom-call | tf_op jit(solution)/shard_map/while/body/eval_jaxpr/jit(_solve_triangular)/triangular_solve | solution.py:177
  1546.7 12.1 cholesky.484
  1594.5 11.9 cholesky.489
  1641.6 39.3 %custom-call.62 = f32[4,128,128]{1,2,0:T(8,128)S(1)} custom-call(f32[4,128,128]{2,1,0:T(8,128)S(1)} %get-tuple-element.661), custom_call_target="InvertDiagBlocksLowerTriangular" | custom-call | tf_op jit(solution)/shard_map/while/body/eval_jaxpr/jit(_solve_triangular)/triangular_solve | solution.py:177
  1722.0 11.9 cholesky.484
  1769.5 11.9 cholesky.489
  1816.8 39.3 %custom-call.62 = f32[4,128,128]{1,2,0:T(8,128)S(1)} custom-call(f32[4,128,128]{2,1,0:T(8,128)S(1)} %get-tuple-element.661), custom_call_target="InvertDiagBlocksLowerTriangular" | custom-call | tf_op jit(solution)/shard_map/while/body/eval_jaxpr/jit(_solve_triangular)/triangular_solve | solution.py:177
  1897.0 11.9 cholesky.484
  1944.5 12.1 cholesky.489
  1991.8 39.3 %custom-call.62 = f32[4,128,128]{1,2,0:T(8,128)S(1)} custom-call(f32[4,128,128]{2,1,0:T(8,128)S(1)} %get-tuple-element.661), custom_call_target="InvertDiagBlocksLowerTriangular" | custom-call | tf_op jit(solution)/shard_map/while/body/eval_jaxpr/jit(_solve_triangular)/triangular_solve | solution.py:177
  2072.0 12.1 cholesky.484
  2119.7 11.9 cholesky.489
  2166.8 39.3 %custom-call.62 = f32[4,128,128]{1,2,0:T(8,128)S(1)} custom-call(f32[4,128,128]{2,1,0:T(8,128)S(1)} %get-tuple-element.661), custom_call_target="InvertDiagBlocksLowerTriangular" | custom-call | tf_op jit(solution)/shard_map/while/body/eval_jaxpr/jit(_solve_triangular)/triangular_solve | solution.py:177
  (1125 shorter events, 1137.1 us)
Async XLA Ops:
  7.2 79.7 %all-gather.15.cloned.1.call-start = ((), (), s32[]{:S(2)}) async-start(), calls=%async_computation.10 | async-start | bytes 4718592 | tf_op jit(solution)/shard_map/all_gather | solution.py:246
  9.3 94.1 %all-gather.37.cloned.1.call-start = ((), (), s32[]{:S(2)}) async-start(), calls=%async_computation.32 | async-start | bytes 1310720 | tf_op jit(solution)/shard_map/while/body/eval_jaxpr/all_gather | solution.py:35
  10.1 111.7 %all-gather.35.cloned.1.call-start = ((), (), s32[]{:S(2)}) async-start(), calls=%async_computation.31 | async-start | bytes 1310720 | tf_op jit(solution)/shard_map/while/body/eval_jaxpr/all_gather | solution.py:35
  10.8 138.8 %reduce-scatter.13.cloned.1.call-start = ((), (), s32[]{:S(2)}) async-start(), calls=%async_computation.12 | async-start | bytes 1310720 | tf_op jit(solution)/shard_map/while/body/eval_jaxpr/reduce_scatter | solution.py:39
  116.6 54.0 %all-gather.17.cloned.1.call-start = ((), (), s32[]{:S(2)}) async-start(), calls=%async_computation.13 | async-start | bytes 1310720 | tf_op jit(solution)/shard_map/while/body/eval_jaxpr/all_gather | solution.py:35
  117.3 83.7 %copy-start.107 = (f32[1,1,512]{2,0,1:T(1,128)}, f32[1,1,512]{2,0,1:T(1,128)S(1)}, u32[]{:S(2)}) copy-start(f32[1,1,512]{2,0,1:T(1,128)S(1)} %get-tuple-element.460) | copy-start | bytes 6148
  117.3 109.4 %copy-start.86 = (f32[1,1,512]{2,0,1:T(1,128)}, f32[1,1,512]{2,0,1:T(1,128)S(1)}, u32[]{:S(2)}) copy-start(f32[1,1,512]{2,0,1:T(1,128)S(1)} %get-tuple-element.459) | copy-start | bytes 6148
  117.3 111.0 %copy-start.90 = (f32[1,1,512]{2,0,1:T(1,128)}, f32[1,1,512]{2,0,1:T(1,128)S(1)}, u32[]{:S(2)}) copy-start(f32[1,1,512]{2,0,1:T(1,128)S(1)} %get-tuple-element.457) | copy-start | bytes 6148
  117.3 183.1 %copy-start.84 = (f32[1,1,512]{2,0,1:T(1,128)}, f32[1,1,512]{2,0,1:T(1,128)S(1)}, u32[]{:S(2)}) copy-start(f32[1,1,512]{2,0,1:T(1,128)S(1)} %get-tuple-element.461) | copy-start | bytes 6148
  150.7 76.0 %copy-start.89 = (f32[256]{0:T(256)}, f32[256]{0:T(256)S(1)}, u32[]{:S(2)}) copy-start(f32[256]{0:T(256)S(1)} %broadcast_multiply_fusion.3) | copy-start | bytes 3076
  151.9 74.8 %copy-start.103 = (f32[256]{0:T(256)}, f32[256]{0:T(256)S(1)}, u32[]{:S(2)}) copy-start(f32[256]{0:T(256)S(1)} %fusion.205) | copy-start | bytes 3076
  153.8 44.9 %reduce-scatter.11.cloned.1.call-start = ((), (), s32[]{:S(2)}) async-start(), calls=%async_computation.11 | async-start | bytes 1310720 | tf_op jit(solution)/shard_map/while/body/eval_jaxpr/reduce_scatter | solution.py:39
  162.7 64.1 %reduce-scatter.15.cloned.1.call-start = ((), (), s32[]{:S(2)}) async-start(), calls=%async_computation.14 | async-start | bytes 1310720 | tf_op jit(solution)/shard_map/while/body/eval_jaxpr/reduce_scatter | solution.py:39
  180.8 46.0 %copy-start.12 = (bf16[256,512]{1,0:T(8,128)(2,1)S(1)}, bf16[256,512]{1,0:T(8,128)(2,1)}, u32[]{:S(2)}) copy-start(bf16[256,512]{1,0:T(8,128)(2,1)} %reduce-scatter.13.cloned.1.call-done) | copy-start | bytes 786436
  180.8 64.9 %all-gather.21.cloned.1.call-start = ((), (), s32[]{:S(2)}) async-start(), calls=%async_computation.16 | async-start | bytes 1310720 | tf_op jit(solution)/shard_map/while/body/eval_jaxpr/all_gather | solution.py:35
  201.0 46.4 %copy-start.101 = (f32[256]{0:T(256)}, f32[256]{0:T(256)S(1)}, u32[]{:S(2)}) copy-start(f32[256]{0:T(256)S(1)} %fusion.204) | copy-start | bytes 3076
  202.9 61.8 %all-gather.19.cloned.1.call-start = ((), (), s32[]{:S(2)}) async-start(), calls=%async_computation.15 | async-start | bytes 1310720 | tf_op jit(solution)/shard_map/while/body/eval_jaxpr/all_gather | solution.py:35
  228.0 38.4 %copy-start.99 = (f32[256]{0:T(256)}, f32[256]{0:T(256)S(1)}, u32[]{:S(2)}) copy-start(f32[256]{0:T(256)S(1)} %broadcast_multiply_fusion.2) | copy-start | bytes 3076
  228.2 39.8 %copy-start.117 = (f32[256]{0:T(256)}, f32[256]{0:T(256)S(1)}, u32[]{:S(2)}) copy-start(f32[256]{0:T(256)S(1)} %multiply_reduce_fusion.13) | copy-start | bytes 3076
  228.3 39.8 %copy-start.108 = (f32[256]{0:T(256)}, f32[256]{0:T(256)S(1)}, u32[]{:S(2)}) copy-start(f32[256]{0:T(256)S(1)} %fusion.206) | copy-start | bytes 3076
  229.2 71.3 %reduce-scatter.17.cloned.1.call-start = ((), (), s32[]{:S(2)}) async-start(), calls=%async_computation.17 | async-start | bytes 1310720 | tf_op jit(solution)/shard_map/while/body/eval_jaxpr/reduce_scatter | solution.py:39
  275.4 46.2 %all-gather.23.cloned.1.call-start = ((), (), s32[]{:S(2)}) async-start(), calls=%async_computation.18 | async-start | bytes 1310720 | tf_op jit(solution)/shard_map/while/body/eval_jaxpr/all_gather | solution.py:35
  304.8 52.2 %reduce-scatter.19.cloned.1.call-start = ((), (), s32[]{:S(2)}) async-start(), calls=%async_computation.19 | async-start | bytes 1310720 | tf_op jit(solution)/shard_map/while/body/eval_jaxpr/reduce_scatter | solution.py:39
  331.9 48.7 %all-gather.25.cloned.1.call-start = ((), (), s32[]{:S(2)}) async-start(), calls=%async_computation.20 | async-start | bytes 1310720 | tf_op jit(solution)/shard_map/while/body/eval_jaxpr/all_gather | solution.py:48
  363.7 48.7 %reduce-scatter.21.cloned.1.call-start = ((), (), s32[]{:S(2)}) async-start(), calls=%async_computation.21 | async-start | bytes 1310720 | tf_op jit(solution)/shard_map/while/body/eval_jaxpr/reduce_scatter | solution.py:52
  387.3 47.8 %all-gather.27.cloned.1.call-start = ((), (), s32[]{:S(2)}) async-start(), calls=%async_computation.22 | async-start | bytes 1310720 | tf_op jit(solution)/shard_map/while/body/eval_jaxpr/all_gather | solution.py:48
  418.2 67.8 %reduce-scatter.23.cloned.1.call-start = ((), (), s32[]{:S(2)}) async-start(), calls=%async_computation.23 | async-start | bytes 2621440 | tf_op jit(solution)/shard_map/while/body/eval_jaxpr/reduce_scatter | solution.py:52
  454.4 32.9 %copy-start.88 = (f32[256]{0:T(256)S(1)}, f32[256]{0:T(256)}, u32[]{:S(2)}) copy-start(f32[256]{0:T(256)} %copy-done.87) | copy-start | bytes 3076
  454.4 32.9 %copy-start.91 = (f32[1,1,512]{2,0,1:T(1,128)S(1)}, f32[1,1,512]{2,0,1:T(1,128)}, u32[]{:S(2)}) copy-start(f32[1,1,512]{2,0,1:T(1,128)} %copy-done.90) | copy-start | bytes 6148
  454.4 32.9 %copy-start.100 = (f32[256]{0:T(256)S(1)}, f32[256]{0:T(256)}, u32[]{:S(2)}) copy-start(f32[256]{0:T(256)} %copy-done.99) | copy-start | bytes 3076
  454.4 32.9 %copy-start.102 = (f32[256]{0:T(256)S(1)}, f32[256]{0:T(256)}, u32[]{:S(2)}) copy-start(f32[256]{0:T(256)} %copy-done.101) | copy-start | bytes 3076
  454.4 32.9 %copy-start.109 = (f32[256]{0:T(256)S(1)}, f32[256]{0:T(256)}, u32[]{:S(2)}) copy-start(f32[256]{0:T(256)} %copy-done.108) | copy-start | bytes 3076
  454.4 32.9 %copy-start.113 = (f32[256]{0:T(256)S(1)}, f32[256]{0:T(256)}, u32[]{:S(2)}) copy-start(f32[256]{0:T(256)} %copy-done.112) | copy-start | bytes 3076
  454.5 35.8 %copy-start.118 = (f32[256]{0:T(256)S(1)}, f32[256]{0:T(256)}, u32[]{:S(2)}) copy-start(f32[256]{0:T(256)} %copy-done.117) | copy-start | bytes 3076
  454.5 54.5 %all-gather.29.cloned.1.call-start = ((), (), s32[]{:S(2)}) async-start(), calls=%async_computation.24 | async-start | bytes 1310720 | tf_op jit(solution)/shard_map/while/body/eval_jaxpr/all_gather | solution.py:48
  492.1 48.7 %reduce-scatter.25.cloned.1.call-start = ((), (), s32[]{:S(2)}) async-start(), calls=%async_computation.25 | async-start | bytes 1310720 | tf_op jit(solution)/shard_map/while/body/eval_jaxpr/reduce_scatter | solution.py:52
  515.8 48.5 %all-gather.31.cloned.1.call-start = ((), (), s32[]{:S(2)}) async-start(), calls=%async_computation.26 | async-start | bytes 1310720 | tf_op jit(solution)/shard_map/while/body/eval_jaxpr/all_gather | solution.py:48
  547.4 36.5 %all-gather.33.cloned.1.call-start = ((), (), s32[]{:S(2)}) async-start(), calls=%async_computation.28 | async-start | bytes 1310720 | tf_op jit(solution)/shard_map/while/body/eval_jaxpr/all_gather | solution.py:48
  556.5 107.2 %reduce-scatter.27.cloned.1.call-start = ((), (), s32[]{:S(2)}) async-start(), calls=%async_computation.27 | async-start | bytes 1310720 | tf_op jit(solution)/shard_map/while/body/eval_jaxpr/reduce_scatter | solution.py:52
  583.5 82.2 %reduce-scatter.29.cloned.1.call-start = ((), (), s32[]{:S(2)}) async-start(), calls=%async_computation.29 | async-start | bytes 1310720 | tf_op jit(solution)/shard_map/while/body/eval_jaxpr/reduce_scatter | solution.py:52
  604.6 180.7 %all-reduce.3.cloned.1.call-start = ((), (), s32[]{:S(2)}) async-start(), calls=%async_computation.30 | async-start | bytes 7340032 | tf_op jit(solution)/shard_map/psum | solution.py:352
  620.9 40.9 %copy-start.81 = (f32[2,5,512]{2,0,1:T(2,128)S(1)}, f32[2,5,512]{2,0,1:T(2,128)}, u32[]{:S(2)}) copy-start(f32[2,5,512]{2,0,1:T(2,128)} %param.31) | copy-start | bytes 61444
  620.9 40.9 %copy-start.105 = (f32[2,5,512]{2,0,1:T(2,128)S(1)}, f32[2,5,512]{2,0,1:T(2,128)}, u32[]{:S(2)}) copy-start(f32[2,5,512]{2,0,1:T(2,128)} %param.32) | copy-start | bytes 61444
  620.9 40.9 %copy-start.106 = (f32[2,5,512]{2,0,1:T(2,128)S(1)}, f32[2,5,512]{2,0,1:T(2,128)}, u32[]{:S(2)}) copy-start(f32[2,5,512]{2,0,1:T(2,128)} %param.33) | copy-start | bytes 61444
  620.9 42.8 %copy-start.23 = (f32[256,512]{1,0:T(8,128)S(1)}, f32[256,512]{1,0:T(8,128)}, u32[]{:S(2)}) copy-start(f32[256,512]{1,0:T(8,128)} %copy-done.22) | copy-start | bytes 1572868
  620.9 42.8 %copy-start.121 = (f32[256]{0:T(256)S(1)}, f32[256]{0:T(256)}, u32[]{:S(2)}) copy-start(f32[256]{0:T(256)} %copy-done.120) | copy-start | bytes 3076
  621.0 44.7 %copy-start.21 = (f32[256,512]{1,0:T(8,128)S(1)}, f32[256,512]{1,0:T(8,128)}, u32[]{:S(2)}) copy-start(f32[256,512]{1,0:T(8,128)} %get-tuple-element.478) | copy-start | bytes 1572868
  621.0 44.7 %copy-start.123 = (f32[256]{0:T(256)S(1)}, f32[256]{0:T(256)}, u32[]{:S(2)}) copy-start(f32[256]{0:T(256)} %copy-done.122) | copy-start | bytes 3076
  (152 other events, 796.6 us)
Sparse Core Ops, SparseCore 0:
  10.7 76.0 all-gather.14
  88.4 14.9 all-gather.36
  105.0 16.7 all-gather.34
  124.7 24.8 reduce-scatter.12
  153.9 16.7 all-gather.16
  173.8 24.8 reduce-scatter.10
  201.8 24.8 reduce-scatter.14
  229.0 16.7 all-gather.20
  247.9 16.7 all-gather.18
  275.5 24.8 reduce-scatter.16
  304.9 16.7 all-gather.22
  332.0 24.9 reduce-scatter.18
  363.8 16.7 all-gather.24
  387.5 24.8 reduce-scatter.20
  418.4 16.7 all-gather.26
  454.6 31.4 reduce-scatter.22
  492.3 16.7 all-gather.28
  515.9 24.8 reduce-scatter.24
  547.6 16.7 all-gather.30
  566.3 16.7 all-gather.32
  585.6 24.8 reduce-scatter.26
  613.2 25.0 reduce-scatter.28
  642.0 143.2 all-reduce.2
where the time goes:
time: 2240 us; the launch traced here: 2220 us
  other arithmetic  1110 us (50%)
  waiting for transfers between devices  510 us (23%)
  matrix products  371 us (17%)
  local copies, waits for them, and re-layouts  145 us (6%)
  blocking collectives  40.2 us (2%)
  loops' own time  26.8 us (1%)
    another operation x136, other arithmetic, renew_basis(): lower_factor = jnp.linalg.cholesky(gram_matrix)  683 us
    another operation x40, other arithmetic, renew_basis(): jax.scipy.linalg.solve_triangular(lower_factor, matrix.T, lower=True)  359 us
    psum x1, waiting for transfers between devices, per_device(): summed = lax.psum(block_grad.astype(jnp.bfloat16), 'dp').astype(jnp.float32)  118 us
    reduce_scatter x5, waiting for transfers between devices, scatter_rows(): lax.psum_scatter(term_fn(jnp.int32(0), row_count * lax.axis_size('tensor'...  109 us
    reduce_scatter x5, waiting for transfers between devices, scatter_grads(): lax.psum_scatter(term_fn(jnp.int32(0), row_count * lax.axis_size('tensor'...  80.9 us
    all_gather x1, waiting for transfers between devices, per_device(): lax.all_gather(master.astype(jnp.bfloat16), 'dp', axis=1, tiled=True)  74.4 us
    all_gather x6, waiting for transfers between devices, gather_rows(): return lax.all_gather(rows_b, 'tensor', axis=0, tiled=True)  69.3 us
    another operation x96, local copies, waits for them, and re-layouts  60 us
  transfers between devices with their start and end apart: 23, of which 20 were waited for; matrix products, arithmetic and copies ran while one was open for 6% of the time, Pallas kernels for 0%

commit v1 on v0

--- a/solution.py
+++ b/solution.py
@@ -1,6 +1,8 @@
 import jax
 import jax.numpy as jnp
 from jax import lax
+from jax.experimental import pallas as pl
+from jax.experimental.pallas import tpu as pltpu
 from jax.sharding import PartitionSpec as P
 
 HEADS = 8
@@ -171,49 +173,251 @@
     return ([grad_in, grad_down], scatter_grads(feed_input_term, row_count))
 
 
-def renew_basis(matrix):
-    gram_matrix = jnp.dot(matrix.T, matrix, precision=highest)
-    lower_factor = jnp.linalg.cholesky(gram_matrix)
-    return jax.scipy.linalg.solve_triangular(lower_factor, matrix.T, lower=True).T
-
-
-def update_slot(inputs):
-    (
-        grad_block,
-        weight,
-        first_moment,
-        second_moment,
-        left_stat,
-        right_stat,
-        left_basis,
-        right_basis,
-    ) = inputs
-    fix_one = 1.0 - 0.9**STEP
-    fix_two = 1.0 - 0.999**STEP
-    turned = jnp.dot(
-        jnp.dot(left_basis.T, grad_block, precision=highest), right_basis, precision=highest
-    )
-    first_new = 0.9 * first_moment + 0.1 * turned
-    second_new = 0.999 * second_moment + 0.001 * turned * turned
-    direction = first_new / fix_one / (jnp.sqrt(second_new / fix_two) + 1e-08)
-    update = jnp.dot(
-        jnp.dot(left_basis, direction, precision=highest), right_basis.T, precision=highest
-    )
-    weight_new = weight - rate_matrix * (update + 0.01 * weight)
-    left_new = 0.95 * left_stat + 0.05 * jnp.dot(grad_block, grad_block.T, precision=highest)
-    right_new = 0.95 * right_stat + 0.05 * jnp.dot(grad_block.T, grad_block, precision=highest)
-    left_basis_new = renew_basis(jnp.dot(left_new, left_basis, precision=highest))
-    right_basis_new = renew_basis(jnp.dot(right_new, right_basis, precision=highest))
-    return (
-        weight_new,
-        first_new,
-        second_new,
-        left_new,
-        right_new,
-        left_basis_new,
-        right_basis_new,
-        weight_new.astype(jnp.bfloat16),
-    )
+F32 = jnp.float32
+BF = jnp.bfloat16
+NN = (((1,), (0,)), ((), ()))
+NT = (((1,), (1,)), ((), ()))
+TN = (((0,), (0,)), ((), ()))
+FIX_ONE = 1.0 - 0.9**STEP
+FIX_TWO = 1.0 - 0.999**STEP
+
+
+def split(v):
+    hi = v.astype(BF)
+    return hi, (v - hi.astype(F32)).astype(BF)
+
+
+def mm(a, b, dims):
+    return lax.dot_general(a, b, dims, preferred_element_type=F32)
+
+
+def mm3(a, b, dims):
+    ah, al = a if isinstance(a, tuple) else split(a)
+    bh, bl = b if isinstance(b, tuple) else split(b)
+    return mm(ah, bh, dims) + (mm(ah, bl, dims) + mm(al, bh, dims))
+
+
+def before_kernel(s_ref, q_ref, a_ref, m_ref):
+    half = s_ref.shape[1] // 2
+    q = split(q_ref[0])
+    a = 0.95 * mm3(s_ref[0], q, NN)
+    a_ref[0] = a
+    ah, al = split(a)
+    m_ref[0, :half, :] = mm3((ah[:, :half], al[:, :half]), (ah, al), TN)
+    m_ref[0, half:, half:] = mm3((ah[:, half:], al[:, half:]), (ah[:, half:], al[:, half:]), TN)
+
+
+def before(stat, basis):
+    n, w, _ = stat.shape
+    spec = pl.BlockSpec((1, w, w), lambda i: (i, 0, 0))
+    return pl.pallas_call(
+        before_kernel,
+        grid=(n,),
+        in_specs=[spec, spec],
+        out_specs=[spec, spec],
+        out_shape=[jax.ShapeDtypeStruct(stat.shape, F32)] * 2,
+        compiler_params=pltpu.CompilerParams(vmem_limit_bytes=60 << 20),
+        cost_estimate=pl.CostEstimate(flops=n * 12 * w**3, bytes_accessed=n * 16 * w * w, transcendentals=0),
+        name="before",
+    )(stat, basis)
+
+
+PANEL = 16
+
+
+def factor_panels(d_ref, count, size):
+    rows = lax.broadcasted_iota(jnp.int32, (PANEL, size), 0)
+    for p in range(size // PANEL):
+        top = p * PANEL
+        left = [d_ref[s, top : top + PANEL, 0:size] for s in range(count)]
+        right = [d_ref[s, top : top + PANEL, size:] for s in range(count)]
+        pivots = [jnp.ones((PANEL, size), F32) for s in range(count)]
+        for r in range(PANEL):
+            for s in range(count):
+                col = jnp.broadcast_to(left[s][:, top + r : top + r + 1], (PANEL, size))
+                piv = jnp.broadcast_to(col[r : r + 1, :], (PANEL, size))
+                pivots[s] = jnp.where(rows == r, piv, pivots[s])
+                if r + 1 < PANEL:
+                    fac = jnp.where(rows > r, col * (1.0 / piv), 0.0)
+                    left[s] = left[s] - fac * left[s][r : r + 1, :]
+                    right[s] = right[s] - fac * right[s][r : r + 1, :]
+        for s in range(count):
+            scale = lax.rsqrt(pivots[s])
+            l_new = left[s] * scale
+            r_new = right[s] * scale
+            d_ref[s, top : top + PANEL, size:] = r_new
+            if top + PANEL < size:
+                lh, ll = split(l_new)
+                rh, rl = split(r_new)
+                lhs = jnp.concatenate([lh, lh, ll], axis=0)
+                rhs = jnp.concatenate(
+                    [jnp.concatenate([lh, rh], axis=1), jnp.concatenate([ll, rl], axis=1), jnp.concatenate([lh, rh], axis=1)],
+                    axis=0,
+                )
+                d_ref[s, top + PANEL :, :] = d_ref[s, top + PANEL :, :] - mm(lhs[:, top + PANEL :], rhs, TN)
+
+
+def after_kernel(
+    g_ref, w_ref, m1_ref, m2_ref, l_ref, ql_ref, s_ref, q_ref, a_ref, m_ref,
+    w_out, m1_out, m2_out, l_out, s_out, qln_out, q_out, c_out,
+    gram, gram_left, x_left, diag,
+):
+    step = pl.program_id(0)
+    count = pl.num_programs(0)
+    n = q_out.shape[0]
+    width = g_ref.shape[2]
+    rows = g_ref.shape[1]
+    g = g_ref[0]
+    q = split(q_ref[0])
+    ql = split(ql_ref[0])
+    p = mm(g, q[0], NN) + mm(g, q[1], NN)
+    turned = mm3(ql, p, TN)
+    first = 0.9 * m1_ref[0] + 0.1 * turned
+    second = 0.999 * m2_ref[0] + 0.001 * turned * turned
+    m1_out[0] = first
+    m2_out[0] = second
+    direction = first / FIX_ONE / (jnp.sqrt(second / FIX_TWO) + 1e-08)
+    update = mm3(ql, mm3(direction, q, NT), NN)
+    weight = w_ref[0]
+    weight = weight - rate_matrix * (update + 0.01 * weight)
+    w_out[0] = weight
+    c_out[0] = weight.astype(BF)
+    k = mm(g, g, NT)
+    left = 0.95 * l_ref[0] + 0.05 * k
+    l_out[0] = left
+    s_out[0] = 0.95 * s_ref[0] + 0.05 * mm(g, g, TN)
+    a = a_ref[0]
+    a_parts = split(a)
+    b = 0.05 * p
+    bh, bl = split(b)
+    h = mm(g, a_parts[0], NN) + mm(g, a_parts[1], NN) + 0.5 * mm3(k, (bh, bl), NN)
+    q_out[step] = a + mm(jnp.concatenate([g, g], axis=0), jnp.concatenate([bh, bl], axis=0), TN)
+    hh, hl = split(h)
+    y = jnp.concatenate([hh, bh, hh, bh, hl, bl], axis=0)
+    z = jnp.concatenate([bh, hh, bl, hl, bh, hh], axis=0)
+    blk = 128
+    for i in range(width // blk):
+        lo = i * blk
+        gram[step, lo : lo + blk, lo:] = m_ref[0, lo : lo + blk, lo:] + mm(y[:, lo : lo + blk], z[:, lo:], TN)
+    xl = mm3(left, ql, NN)
+    x_left[step] = xl
+    gl = mm3(xl, xl, TN)
+    gram_left[step] = gl
+
+    @pl.when(step == count - 1)
+    def _():
+        eye = (lax.broadcasted_iota(jnp.int32, (blk, blk), 0) == lax.broadcasted_iota(jnp.int32, (blk, blk), 1)).astype(F32)
+        blocks = width // blk
+
+        def block_step(kk, carry):
+            for kb in range(blocks):
+                @pl.when(kk == kb)
+                def _():
+                    for s in range(n):
+                        diag[s, :, :blk] = gram[s, kb * blk : kb * blk + blk, kb * blk : kb * blk + blk]
+                        diag[s, :, blk:] = eye
+
+            @pl.when(kk == blocks)
+            def _():
+                for s in range(n):
+                    diag[s, :, :blk] = eye
+                    diag[s, :rows, :rows] = gram_left[s]
+                    diag[s, :, blk:] = eye
+
+            factor_panels(diag, n, blk)
+
+            for kb in range(blocks):
+                @pl.when(kk == kb)
+                def _():
+                    lo = kb * blk
+                    hi = lo + blk
+
+                    def one(s, c):
+                        inv = diag[s, :, blk:]
+                        gram[s, lo:hi, lo:hi] = inv
+                        if blocks == 1:
+                            return c
+                        ih, il = split(inv)
+                        lhs = jnp.concatenate([ih, ih, il], axis=1)
+
+                        def scaled(part):
+                            ph, plo = split(part)
+                            return mm(lhs, jnp.concatenate([ph, plo, ph], axis=0), NN)
+
+                        if kb > 0:
+                            gram[s, lo:hi, :lo] = scaled(gram[s, lo:hi, :lo])
+                        if hi < width:
+                            up = scaled(gram[s, lo:hi, hi:])
+                            uh, ul = split(up)
+                            rh, rl = split(gram[s, lo:hi, :hi])
+                            us = jnp.concatenate([uh, uh, ul], axis=0)
+                            vs = jnp.concatenate([uh, ul, uh], axis=0)
+                            rs = jnp.concatenate([rh, rl, rh], axis=0)
+                            below = mm(us, rs, TN)
+                            if kb > 0:
+                                gram[s, hi:, :lo] = gram[s, hi:, :lo] - below[:, :lo]
+                            gram[s, hi:, lo:hi] = -below[:, lo:]
+                            for i in range(kb + 1, blocks):
+                                b0 = i * blk
+                                gram[s, b0 : b0 + blk, b0:] = gram[s, b0 : b0 + blk, b0:] - mm(
+                                    us[:, b0 - hi : b0 - hi + blk], vs[:, b0 - hi :], TN
+                                )
+                        return c
+
+                    if kb == 0:
+                        for s in range(n):
+                            for i in range(1, blocks):
+                                gram[s, i * blk : i * blk + blk, : i * blk] = jnp.zeros((blk, i * blk), F32)
+                    lax.fori_loop(0, n, one, 0)
+            return carry
+
+        lax.fori_loop(0, blocks + 1, block_step, 0)
+
+        def finish(s, c):
+            x = split(q_out[s])
+            for i in range(0, width, 2 * blk):
+                hi = i + 2 * blk
+                zz = gram[s, i:hi, :hi]
+                r_i = lax.broadcasted_iota(jnp.int32, (2 * blk, hi), 0) + i
+                c_i = lax.broadcasted_iota(jnp.int32, (2 * blk, hi), 1)
+                zz = jnp.where(c_i <= r_i, zz, 0.0)
+                q_out[s, :, i:hi] = mm3((x[0][:, :hi], x[1][:, :hi]), zz, NT)
+            qln_out[s] = mm3(x_left[s], diag[s, :rows, blk : blk + rows], NT)
+            return c
+
+        lax.fori_loop(0, n, finish, 0)
+
+
+def after(grad, weight, m1, m2, left, ql, stat, q, a, m):
+    n, rows, width = weight.shape
+    wide = pl.BlockSpec((1, width, width), lambda i: (i, 0, 0))
+    flat = pl.BlockSpec((1, rows, width), lambda i: (i, 0, 0))
+    small = pl.BlockSpec((1, rows, rows), lambda i: (i, 0, 0))
+    sd = jax.ShapeDtypeStruct
+    return pl.pallas_call(
+        after_kernel,
+        grid=(n,),
+        in_specs=[flat, flat, flat, flat, small, small, wide, wide, wide, wide],
+        out_specs=[
+            flat, flat, flat, small, wide,
+            pl.BlockSpec((n, rows, rows), lambda i: (0, 0, 0)),
+            pl.BlockSpec((n, width, width), lambda i: (0, 0, 0)),
+            flat,
+        ],
+        out_shape=[
+            sd(weight.shape, F32), sd(weight.shape, F32), sd(weight.shape, F32), sd(left.shape, F32), sd(stat.shape, F32),
+            sd(ql.shape, F32), sd(q.shape, F32), sd(weight.shape, BF),
+        ],
+        scratch_shapes=[
+            pltpu.VMEM((n, width, width), F32),
+            pltpu.VMEM((n, rows, rows), F32),
+            pltpu.VMEM((n, rows, rows), F32),
+            pltpu.VMEM((n, 128, 256), F32),
+        ],
+        compiler_params=pltpu.CompilerParams(vmem_limit_bytes=62 << 20),
+        cost_estimate=pl.CostEstimate(flops=n * 12 * width**3, bytes_accessed=n * 24 * width * width, transcendentals=0),
+        name="after",
+    )(grad, weight, m1, m2, left, ql, stat, q, a, m)
 
 
 def per_device(
@@ -243,6 +447,7 @@
     seq_full = row_count * tensor_count
     block_rows = master.shape[2]
     width = master.shape[3]
+    product, gram = before(stat_right[0], basis_right[0])
     gathered = lax.all_gather(master.astype(jnp.bfloat16), "dp", axis=1, tiled=True)
     slot_of = slot_positions(owners[0], capacity)
     blocks = gathered[0][slot_of]
@@ -349,22 +554,23 @@
     )
     decoded, src_grad, tgt_grad = stacked
     block_grad, norm_local = totals
-    summed = lax.psum(block_grad.astype(jnp.bfloat16), "dp").astype(jnp.float32)
-    buffer = jnp.zeros((slot_count, block_rows, width), jnp.float32).at[slot_of].set(summed)
-    own_grad = lax.dynamic_slice_in_dim(buffer, lax.axis_index("dp") * capacity, capacity, 0)
+    held = slot_of[None, :] == jnp.arange(slot_count, dtype=jnp.int32)[:, None]
+    block_of = jnp.sum(jnp.where(held, jnp.arange(slot_of.shape[0], dtype=jnp.int32)[None, :], 0), axis=1)
+    used = jnp.any(held, axis=1)
+    in_slots = jnp.where(used[:, None, None], block_grad.astype(jnp.bfloat16)[block_of], 0)
+    own_grad = lax.psum_scatter(in_slots, "dp", scatter_dimension=0, tiled=True)
     norm_grad = lax.psum(norm_local, ("dp", "tensor"))
-    results = lax.map(
-        update_slot,
-        (
-            own_grad,
-            master[0],
-            rotated_first_moment[0],
-            rotated_second_moment[0],
-            stat_left[0],
-            stat_right[0],
-            basis_left[0],
-            basis_right[0],
-        ),
+    results = after(
+        own_grad,
+        master[0],
+        rotated_first_moment[0],
+        rotated_second_moment[0],
+        stat_left[0],
+        basis_left[0],
+        stat_right[0],
+        basis_right[0],
+        product,
+        gram,
     )
     fix_one = 1.0 - 0.9**STEP
     fix_two = 1.0 - 0.999**STEP

time: 2240 us -> 894 us (0.40)
  other arithmetic: 1110 us -> 62.2 us
  matrix products: 371 us -> 135 us
  Pallas kernels: 0 us -> 158 us
  local copies, waits for them, and re-layouts: 145 us -> 40.6 us
  waiting for transfers between devices: 510 us -> 426 us
  loops' own time: 26.8 us -> 0 us
    another operation x183 -> x0, other arithmetic: 1040 us -> none  [the longest x136 683 us: renew_basis(): lower_factor = jnp.linalg.cholesky(gram_matrix)]
    pallas_call x0 -> x2, Pallas kernels: none -> 158 us  [the longest x1 141 us: after(): pl.pallas_call(after_kernel, grid=(n,), in_specs=[flat, flat, flat, flat,...]
    dot_general x80 -> x0, matrix products: 154 us -> none  [the longest x8 26.6 us: update_slot(): jnp.dot(grad_block.T, grad_block, precision=highest)]
    psum x1 -> x0, waiting for transfers between devices: 118 us -> none  [per_device(): summed = lax.psum(block_grad.astype(jnp.bfloat16), 'dp').astype(jnp.float32)]
    another operation x112 -> x0, matrix products: 87.9 us -> none  [the longest x64 44.2 us: renew_basis(): jax.scipy.linalg.solve_triangular(lower_factor, matrix.T, lower=True)]
    another operation x136 -> x0, local copies, waits for them, and re-layouts: 61.1 us -> none
    reduce_scatter x0 -> x1, waiting for transfers between devices: none -> 36.5 us  [per_device(): own_grad = lax.psum_scatter(in_slots, 'dp', scatter_dimension=0, tiled=True)]
    another operation x9 -> x0, loops' own time: 26.8 us -> none  [the longest x1 24.1 us: per_device(): lax.map(update_slot, (own_grad, master[0], rotated_first_moment[0], rotat...]
  transfers between devices with their start and end apart: 23 -> 23, of which waited for: 20 -> 20; matrix products, arithmetic and copies ran while one was open for 6% -> 15% of each run, Pallas kernels for 0% -> 2%
where the time goes in v1:
time: 894 us; the launch traced here: 884 us
  waiting for transfers between devices  426 us (48%)
  Pallas kernels  158 us (18%)
  matrix products  135 us (15%)
  other arithmetic  62.2 us (7%)
  blocking collectives  42.4 us (5%)
  local copies, waits for them, and re-layouts  40.6 us (5%)
  between operations  17.6 us (2%)
    pallas_call x1, Pallas kernels, after(): pl.pallas_call(after_kernel, grid=(n,), in_specs=[flat, flat, flat, flat,...  141 us
    reduce_scatter x5, waiting for transfers between devices, scatter_rows(): lax.psum_scatter(term_fn(jnp.int32(0), row_count * lax.axis_size('tensor'...  108 us
    reduce_scatter x5, waiting for transfers between devices, scatter_grads(): lax.psum_scatter(term_fn(jnp.int32(0), row_count * lax.axis_size('tensor'...  80.1 us
    all_gather x1, waiting for transfers between devices, per_device(): lax.all_gather(master.astype(jnp.bfloat16), 'dp', axis=1, tiled=True)  73.9 us
    all_gather x6, waiting for transfers between devices, gather_rows(): return lax.all_gather(rows_b, 'tensor', axis=0, tiled=True)  68.5 us
    all_gather x5, waiting for transfers between devices, gather_grads(): return lax.all_gather(rows_b, 'tensor', axis=0, tiled=True)  56.8 us
    psum x1, blocking collectives, per_device(): norm_grad = lax.psum(norm_local, ('dp', 'tensor'))  42.4 us
    reduce_scatter x1, waiting for transfers between devices, per_device(): own_grad = lax.psum_scatter(in_slots, 'dp', scatter_dimension=0, tiled=True)  36.5 us
  transfers between devices with their start and end apart: 23, of which 20 were waited for; matrix products, arithmetic and copies ran while one was open for 15% of the time, Pallas kernels for 2%

profile of v1, /device:TPU:0, one launch (start us, length us, event | category | flops | bytes accessed | tf_op | source)
XLA Modules:
  0.0 884.3 jit_solution(8683310663979821170)
XLA Ops:
  13.0 73.9 %all-gather.15.cloned.1.call-done = bf16[1,64,64,512]{3,2,0,1:T(8,128)(2,1)} async-done(((bf16[1,8,64,512]{3,2,0,1:T(8,128)(2,1)}), bf16[1,64,64,512]{3,2,0,1:T(8,128)(2,1)}) %all-gather.15.cloned.1.call-update) | async-done | bytes 4194320 | tf_op jit(solution)/shard_map/all_gather | solution.py:451
  86.9 4.9 gather_fusion
  91.8 2.4 fusion.153
  94.2 9.3 %all-gather.37.cloned.1.call-done = bf16[1,1024,512]{2,1,0:T(8,128)(2,1)} async-done(((bf16[1,256,512]{2,1,0:T(8,128)(2,1)}), bf16[1,1024,512]{2,1,0:T(8,128)(2,1)}) %all-gather.37.cloned.1.call-update) | async-done | bytes 1048592 | tf_op jit(solution)/shard_map/while/body/eval_jaxpr/all_gather | solution.py:37
  114.2 2.4 bitcast_convert_fusion.2
  117.7 4.1 all-gather.35.cloned.1.call-done
  127.2 3.4 copy-done.2
  131.7 17.9 %reduce-scatter.14.cloned.1.call-done = bf16[256,512]{1,0:T(8,128)(2,1)} async-done(((bf16[1024,512]{1,0:T(8,128)(2,1)}), bf16[256,512]{1,0:T(8,128)(2,1)}) %reduce-scatter.14.cloned.1.call-update) | async-done | bytes 262160 | tf_op jit(solution)/shard_map/while/body/eval_jaxpr/reduce_scatter | solution.py:41
  154.6 5.0 fusion.53
  162.7 2.7 fusion.154
  165.4 5.3 all-gather.17.cloned.1.call-done
  170.7 7.6 multiply_convert_fusion.4
  181.0 17.8 %reduce-scatter.12.cloned.1.call-done = bf16[256,512]{1,0:T(8,128)(2,1)} async-done(((bf16[1024,512]{1,0:T(8,128)(2,1)}), bf16[256,512]{1,0:T(8,128)(2,1)}) %reduce-scatter.12.cloned.1.call-update) | async-done | bytes 262160 | tf_op jit(solution)/shard_map/while/body/eval_jaxpr/reduce_scatter | solution.py:41
  203.0 23.8 %reduce-scatter.16.cloned.1.call-done = bf16[256,512]{1,0:T(8,128)(2,1)} async-done(((bf16[1024,512]{1,0:T(8,128)(2,1)}), bf16[256,512]{1,0:T(8,128)(2,1)}) %reduce-scatter.16.cloned.1.call-update) | async-done | bytes 262160 | tf_op jit(solution)/shard_map/while/body/eval_jaxpr/reduce_scatter | solution.py:41
  230.0 15.8 %all-gather.21.cloned.1.call-done = bf16[1024,512]{1,0:T(8,128)(2,1)} async-done(((bf16[256,512]{1,0:T(8,128)(2,1)}), bf16[1024,512]{1,0:T(8,128)(2,1)}) %all-gather.21.cloned.1.call-update) | async-done | bytes 1048592 | tf_op jit(solution)/shard_map/while/body/eval_jaxpr/all_gather | solution.py:37
  247.5 17.3 %all-gather.19.cloned.1.call-done = bf16[1024,512]{1,0:T(8,128)(2,1)} async-done(((bf16[256,512]{1,0:T(8,128)(2,1)}), bf16[1024,512]{1,0:T(8,128)(2,1)}) %all-gather.19.cloned.1.call-update) | async-done | bytes 1048592 | tf_op jit(solution)/shard_map/while/body/eval_jaxpr/all_gather | solution.py:37
  273.7 2.4 bitcast_convert_fusion.1
  276.6 24.6 %reduce-scatter.18.cloned.1.call-done = bf16[256,512]{1,0:T(8,128)(2,1)} async-done(((bf16[1024,512]{1,0:T(8,128)(2,1)}), bf16[256,512]{1,0:T(8,128)(2,1)}) %reduce-scatter.18.cloned.1.call-update) | async-done | bytes 262160 | tf_op jit(solution)/shard_map/while/body/eval_jaxpr/reduce_scatter | solution.py:41
  305.5 16.8 %all-gather.23.cloned.1.call-done = bf16[1024,512]{1,0:T(8,128)(2,1)} async-done(((bf16[256,512]{1,0:T(8,128)(2,1)}), bf16[1024,512]{1,0:T(8,128)(2,1)}) %all-gather.23.cloned.1.call-update) | async-done | bytes 1048592 | tf_op jit(solution)/shard_map/while/body/eval_jaxpr/all_gather | solution.py:37
  322.4 7.6 multiply_convert_fusion.3
  333.3 24.4 %reduce-scatter.20.cloned.1.call-done = bf16[256,512]{1,0:T(8,128)(2,1)} async-done(((bf16[1024,512]{1,0:T(8,128)(2,1)}), bf16[256,512]{1,0:T(8,128)(2,1)}) %reduce-scatter.20.cloned.1.call-update) | async-done | bytes 262160 | tf_op jit(solution)/shard_map/while/body/eval_jaxpr/reduce_scatter | solution.py:41
  364.5 16.8 %all-gather.25.cloned.1.call-done = bf16[1024,512]{1,0:T(8,128)(2,1)} async-done(((bf16[256,512]{1,0:T(8,128)(2,1)}), bf16[1024,512]{1,0:T(8,128)(2,1)}) %all-gather.25.cloned.1.call-update) | async-done | bytes 1048592 | tf_op jit(solution)/shard_map/while/body/eval_jaxpr/all_gather | solution.py:50
  381.3 4.0 add_convert_fusion.1
  388.1 25.0 %reduce-scatter.22.cloned.1.call-done = bf16[256,512]{1,0:T(8,128)(2,1)} async-done(((bf16[1024,512]{1,0:T(8,128)(2,1)}), bf16[256,512]{1,0:T(8,128)(2,1)}) %reduce-scatter.22.cloned.1.call-update) | async-done | bytes 262160 | tf_op jit(solution)/shard_map/while/body/eval_jaxpr/reduce_scatter | solution.py:54
  419.9 15.9 %all-gather.27.cloned.1.call-done = bf16[1024,512]{1,0:T(8,128)(2,1)} async-done(((bf16[256,512]{1,0:T(8,128)(2,1)}), bf16[1024,512]{1,0:T(8,128)(2,1)}) %all-gather.27.cloned.1.call-update) | async-done | bytes 1048592 | tf_op jit(solution)/shard_map/while/body/eval_jaxpr/all_gather | solution.py:50
  437.5 4.9 fusion.36
  442.5 5.3 multiply_reduce_fusion.2
  447.9 2.5 multiply_convert_fusion.2
  458.6 31.5 %reduce-scatter.24.cloned.1.call-done = bf16[256,1024]{1,0:T(8,128)(2,1)} async-done(((bf16[1024,1024]{1,0:T(8,128)(2,1)}), bf16[256,1024]{1,0:T(8,128)(2,1)}) %reduce-scatter.24.cloned.1.call-update) | async-done | bytes 524304 | tf_op jit(solution)/shard_map/while/body/eval_jaxpr/reduce_scatter | solution.py:54
  491.4 2.9 multiply_reduce_fusion.4
  496.3 16.8 %all-gather.29.cloned.1.call-done = bf16[1024,512]{1,0:T(8,128)(2,1)} async-done(((bf16[256,512]{1,0:T(8,128)(2,1)}), bf16[1024,512]{1,0:T(8,128)(2,1)}) %all-gather.29.cloned.1.call-update) | async-done | bytes 1048592 | tf_op jit(solution)/shard_map/while/body/eval_jaxpr/all_gather | solution.py:50
  513.1 4.0 add_convert_fusion
  521.5 23.5 %reduce-scatter.26.cloned.1.call-done = bf16[256,512]{1,0:T(8,128)(2,1)} async-done(((bf16[1024,512]{1,0:T(8,128)(2,1)}), bf16[256,512]{1,0:T(8,128)(2,1)}) %reduce-scatter.26.cloned.1.call-update) | async-done | bytes 262160 | tf_op jit(solution)/shard_map/while/body/eval_jaxpr/reduce_scatter | solution.py:54
  545.1 3.2 multiply_reduce_fusion.6
  550.5 3.2 convolution_convert_fusion.4
  559.9 7.2 all-gather.31.cloned.1.call-done
  568.8 5.4 multiply_reduce_fusion.1
  574.7 2.5 multiply_convert_fusion.1
  584.5 2.4 fusion.24
  595.7 5.5 multiply_reduce_fusion
  601.8 2.5 multiply_convert_fusion
  611.5 2.4 fusion.22
  624.5 5.1 gather_fusion.1
  629.6 4.5 broadcast_select_fusion
  634.4 17.0 %before.1 = (f32[8,512,512]{2,1,0:T(8,128)}, f32[8,512,512]{2,1,0:T(8,128)}) custom-call(f32[8,512,512]{2,1,0:T(8,128)} %bitcast.521, f32[8,512,512]{2,1,0:T(8,128)} %bitcast.523), custom_call_target="tpu_custom_call" | custom-call | flops 12884901888 | bytes 33554432 | tf_op jit(solution)/shard_map/before/pallas_call | solution.py:213
  651.5 42.4 %psum.7 = f32[2,5,512]{2,1,0:T(8,128)S(1)} all-reduce(f32[2,5,512]{2,1,0:T(8,128)S(1)} %pad_maximum_fusion.1), channel_id=1, replica_groups=mesh['dp'=8,'tensor'=4] {'dp','tensor'}, use_global_device_ids=true, to_apply=%region_53.54 | all-reduce | flops 5120 | bytes 40960 | tf_op jit(solution)/shard_map/psum | solution.py:562
  699.6 36.5 %reduce-scatter.32.cloned.1.call-done.g_ref = bf16[8,64,512]{2,1,0:T(8,128)(2,1)} async-done(((bf16[64,64,512]{2,1,0:T(8,128)(2,1)}), bf16[8,64,512]{2,1,0:T(8,128)(2,1)}) %reduce-scatter.32.cloned.1.call-update) | async-done | bytes 524304 | tf_op jit(solution)/shard_map/reduce_scatter | solution.py:561
  736.1 141.5 %after.1 = (f32[8,64,512]{2,1,0:T(8,128)}, f32[8,64,512]{2,1,0:T(8,128)}, f32[8,64,512]{2,1,0:T(8,128)}, f32[8,64,64]{2,1,0:T(8,128)}, f32[8,512,512]{2,1,0:T(8,...) custom-call(bf16[8,64,512]{2,1,0:T(8,128)(2,1)} %reduce-scatter.32.cloned.1.call-done.g_ref, ...), custom_call_target="tpu_custom_call" | custom-call | flops 12884901888 | bytes 50331648 | tf_op jit(solution)/shard_map/after/pallas_call | solution.py:397
  (499 shorter events, 142.8 us)
Async XLA Ops:
  7.2 79.7 %all-gather.15.cloned.1.call-start = ((), (), s32[]{:S(2)}) async-start(), calls=%async_computation.11 | async-start | bytes 4718592 | tf_op jit(solution)/shard_map/all_gather | solution.py:451
  9.3 94.1 %all-gather.37.cloned.1.call-start = ((), (), s32[]{:S(2)}) async-start(), calls=%async_computation.33 | async-start | bytes 1310720 | tf_op jit(solution)/shard_map/while/body/eval_jaxpr/all_gather | solution.py:37
  10.1 111.7 %all-gather.35.cloned.1.call-start = ((), (), s32[]{:S(2)}) async-start(), calls=%async_computation.32 | async-start | bytes 1310720 | tf_op jit(solution)/shard_map/while/body/eval_jaxpr/all_gather | solution.py:37
  10.8 138.8 %reduce-scatter.14.cloned.1.call-start = ((), (), s32[]{:S(2)}) async-start(), calls=%async_computation.13 | async-start | bytes 1310720 | tf_op jit(solution)/shard_map/while/body/eval_jaxpr/reduce_scatter | solution.py:41
  12.9 94.0 %copy-start.110 = (pred[1024]{0:T(1024)(128)(4,1)}, pred[1024]{0:T(1024)(128)(4,1)S(1)}, u32[]{:S(2)}) copy-start(pred[1024]{0:T(1024)(128)(4,1)S(1)} %iota_compare_fusion.3) | copy-start | bytes 3076
  116.6 54.1 %all-gather.17.cloned.1.call-start = ((), (), s32[]{:S(2)}) async-start(), calls=%async_computation.14 | async-start | bytes 1310720 | tf_op jit(solution)/shard_map/while/body/eval_jaxpr/all_gather | solution.py:37
  117.3 34.7 %copy-start.105 = (f32[1,1,512]{2,0,1:T(1,128)}, f32[1,1,512]{2,0,1:T(1,128)S(1)}, u32[]{:S(2)}) copy-start(f32[1,1,512]{2,0,1:T(1,128)S(1)} %get-tuple-element.233) | copy-start | bytes 6148
  117.3 83.8 %copy-start.104 = (f32[1,1,512]{2,0,1:T(1,128)}, f32[1,1,512]{2,0,1:T(1,128)S(1)}, u32[]{:S(2)}) copy-start(f32[1,1,512]{2,0,1:T(1,128)S(1)} %get-tuple-element.235) | copy-start | bytes 6148
  117.3 109.5 %copy-start.79 = (f32[1,1,512]{2,0,1:T(1,128)}, f32[1,1,512]{2,0,1:T(1,128)S(1)}, u32[]{:S(2)}) copy-start(f32[1,1,512]{2,0,1:T(1,128)S(1)} %get-tuple-element.234) | copy-start | bytes 6148
  117.3 183.9 %copy-start.76 = (f32[1,1,512]{2,0,1:T(1,128)}, f32[1,1,512]{2,0,1:T(1,128)S(1)}, u32[]{:S(2)}) copy-start(f32[1,1,512]{2,0,1:T(1,128)S(1)} %get-tuple-element.236) | copy-start | bytes 6148
  150.8 76.0 %copy-start.84 = (f32[256]{0:T(256)}, f32[256]{0:T(256)S(1)}, u32[]{:S(2)}) copy-start(f32[256]{0:T(256)S(1)} %broadcast_multiply_fusion.3) | copy-start | bytes 3076
  153.8 45.0 %reduce-scatter.12.cloned.1.call-start = ((), (), s32[]{:S(2)}) async-start(), calls=%async_computation.12 | async-start | bytes 1310720 | tf_op jit(solution)/shard_map/while/body/eval_jaxpr/reduce_scatter | solution.py:41
  162.7 64.1 %reduce-scatter.16.cloned.1.call-start = ((), (), s32[]{:S(2)}) async-start(), calls=%async_computation.15 | async-start | bytes 1310720 | tf_op jit(solution)/shard_map/while/body/eval_jaxpr/reduce_scatter | solution.py:41
  180.9 45.9 %copy-start.11 = (bf16[256,512]{1,0:T(8,128)(2,1)S(1)}, bf16[256,512]{1,0:T(8,128)(2,1)}, u32[]{:S(2)}) copy-start(bf16[256,512]{1,0:T(8,128)(2,1)} %reduce-scatter.14.cloned.1.call-done) | copy-start | bytes 786436
  181.0 64.8 %all-gather.21.cloned.1.call-start = ((), (), s32[]{:S(2)}) async-start(), calls=%async_computation.17 | async-start | bytes 1310720 | tf_op jit(solution)/shard_map/while/body/eval_jaxpr/all_gather | solution.py:37
  202.9 61.8 %all-gather.19.cloned.1.call-start = ((), (), s32[]{:S(2)}) async-start(), calls=%async_computation.16 | async-start | bytes 1310720 | tf_op jit(solution)/shard_map/while/body/eval_jaxpr/all_gather | solution.py:37
  228.1 36.7 %copy-start.94 = (f32[256]{0:T(256)}, f32[256]{0:T(256)S(1)}, u32[]{:S(2)}) copy-start(f32[256]{0:T(256)S(1)} %broadcast_multiply_fusion.2) | copy-start | bytes 3076
  228.3 36.5 %copy-start.117 = (f32[256]{0:T(256)}, f32[256]{0:T(256)S(1)}, u32[]{:S(2)}) copy-start(f32[256]{0:T(256)S(1)} %multiply_reduce_fusion.13) | copy-start | bytes 3076
  228.3 36.5 %copy-start.106 = (f32[256]{0:T(256)}, f32[256]{0:T(256)S(1)}, u32[]{:S(2)}) copy-start(f32[256]{0:T(256)S(1)} %fusion.121) | copy-start | bytes 3076
  229.9 71.3 %reduce-scatter.18.cloned.1.call-start = ((), (), s32[]{:S(2)}) async-start(), calls=%async_computation.18 | async-start | bytes 1310720 | tf_op jit(solution)/shard_map/while/body/eval_jaxpr/reduce_scatter | solution.py:41
  276.1 46.2 %all-gather.23.cloned.1.call-start = ((), (), s32[]{:S(2)}) async-start(), calls=%async_computation.19 | async-start | bytes 1310720 | tf_op jit(solution)/shard_map/while/body/eval_jaxpr/all_gather | solution.py:37
  305.5 52.2 %reduce-scatter.20.cloned.1.call-start = ((), (), s32[]{:S(2)}) async-start(), calls=%async_computation.20 | async-start | bytes 1310720 | tf_op jit(solution)/shard_map/while/body/eval_jaxpr/reduce_scatter | solution.py:41
  332.7 48.6 %all-gather.25.cloned.1.call-start = ((), (), s32[]{:S(2)}) async-start(), calls=%async_computation.21 | async-start | bytes 1310720 | tf_op jit(solution)/shard_map/while/body/eval_jaxpr/all_gather | solution.py:50
  364.4 48.7 %reduce-scatter.22.cloned.1.call-start = ((), (), s32[]{:S(2)}) async-start(), calls=%async_computation.22 | async-start | bytes 1310720 | tf_op jit(solution)/shard_map/while/body/eval_jaxpr/reduce_scatter | solution.py:54
  388.0 47.8 %all-gather.27.cloned.1.call-start = ((), (), s32[]{:S(2)}) async-start(), calls=%async_computation.23 | async-start | bytes 1310720 | tf_op jit(solution)/shard_map/while/body/eval_jaxpr/all_gather | solution.py:50
  418.9 71.2 %reduce-scatter.24.cloned.1.call-start = ((), (), s32[]{:S(2)}) async-start(), calls=%async_computation.24 | async-start | bytes 2621440 | tf_op jit(solution)/shard_map/while/body/eval_jaxpr/reduce_scatter | solution.py:54
  458.5 32.8 %copy-start.10 = (bf16[256,512]{1,0:T(8,128)(2,1)S(1)}, bf16[256,512]{1,0:T(8,128)(2,1)}, u32[]{:S(2)}) copy-start(bf16[256,512]{1,0:T(8,128)(2,1)} %reduce-scatter.12.cloned.1.call-done) | copy-start | bytes 786436
  458.5 32.8 %copy-start.77 = (f32[1,1,512]{2,0,1:T(1,128)S(1)}, f32[1,1,512]{2,0,1:T(1,128)}, u32[]{:S(2)}) copy-start(f32[1,1,512]{2,0,1:T(1,128)} %copy-done.76) | copy-start | bytes 6148
  458.5 32.9 %copy-start.82 = (f32[256]{0:T(256)S(1)}, f32[256]{0:T(256)}, u32[]{:S(2)}) copy-start(f32[256]{0:T(256)} %copy-done.81) | copy-start | bytes 3076
  458.5 32.9 %copy-start.86 = (f32[1,1,512]{2,0,1:T(1,128)S(1)}, f32[1,1,512]{2,0,1:T(1,128)}, u32[]{:S(2)}) copy-start(f32[1,1,512]{2,0,1:T(1,128)} %get-tuple-element.232) | copy-start | bytes 6148
  458.5 32.9 %copy-start.95 = (f32[256]{0:T(256)S(1)}, f32[256]{0:T(256)}, u32[]{:S(2)}) copy-start(f32[256]{0:T(256)} %copy-done.94) | copy-start | bytes 3076
  458.5 32.9 %copy-start.97 = (f32[256]{0:T(256)S(1)}, f32[256]{0:T(256)}, u32[]{:S(2)}) copy-start(f32[256]{0:T(256)} %copy-done.96) | copy-start | bytes 3076
  458.5 32.9 %copy-start.107 = (f32[256]{0:T(256)S(1)}, f32[256]{0:T(256)}, u32[]{:S(2)}) copy-start(f32[256]{0:T(256)} %copy-done.106) | copy-start | bytes 3076
  458.5 32.9 %copy-start.112 = (f32[256]{0:T(256)S(1)}, f32[256]{0:T(256)}, u32[]{:S(2)}) copy-start(f32[256]{0:T(256)} %copy-done.111) | copy-start | bytes 3076
  458.6 35.7 %copy-start.118 = (f32[256]{0:T(256)S(1)}, f32[256]{0:T(256)}, u32[]{:S(2)}) copy-start(f32[256]{0:T(256)} %copy-done.117) | copy-start | bytes 3076
  458.6 54.5 %all-gather.29.cloned.1.call-start = ((), (), s32[]{:S(2)}) async-start(), calls=%async_computation.25 | async-start | bytes 1310720 | tf_op jit(solution)/shard_map/while/body/eval_jaxpr/all_gather | solution.py:50
  494.6 50.4 %copy-start.108 = (f32[256]{0:T(256)}, f32[256]{0:T(256)S(1)}, u32[]{:S(2)}) copy-start(f32[256]{0:T(256)S(1)} %negate_multiply_fusion.4) | copy-start | bytes 3076
  496.2 48.8 %reduce-scatter.26.cloned.1.call-start = ((), (), s32[]{:S(2)}) async-start(), calls=%async_computation.26 | async-start | bytes 1310720 | tf_op jit(solution)/shard_map/while/body/eval_jaxpr/reduce_scatter | solution.py:54
  520.0 47.1 %all-gather.31.cloned.1.call-start = ((), (), s32[]{:S(2)}) async-start(), calls=%async_computation.27 | async-start | bytes 1310720 | tf_op jit(solution)/shard_map/while/body/eval_jaxpr/all_gather | solution.py:50
  550.2 43.7 %all-gather.33.cloned.1.call-start = ((), (), s32[]{:S(2)}) async-start(), calls=%async_computation.29 | async-start | bytes 1310720 | tf_op jit(solution)/shard_map/while/body/eval_jaxpr/all_gather | solution.py:50
  559.8 136.0 %reduce-scatter.28.cloned.1.call-start = ((), (), s32[]{:S(2)}) async-start(), calls=%async_computation.28 | async-start | bytes 1310720 | tf_op jit(solution)/shard_map/while/body/eval_jaxpr/reduce_scatter | solution.py:54
  586.9 110.8 %reduce-scatter.30.cloned.1.call-start = ((), (), s32[]{:S(2)}) async-start(), calls=%async_computation.30 | async-start | bytes 1310720 | tf_op jit(solution)/shard_map/while/body/eval_jaxpr/reduce_scatter | solution.py:54
  613.9 122.2 %reduce-scatter.32.cloned.1.call-start = ((), (), s32[]{:S(2)}) async-start(), calls=%async_computation.31 | async-start | bytes 4718592 | tf_op jit(solution)/shard_map/reduce_scatter | solution.py:561
  634.3 59.6 %copy-start.73 = (f32[2,5,512]{2,0,1:T(2,128)S(1)}, f32[2,5,512]{2,0,1:T(2,128)}, u32[]{:S(2)}) copy-start(f32[2,5,512]{2,0,1:T(2,128)} %param.29) | copy-start | bytes 61444
  634.3 59.6 %copy-start.102 = (f32[2,5,512]{2,0,1:T(2,128)S(1)}, f32[2,5,512]{2,0,1:T(2,128)}, u32[]{:S(2)}) copy-start(f32[2,5,512]{2,0,1:T(2,128)} %param.30) | copy-start | bytes 61444
  634.3 59.6 %copy-start.103 = (f32[2,5,512]{2,0,1:T(2,128)S(1)}, f32[2,5,512]{2,0,1:T(2,128)}, u32[]{:S(2)}) copy-start(f32[2,5,512]{2,0,1:T(2,128)} %param.31) | copy-start | bytes 61444
  634.3 61.5 %copy-start.121 = (f32[256]{0:T(256)S(1)}, f32[256]{0:T(256)}, u32[]{:S(2)}) copy-start(f32[256]{0:T(256)} %copy-done.120) | copy-start | bytes 3076
  634.3 63.4 %copy-start.123 = (f32[256]{0:T(256)S(1)}, f32[256]{0:T(256)}, u32[]{:S(2)}) copy-start(f32[256]{0:T(256)} %copy-done.122) | copy-start | bytes 3076
  (133 other events, 907.0 us)
Sparse Core Ops, SparseCore 0:
  10.7 76.0 all-gather.14
  88.4 14.9 all-gather.36
  105.0 16.7 all-gather.34
  124.7 24.9 reduce-scatter.13
  153.9 16.7 all-gather.16
  173.8 24.9 reduce-scatter.11
  201.9 24.8 reduce-scatter.15
  229.0 16.7 all-gather.20
  248.0 16.7 all-gather.18
  276.3 24.8 reduce-scatter.17
  305.6 16.7 all-gather.22
  332.8 24.8 reduce-scatter.19
  364.5 16.7 all-gather.24
  388.2 24.8 reduce-scatter.21
  419.1 16.7 all-gather.26
  458.7 31.4 reduce-scatter.23
  496.3 16.7 all-gather.28
  520.1 24.8 reduce-scatter.25
  550.3 16.7 all-gather.30
  569.1 16.7 all-gather.32
  589.0 24.8 reduce-scatter.27
  617.1 24.9 reduce-scatter.29
  646.3 89.7 reduce-scatter.31

commit v2 on v1

v2 whole, which is shorter than its diff:
```python
import jax
import jax.numpy as jnp
from jax import lax
from jax.experimental import pallas as pl
from jax.experimental.pallas import tpu as pltpu
from jax.sharding import PartitionSpec as P

HEADS = 8
STEP = 10
FFB = 32


highest = lax.Precision.HIGHEST
rate_matrix = 0.3
rate_vector = 0.6


def slot_positions(owner_row, capacity):
    block_ids = jnp.arange(owner_row.shape[0], dtype=jnp.int32)
    same_owner = (owner_row[:, None] == owner_row[None, :]).astype(jnp.int32)
    earlier = (block_ids[None, :] < block_ids[:, None]).astype(jnp.int32)
    rank_of = jnp.sum(same_owner * earlier, axis=1)
    return owner_row * capacity + rank_of


def layer_norm(values, norm_gain, norm_shift):
    center = values - jnp.mean(values, axis=-1, keepdims=True)
    spread = jnp.mean(center * center, axis=-1, keepdims=True)
    return center * lax.rsqrt(spread + 1e-05) * norm_gain + norm_shift


F32 = jnp.float32
BF = jnp.bfloat16
NN = (((1,), (0,)), ((), ()))
NT = (((1,), (1,)), ((), ()))
TN = (((0,), (0,)), ((), ()))
FIX_ONE = 1.0 - 0.9**STEP
FIX_TWO = 1.0 - 0.999**STEP


def split(v):
    hi = v.astype(BF)
    return hi, (v - hi.astype(F32)).astype(BF)


def mm(a, b, dims):
    return lax.dot_general(a, b, dims, preferred_element_type=F32)


def mm3(a, b, dims):
    ah, al = a if isinstance(a, tuple) else split(a)
    bh, bl = b if isinstance(b, tuple) else split(b)
    return mm(ah, bh, dims) + (mm(ah, bl, dims) + mm(al, bh, dims))


def before_kernel(s_ref, q_ref, a_ref, m_ref):
    half = s_ref.shape[1] // 2
    q = split(q_ref[0])
    a = 0.95 * mm3(s_ref[0], q, NN)
    a_ref[0] = a
    ah, al = split(a)
    m_ref[0, :half, :] = mm3((ah[:, :half], al[:, :half]), (ah, al), TN)
    m_ref[0, half:, half:] = mm3((ah[:, half:], al[:, half:]), (ah[:, half:], al[:, half:]), TN)


def before(stat, basis):
    n, w, _ = stat.shape
    spec = pl.BlockSpec((1, w, w), lambda i: (i, 0, 0))
    return pl.pallas_call(
        before_kernel,
        grid=(n,),
        in_specs=[spec, spec],
        out_specs=[spec, spec],
        out_shape=[jax.ShapeDtypeStruct(stat.shape, F32)] * 2,
        compiler_params=pltpu.CompilerParams(vmem_limit_bytes=60 << 20),
        cost_estimate=pl.CostEstimate(flops=n * 12 * w**3, bytes_accessed=n * 16 * w * w, transcendentals=0),
        name="before",
    )(stat, basis)


PANEL = 16
BLOCK = 128


def reciprocal(v):
    guess = pl.reciprocal(v, approx=True)
    for _ in range(2):
        guess = guess * (2.0 - v * guess)
    return guess


def factor_panels(dm, dw, pm, pw, um, uw, n, panels):
    size = BLOCK
    end = panels * PANEL
    for s in range(n):
        pm[s * PANEL : s * PANEL + PANEL, :] = dm[s * size : s * size + PANEL, :]
        pw[s * PANEL : s * PANEL + PANEL, :] = dw[s * size : s * size + PANEL, :]
    for p in range(panels):
        top = p * PANEL
        low = top + PANEL
        rows = [pm[pl.ds(a, n, stride=PANEL), :] for a in range(PANEL)]
        eyes = [pw[pl.ds(a, n, stride=PANEL), :] for a in range(PANEL)]
        corner = {}
        for a in range(PANEL):
            for b in range(a, PANEL):
                corner[a, b] = jnp.broadcast_to(rows[a][:, top + b : top + b + 1], (n, size))
        for r in range(PANEL):
            inverse = reciprocal(corner[r, r])
            for a in range(r + 1, PANEL):
                factor = corner[r, a] * inverse
                for b in range(a, PANEL):
                    corner[a, b] = corner[a, b] - factor * corner[r, b]
                rows[a] = rows[a] - factor * rows[r]
                eyes[a] = eyes[a] - factor * eyes[r]
            scale = lax.rsqrt(corner[r, r])
            um[pl.ds(r, n, stride=PANEL), :] = rows[r] * scale
            uw[pl.ds(r, n, stride=PANEL), :] = eyes[r] * scale
        pending = []
        for s in range(n):
            base = s * size
            upper = um[s * PANEL : s * PANEL + PANEL, :]
            lower = uw[s * PANEL : s * PANEL + PANEL, :]
            dw[base + top : base + low, :] = lower
            if low < end:
                uh, ul = split(upper)
                lh, ll = split(lower)
                lhs = jnp.concatenate([uh, uh, ul], axis=0)
                high = jnp.concatenate([uh, lh], axis=1)
                rest = jnp.concatenate([ul, ll], axis=1)
                rhs = jnp.concatenate([high, rest, high], axis=0)
                u = mm(lhs[:, low : low + PANEL], rhs, TN)
                pm[s * PANEL : s * PANEL + PANEL, :] = dm[base + low : base + low + PANEL, :] - u[:, :size]
                pw[s * PANEL : s * PANEL + PANEL, :] = dw[base + low : base + low + PANEL, :] - u[:, size:]
                if low + PANEL < end:
                    pending.append((base, lhs, rhs))
        for base, lhs, rhs in pending:
            u = mm(lhs[:, low + PANEL : end], rhs, TN)
            lo, hi = base + low + PANEL, base + end
            dm[lo:hi, :] = dm[lo:hi, :] - u[:, :size]
            dw[lo:hi, :] = dw[lo:hi, :] - u[:, size:]


def after_kernel(
    g_ref, w_ref, m1_ref, m2_ref, l_ref, ql_ref, s_ref, q_ref, a_ref, m_ref,
    w_out, m1_out, m2_out, l_out, s_out, qln_out, q_out, c_out,
    gram, gram_left, x_left, dm, dw, pm, pw, um, uw,
):
    step = pl.program_id(0)
    count = pl.num_programs(0)
    n = q_out.shape[0]
    width = g_ref.shape[2]
    rows = g_ref.shape[1]
    g = g_ref[0]
    q = split(q_ref[0])
    ql = split(ql_ref[0])
    p = mm(g, q[0], NN) + mm(g, q[1], NN)
    turned = mm3(ql, p, TN)
    first = 0.9 * m1_ref[0] + 0.1 * turned
    second = 0.999 * m2_ref[0] + 0.001 * turned * turned
    m1_out[0] = first
    m2_out[0] = second
    direction = first / FIX_ONE / (jnp.sqrt(second / FIX_TWO) + 1e-08)
    update = mm3(ql, mm3(direction, q, NT), NN)
    weight = w_ref[0]
    weight = weight - rate_matrix * (update + 0.01 * weight)
    w_out[0] = weight
    c_out[0] = weight.astype(BF)
    k = mm(g, g, NT)
    left = 0.95 * l_ref[0] + 0.05 * k
    l_out[0] = left
    s_out[0] = 0.95 * s_ref[0] + 0.05 * mm(g, g, TN)
    a = a_ref[0]
    a_parts = split(a)
    b = 0.05 * p
    bh, bl = split(b)
    h = mm(g, a_parts[0], NN) + mm(g, a_parts[1], NN) + 0.5 * mm3(k, (bh, bl), NN)
    q_out[step] = a + mm(jnp.concatenate([g, g], axis=0), jnp.concatenate([bh, bl], axis=0), TN)
    hh, hl = split(h)
    y = jnp.concatenate([hh, bh, hh, bh, hl, bl], axis=0)
    z = jnp.concatenate([bh, hh, bl, hl, bh, hh], axis=0)
    blk = BLOCK
    for i in range(width // blk):
        lo = i * blk
        gram[step, lo : lo + blk, lo:] = m_ref[0, lo : lo + blk, lo:] + mm(y[:, lo : lo + blk], z[:, lo:], TN)
    xl = mm3(left, ql, NN)
    x_left[step] = xl
    gl = mm3(xl, xl, TN)
    gram_left[step] = gl

    @pl.when(step == count - 1)
    def _():
        eye = (lax.broadcasted_iota(jnp.int32, (blk, blk), 0) == lax.broadcasted_iota(jnp.int32, (blk, blk), 1)).astype(F32)
        blocks = width // blk

        def at(s):
            return slice(s * blk, s * blk + blk)

        for s in range(n):
            dm[at(s), :] = eye
            dm[s * blk : s * blk + rows, :rows] = gram_left[s]
            dw[at(s), :] = eye
        factor_panels(dm, dw, pm, pw, um, uw, n, rows // PANEL)
        for s in range(n):
            qln_out[s] = mm3(x_left[s], dw[s * blk : s * blk + rows, :rows], NT)

        def block_step(kk, carry):
            for kb in range(blocks):
                @pl.when(kk == kb)
                def _():
                    for s in range(n):
                        dm[at(s), :] = gram[s, kb * blk : kb * blk + blk, kb * blk : kb * blk + blk]
            for s in range(n):
                dw[at(s), :] = eye
            factor_panels(dm, dw, pm, pw, um, uw, n, blk // PANEL)

            for kb in range(blocks):
                @pl.when(kk == kb)
                def _():
                    lo = kb * blk
                    hi = lo + blk

                    def one(s, c):
                        inv = dw[pl.ds(pl.multiple_of(s * blk, blk), blk), :]
                        gram[s, lo:hi, lo:hi] = inv
                        if blocks == 1:
                            return c
                        ih, il = split(inv)
                        lhs = jnp.concatenate([ih, ih, il], axis=1)

                        def scaled(part):
                            ph, plo = split(part)
                            return mm(lhs, jnp.concatenate([ph, plo, ph], axis=0), NN)

                        if kb > 0:
                            gram[s, lo:hi, :lo] = scaled(gram[s, lo:hi, :lo])
                        if hi < width:
                            up = scaled(gram[s, lo:hi, hi:])
                            uh, ul = split(up)
                            rh, rl = split(gram[s, lo:hi, :hi])
                            us = jnp.concatenate([uh, uh, ul], axis=0)
                            vs = jnp.concatenate([uh, ul, uh], axis=0)
                            rs = jnp.concatenate([rh, rl, rh], axis=0)
                            below = mm(us, rs, TN)
                            if kb > 0:
                                gram[s, hi:, :lo] = gram[s, hi:, :lo] - below[:, :lo]
                            gram[s, hi:, lo:hi] = -below[:, lo:]
                            for i in range(kb + 1, blocks):
                                b0 = i * blk
                                gram[s, b0 : b0 + blk, b0:] = gram[s, b0 : b0 + blk, b0:] - mm(
                                    us[:, b0 - hi : b0 - hi + blk], vs[:, b0 - hi :], TN
                                )
                        return c

                    lax.fori_loop(0, n, one, 0, unroll=min(n, 4))
            return carry

        lax.fori_loop(0, blocks, block_step, 0)

        def finish(s, c):
            x = split(q_out[s])
            for i in range(0, width, 2 * blk):
                hi = i + 2 * blk
                zz = gram[s, i:hi, :hi]
                r_i = lax.broadcasted_iota(jnp.int32, (2 * blk, hi), 0) + i
                c_i = lax.broadcasted_iota(jnp.int32, (2 * blk, hi), 1)
                zz = jnp.where(c_i <= r_i, zz, 0.0)
                q_out[s, :, i:hi] = mm3((x[0][:, :hi], x[1][:, :hi]), zz, NT)
            return c

        lax.fori_loop(0, n, finish, 0, unroll=min(n, 2))


def after(grad, weight, m1, m2, left, ql, stat, q, a, m):
    n, rows, width = weight.shape
    wide = pl.BlockSpec((1, width, width), lambda i: (i, 0, 0))
    flat = pl.BlockSpec((1, rows, width), lambda i: (i, 0, 0))
    small = pl.BlockSpec((1, rows, rows), lambda i: (i, 0, 0))
    sd = jax.ShapeDtypeStruct
    return pl.pallas_call(
        after_kernel,
        grid=(n,),
        in_specs=[flat, flat, flat, flat, small, small, wide, wide, wide, wide],
        out_specs=[
            flat, flat, flat, small, wide,
            pl.BlockSpec((n, rows, rows), lambda i: (0, 0, 0)),
            pl.BlockSpec((n, width, width), lambda i: (0, 0, 0)),
            flat,
        ],
        out_shape=[
            sd(weight.shape, F32), sd(weight.shape, F32), sd(weight.shape, F32), sd(left.shape, F32), sd(stat.shape, F32),
            sd(ql.shape, F32), sd(q.shape, F32), sd(weight.shape, BF),
        ],
        scratch_shapes=[
            pltpu.VMEM((n, width, width), F32),
            pltpu.VMEM((n, rows, rows), F32),
            pltpu.VMEM((n, rows, rows), F32),
            pltpu.VMEM((n * BLOCK, BLOCK), F32),
            pltpu.VMEM((n * BLOCK, BLOCK), F32),
            pltpu.VMEM((n * PANEL, BLOCK), F32),
            pltpu.VMEM((n * PANEL, BLOCK), F32),
            pltpu.VMEM((n * PANEL, BLOCK), F32),
            pltpu.VMEM((n * PANEL, BLOCK), F32),
        ],
        compiler_params=pltpu.CompilerParams(vmem_limit_bytes=62 << 20),
        cost_estimate=pl.CostEstimate(flops=n * 12 * width**3, bytes_accessed=n * 24 * width * width, transcendentals=0),
        name="after",
    )(grad, weight, m1, m2, left, ql, stat, q, a, m)


def swap_core(values):
    count = lax.axis_size("tensor")
    return lax.ppermute(values, "tensor", [(i, i ^ 1) for i in range(count)])


def chip_bits():
    bit, bits = 2, []
    while bit < lax.axis_size("tensor"):
        bits.append(bit)
        bit *= 2
    return bits


def swap_chip(values, bit):
    count = lax.axis_size("tensor")
    return lax.ppermute(values, "tensor", [(i, i ^ bit) for i in range(count)])


def gather_chips(rows):
    for bit in chip_bits():
        other = swap_chip(rows, bit)
        upper = (lax.axis_index("tensor") & bit) != 0
        rows = jnp.where(
            upper, jnp.concatenate([other, rows], axis=0), jnp.concatenate([rows, other], axis=0)
        )
    return rows


def sum_chips(part):
    for bit in chip_bits():
        part = part.astype(BF)
        part = part.astype(F32) + swap_chip(part, bit).astype(F32)
    return part.astype(F32)


def own_rows(values):
    chips = lax.axis_size("tensor") // 2
    count = values.shape[0] // chips
    return lax.dynamic_slice_in_dim(values, (lax.axis_index("tensor") // 2) * count, count, 0)


def sum_chips_own(part):
    for bit in reversed(chip_bits()):
        half = part.shape[0] // 2
        upper = (lax.axis_index("tensor") & bit) != 0
        keep = jnp.where(upper, part[half:], part[:half])
        give = jnp.where(upper, part[:half], part[half:]).astype(BF)
        part = keep.astype(F32) + swap_chip(give, bit).astype(F32)
    return part


def sum_everywhere(values):
    values = values + swap_core(values)
    count = lax.axis_size("dp")
    if count & (count - 1):
        return lax.psum(values, "dp")
    bit = 1
    while bit < count:
        values = values + lax.ppermute(values, "dp", [(i, i ^ bit) for i in range(count)])
        bit *= 2
    return values


def project(rows, matrix):
    return mm(rows, matrix, NT)


def join_core(own, width):
    other = swap_core(own)
    half = width // 2
    parts = []
    for start in range(0, own.shape[1], width):
        parts.append(other[:, start + half : start + width])
        parts.append(other[:, start : start + half])
    return jnp.concatenate([own, jnp.concatenate(parts, axis=1)], axis=0)


def attention_scores(query, key, allowed):
    scale = query.shape[-1] ** (-0.5)
    scores = jnp.einsum("qhe,khe->hqk", query, key, preferred_element_type=F32) * scale
    return jnp.where(allowed[None], scores, -1e30)


def heads_of(rows, size):
    return rows.reshape(rows.shape[0], -1, size)


def attention_forward(query_rows, key_rows, weights, allowed, size):
    w_query, w_key, w_value, w_out = weights
    width = w_query.shape[0]
    query = project(query_rows, w_query).astype(BF)
    pair = project(key_rows, jnp.concatenate([w_key, w_value], axis=0)).astype(BF)
    pair = join_core(pair, width)
    key, value = pair[:, :width], pair[:, width:]
    scores = attention_scores(heads_of(query, size), heads_of(key, size), allowed)
    top = jnp.max(scores, axis=-1, keepdims=True)
    powers = jnp.exp(scores - top)
    total = jnp.sum(powers, axis=-1, keepdims=True)
    chance = powers / total
    log_total = top + jnp.log(total)
    mixed = jnp.einsum("hqk,khe->qhe", chance.astype(BF), heads_of(value, size), preferred_element_type=F32)
    mixed = mixed.astype(BF).reshape(query.shape)
    return mm(mixed, w_out, NN), (query, key, value, log_total, mixed)


def attention_backward(grad, saved, weights, query_rows, key_rows, allowed, size):
    w_query, w_key, w_value, w_out = weights
    query, key, value, log_total, mixed = saved
    width = query.shape[1]
    own = key_rows.shape[0]
    grad_b = grad.astype(BF)
    grad_mixed = heads_of(mm(grad_b, w_out, NT).astype(BF), size)
    grad_out_w = mm(mixed, grad_b, TN)
    query_h, key_h, value_h = heads_of(query, size), heads_of(key, size), heads_of(value, size)
    scores = attention_scores(query_h, key_h, allowed)
    chance = jnp.exp(scores - log_total)
    grad_value = jnp.einsum("hqk,qhe->khe", chance.astype(BF), grad_mixed, preferred_element_type=F32)
    grad_chance = jnp.einsum("qhe,khe->hqk", grad_mixed, value_h, preferred_element_type=F32)
    inner = jnp.sum(chance * grad_chance, axis=-1, keepdims=True)
    grad_score = (chance * (grad_chance - inner)).astype(BF)
    scale = size ** (-0.5)
    grad_query = jnp.einsum("hqk,khe->qhe", grad_score, key_h, preferred_element_type=F32) * scale
    grad_key = jnp.einsum("hqk,qhe->khe", grad_score, query_h, preferred_element_type=F32) * scale
    grad_query = grad_query.astype(BF).reshape(query.shape)
    both = jnp.concatenate([grad_key.reshape(key.shape), grad_value.reshape(key.shape)], axis=1)
    half = width // 2
    away = both[own:].astype(BF)
    away = swap_core(away)
    away = jnp.concatenate(
        [away[:, half:width], away[:, :half], away[:, width + half :], away[:, width : width + half]], axis=1
    )
    both = (both[:own] + away.astype(F32)).astype(BF)
    grad_key, grad_value = both[:, :width], both[:, width:]
    grads = [
        mm(grad_query, query_rows, TN),
        mm(grad_key, key_rows, TN),
        mm(grad_value, key_rows, TN),
        grad_out_w,
    ]
    part_query = mm(grad_query, w_query, NN)
    part_key = mm(grad_key, w_key, NN) + mm(grad_value, w_value, NN)
    return grads, part_query, part_key


def gelu(values):
    return jax.nn.gelu(values, approximate=False)


def feed_forward(rows, w_in, w_down):
    hidden = project(rows, w_in)
    active = gelu(hidden).astype(BF)
    return mm(active, w_down, NN), (hidden, active)


def feed_backward(grad, saved, w_in, w_down, rows):
    hidden, active = saved
    grad_b = grad.astype(BF)
    grad_active = mm(grad_b, w_down, NT)
    grad_hidden = jax.vjp(gelu, hidden)[1](grad_active)[0].astype(BF)
    grads = [mm(grad_hidden, rows, TN), mm(active, grad_b, TN)]
    return grads, mm(grad_hidden, w_in, NN)


def per_device(
    source,
    target,
    out_grad,
    src_len,
    tgt_len,
    owners,
    master,
    rotated_first_moment,
    rotated_second_moment,
    stat_left,
    stat_right,
    basis_left,
    basis_right,
    norm_params,
    norm_one,
    norm_two,
):
    tensor_count = lax.axis_size("tensor")
    me = lax.axis_index("tensor")
    core = me & 1
    head_count = HEADS // tensor_count
    col_count = FFB // tensor_count
    capacity = master.shape[1]
    slot_count = capacity * lax.axis_size("dp")
    row_count = source.shape[1]
    block_rows = master.shape[2]
    width = master.shape[3]

    product, gram = before(stat_right[0], basis_right[0])
    gathered = lax.all_gather(master[0].astype(BF), "dp", axis=0, tiled=True)
    slot_of = slot_positions(owners[0], capacity)
    blocks = gathered[slot_of]
    other_blocks = swap_core(blocks)
    extents = [head_count] * 4 + [col_count] * 2 + [head_count] * 8 + [col_count] * 2
    matrices = []
    offset = 0
    for extent in extents:
        matrices.append(
            jnp.concatenate([blocks[offset : offset + extent], other_blocks[offset : offset + extent]], axis=0).reshape(
                2 * extent * block_rows, width
            )
        )
        offset += extent

    chips = tensor_count // 2
    local = lax.iota(jnp.int32, row_count * chips)
    own_pos = (local // row_count) * (2 * row_count) + core * row_count + local % row_count
    other_pos = own_pos + (1 - 2 * core) * row_count
    key_pos = jnp.concatenate([own_pos, other_pos])
    gains = norm_params[0]
    shifts = norm_params[1]
    src_size = src_len[0]
    tgt_size = tgt_len[0]
    total_rows = local.shape[0]
    enc_allowed = jnp.broadcast_to(key_pos[None, :] < src_size, (total_rows, 2 * total_rows))
    dec_allowed = (key_pos[None, :] <= own_pos[:, None]) & (key_pos[None, :] < tgt_size)
    keep_rows = (own_pos < tgt_size).astype(F32)[:, None]

    src = gather_chips(source[0])
    tgt = gather_chips(target[0])
    cot = gather_chips(out_grad[0])

    branch_one, saved_one = attention_forward(src, src, matrices[0:4], enc_allowed, block_rows)
    z_one = src.astype(F32) + sum_chips(branch_one)
    h_one, pull_one = jax.vjp(layer_norm, z_one, gains[0], shifts[0])
    h_one_b = h_one.astype(BF)
    branch_two, saved_two = feed_forward(h_one_b, matrices[4], matrices[5])
    z_two = h_one + sum_chips(branch_two)
    encoded, pull_two = jax.vjp(layer_norm, z_two, gains[1], shifts[1])
    encoded_b = encoded.astype(BF)
    branch_three, saved_three = attention_forward(tgt, tgt, matrices[6:10], dec_allowed, block_rows)
    z_three = tgt.astype(F32) + sum_chips(branch_three)
    g_one, pull_three = jax.vjp(layer_norm, z_three, gains[2], shifts[2])
    g_one_b = g_one.astype(BF)
    branch_four, saved_four = attention_forward(g_one_b, encoded_b, matrices[10:14], enc_allowed, block_rows)
    z_four = g_one + sum_chips(branch_four)
    g_two, pull_four = jax.vjp(layer_norm, z_four, gains[3], shifts[3])
    g_two_b = g_two.astype(BF)
    branch_five, saved_five = feed_forward(g_two_b, matrices[14], matrices[15])
    z_five = g_two + sum_chips(branch_five)
    normed, pull_five = jax.vjp(layer_norm, z_five, gains[4], shifts[4])
    decoded = own_rows((normed * keep_rows).astype(BF))

    grad_z_five, gain_five, shift_five = pull_five(cot.astype(F32) * keep_rows)
    weights_five, rows_five = feed_backward(grad_z_five, saved_five, matrices[14], matrices[15], g_two_b)
    grad_z_four, gain_four, shift_four = pull_four(grad_z_five + sum_chips(rows_five))
    weights_four, query_four, key_four = attention_backward(
        grad_z_four, saved_four, matrices[10:14], g_one_b, encoded_b, enc_allowed, block_rows
    )
    grad_encoded = sum_chips(key_four)
    grad_z_three, gain_three, shift_three = pull_three(grad_z_four + sum_chips(query_four))
    weights_three, query_three, key_three = attention_backward(
        grad_z_three, saved_three, matrices[6:10], tgt, tgt, dec_allowed, block_rows
    )
    tgt_grad = own_rows(grad_z_three) + sum_chips_own(query_three + key_three)
    grad_z_two, gain_two, shift_two = pull_two(grad_encoded)
    weights_two, rows_two = feed_backward(grad_z_two, saved_two, matrices[4], matrices[5], h_one_b)
    grad_z_one, gain_one, shift_one = pull_one(grad_z_two + sum_chips(rows_two))
    weights_one, query_one, key_one = attention_backward(
        grad_z_one, saved_one, matrices[0:4], src, src, enc_allowed, block_rows
    )
    src_grad = own_rows(grad_z_one) + sum_chips_own(query_one + key_one)

    def reduce_core(grads):
        mine, away = [], []
        for item in grads:
            half = item.shape[0] // 2
            mine.append(item[:half].reshape(-1, block_rows, width))
            away.append(item[half:].reshape(-1, block_rows, width))
        other = swap_core(jnp.concatenate(away, axis=0).astype(BF))
        return (jnp.concatenate(mine, axis=0) + other.astype(F32)).astype(BF)

    block_grad = jnp.concatenate(
        [reduce_core(item) for item in (weights_one, weights_two, weights_three, weights_four, weights_five)], axis=0
    )
    norm_local = jnp.stack(
        [
            jnp.stack([gain_one, gain_two, gain_three, gain_four, gain_five]),
            jnp.stack([shift_one, shift_two, shift_three, shift_four, shift_five]),
        ]
    )
    held = slot_of[None, :] == jnp.arange(slot_count, dtype=jnp.int32)[:, None]
    block_of = jnp.sum(jnp.where(held, jnp.arange(slot_of.shape[0], dtype=jnp.int32)[None, :], 0), axis=1)
    used = jnp.any(held, axis=1)
    in_slots = jnp.where(used[:, None, None], block_grad[block_of], 0)
    own_grad = lax.psum_scatter(in_slots, "dp", scatter_dimension=0, tiled=True)
    norm_grad = sum_everywhere(norm_local)
    results = after(
        own_grad,
        master[0],
        rotated_first_moment[0],
        rotated_second_moment[0],
        stat_left[0],
        basis_left[0],
        stat_right[0],
        basis_right[0],
        product,
        gram,
    )
    norm_one_new = 0.9 * norm_one + 0.1 * norm_grad
    norm_two_new = 0.999 * norm_two + 0.001 * norm_grad * norm_grad
    norm_new = norm_params - rate_vector * (norm_one_new / FIX_ONE) / (jnp.sqrt(norm_two_new / FIX_TWO) + 1e-08)
    return (
        decoded[None],
        src_grad[None],
        tgt_grad[None],
        results[0][None],
        results[1][None],
        results[2][None],
        results[3][None],
        results[4][None],
        results[5][None],
        results[6][None],
        results[7][None],
        norm_new,
        norm_one_new,
        norm_two_new,
    )


def solution(mesh):
    in_specs = (
        P("dp", "tensor", None),
        P("dp", "tensor", None),
        P("dp", "tensor", None),
        P("dp"),
        P("dp"),
        P("tensor", None),
        P("tensor", "dp", None, None),
        P("tensor", "dp", None, None),
        P("tensor", "dp", None, None),
        P("tensor", "dp", None, None),
        P("tensor", "dp", None, None),
        P("tensor", "dp", None, None),
        P("tensor", "dp", None, None),
        P(),
        P(),
        P(),
    )
    out_specs = (
        P("dp", "tensor", None),
        P("dp", "tensor", None),
        P("dp", "tensor", None),
        P("tensor", "dp", None, None),
        P("tensor", "dp", None, None),
        P("tensor", "dp", None, None),
        P("tensor", "dp", None, None),
        P("tensor", "dp", None, None),
        P("tensor", "dp", None, None),
        P("tensor", "dp", None, None),
        P("tensor", "dp", None, None),
        P(),
        P(),
        P(),
    )
    return jax.shard_map(
        per_device, mesh=mesh, in_specs=in_specs, out_specs=out_specs, check_vma=False
    )
```

time: 894 us -> 530 us (0.59)
  waiting for transfers between devices: 426 us -> 205 us
  Pallas kernels: 158 us -> 88.3 us
  matrix products: 135 us -> 76 us
  blocking collectives: 42.4 us -> 0 us
  starting transfers between devices: 2.36 us -> 21.5 us
  local copies, waits for them, and re-layouts: 40.6 us -> 52.2 us
    reduce_scatter x10 -> x0, waiting for transfers between devices: 189 us -> none  [the longest x5 108 us: scatter_rows(): lax.psum_scatter(term_fn(jnp.int32(0), row_count * lax.axis_size('tensor'...]
    all_gather x12 -> x1, waiting for transfers between devices: 199 us -> 77.2 us  [per_device(): gathered = lax.all_gather(master[0].astype(BF), 'dp', axis=0, tiled=True)]
    ppermute x0 -> x30, waiting for transfers between devices: none -> 84.7 us  [the longest x14 77.8 us: swap_chip(): return lax.ppermute(values, 'tensor', [(i, i ^ bit) for i in range(count)])]
    pallas_call x1, Pallas kernels: 141 us -> 71.3 us  [after(): pl.pallas_call(after_kernel, grid=(n,), in_specs=[flat, flat, flat, flat,...]
    dot_general x66 -> x63, matrix products: 135 us -> 76 us  [the longest x45 36.6 us: mm(): return lax.dot_general(a, b, dims, preferred_element_type=F32)]
    psum x1 -> x0, blocking collectives: 42.4 us -> none  [per_device(): norm_grad = lax.psum(norm_local, ('dp', 'tensor'))]
    ppermute x0 -> x30, starting transfers between devices: none -> 21.4 us  [the longest x14 17.9 us: swap_chip(): return lax.ppermute(values, 'tensor', [(i, i ^ bit) for i in range(count)])]
    concatenate x1 -> x26, other arithmetic: 1.56 us -> 13.4 us  [the longest x16 6.12 us: per_device(): jnp.concatenate([blocks[offset:offset + extent], other_blocks[offset:offs...]
  transfers between devices with their start and end apart: 23 -> 32, of which waited for: 20 -> 17; matrix products, arithmetic and copies ran while one was open for 15% -> 28% of each run, Pallas kernels for 2% -> 3%
where the time goes in v2:
time: 530 us; the launch traced here: 523 us
  waiting for transfers between devices  205 us (39%)
  Pallas kernels  88.3 us (17%)
  matrix products  76 us (14%)
  other arithmetic  61.2 us (12%)
  local copies, waits for them, and re-layouts  52.2 us (10%)
  starting transfers between devices  21.5 us (4%)
  between operations  18.8 us (4%)
    ppermute x14, waiting for transfers between devices, swap_chip(): return lax.ppermute(values, 'tensor', [(i, i ^ bit) for i in range(count)])  77.8 us
    all_gather x1, waiting for transfers between devices, per_device(): gathered = lax.all_gather(master[0].astype(BF), 'dp', axis=0, tiled=True)  77.2 us
    pallas_call x1, Pallas kernels, after(): pl.pallas_call(after_kernel, grid=(n,), in_specs=[flat, flat, flat, flat,...  71.3 us
    reduce_scatter x1, waiting for transfers between devices, per_device(): own_grad = lax.psum_scatter(in_slots, 'dp', scatter_dimension=0, tiled=True)  42.8 us
    dot_general x45, matrix products, mm(): return lax.dot_general(a, b, dims, preferred_element_type=F32)  36.6 us
    unnamed x358, local copies, waits for them, and re-layouts  24.6 us
    ppermute x14, starting transfers between devices, swap_chip(): return lax.ppermute(values, 'tensor', [(i, i ^ bit) for i in range(count)])  17.9 us
    pallas_call x1, Pallas kernels, before(): pl.pallas_call(before_kernel, grid=(n,), in_specs=[spec, spec], out_specs...  17.1 us
  transfers between devices with their start and end apart: 32, of which 17 were waited for; matrix products, arithmetic and copies ran while one was open for 28% of the time, Pallas kernels for 3%

profile of v2, /device:TPU:0, one launch (start us, length us, event | category | flops | bytes accessed | tf_op | source)
XLA Modules:
  0.0 522.7 jit_solution(2502624425503806678)
XLA Ops:
  7.2 2.1 bitcast_convert_fusion
  9.7 77.2 %all-gather.2.cloned.1.call-done = bf16[64,64,512]{2,1,0:T(8,128)(2,1)} async-done(((bf16[8,64,512]{2,1,0:T(8,128)(2,1)}), bf16[64,64,512]{2,1,0:T(8,128)(2,1)}) %all-gather.2.cloned.1.call-update) | async-done | bytes 4194320 | tf_op jit(solution)/shard_map/all_gather | solution.py:503
  86.9 4.9 gather_fusion
  100.9 2.3 fusion.182
  104.3 2.3 fusion.183
  106.7 6.0 %collective-permute-done.4 = bf16[256,512]{0,1:T(8,128)(2,1)S(1)} collective-permute-done((bf16[256,512]{0,1:T(8,128)(2,1)S(1)}, bf16[256,512]{0,1:T(8,128)(2,1)S(1)}, u32[]{:S(2)}, u32[]{:S(2)}) %collective-permute-start.4) | collective-permute-done | bytes 262176 | tf_op jit(solution)/shard_map/ppermute | solution.py:325
  119.0 2.6 fusion.181
  127.8 2.5 fusion.18
  130.3 2.2 fusion.1
  133.7 2.5 fusion.42
  143.3 2.5 fusion.46
  146.9 4.5 collective-permute-done.6
  152.5 7.0 %multiply_convert_fusion.4 = (bf16[512,1024]{1,0:T(8,128)(2,1)S(1)}, f32[512,1024]{1,0:T(8,128)}, f32[512,1024]{1,0:T(8,128)}) fusion(bf16[1024,512]{1,0:T(8,128)(2,1)S(1)} %bitcast.349, f32[512,512]{0,1:T(8,128)S(1)} %get-tuple-element.134, f32[512]{0:T(512)S(1)} %bitcast.421, f32[512]{0:T(512)S(1)} %bitcast.399, f32[512]{0:T(512)S(1)} %fusion.137, ...), kind=kOutput, calls=%fused_computation.67 | convolution fusion | flops 572260352 | bytes 7348224 | tf_op jit(solution)/shard_map/dot_general | solution.py:47
  162.7 10.3 %collective-permute-done.7 = bf16[512,512]{0,1:T(8,128)(2,1)S(1)} collective-permute-done((bf16[512,512]{0,1:T(8,128)(2,1)S(1)}, bf16[512,512]{0,1:T(8,128)(2,1)S(1)}, u32[]{:S(2)}, u32[]{:S(2)}) %collective-permute-start.7) | collective-permute-done | bytes 524320 | tf_op jit(solution)/shard_map/ppermute | solution.py:325
  178.1 2.1 copy.123
  180.2 2.1 copy.122
  182.3 2.4 fusion.19
  184.7 2.0 fusion.2
  186.8 2.7 fusion.41
  193.2 10.7 %collective-permute-done.9 = bf16[512,512]{0,1:T(8,128)(2,1)S(1)} collective-permute-done((bf16[512,512]{0,1:T(8,128)(2,1)S(1)}, bf16[512,512]{0,1:T(8,128)(2,1)S(1)}, u32[]{:S(2)}, u32[]{:S(2)}) %collective-permute-start.9) | collective-permute-done | bytes 524320 | tf_op jit(solution)/shard_map/ppermute | solution.py:325
  204.5 5.3 %multiply_convert_fusion.3 = (bf16[512,1024]{1,0:T(8,128)(2,1)S(1)}, f32[512,1024]{1,0:T(8,128)S(1)}, f32[512,1024]{1,0:T(8,128)S(1)}) fusion(bf16[1024,512]{1,0:T(8,128)(2,1)S(1)} %bitcast.355, f32[512,512]{0,1:T(8,128)S(1)} %get-tuple-element.126, f32[512]{0:T(512)S(1)} %bitcast.424, f32[512]{0:T(512)S(1)} %bitcast.410, f32[512]{0:T(512)S(1)} %fusion.139, ...), kind=kOutput, calls=%fused_computation.54 | convolution fusion | flops 572260352 | bytes 7348224 | tf_op jit(solution)/shard_map/dot_general | solution.py:47
  212.2 11.6 %collective-permute-done.10 = bf16[512,512]{0,1:T(8,128)(2,1)S(1)} collective-permute-done((bf16[512,512]{0,1:T(8,128)(2,1)S(1)}, bf16[512,512]{0,1:T(8,128)(2,1)S(1)}, u32[]{:S(2)}, u32[]{:S(2)}) %collective-permute-start.10) | collective-permute-done | bytes 524320 | tf_op jit(solution)/shard_map/ppermute | solution.py:325
  225.8 3.3 fusion.172
  236.7 6.8 %collective-permute-done.12 = bf16[512,512]{0,1:T(8,128)(2,1)S(1)} collective-permute-done((bf16[512,512]{0,1:T(8,128)(2,1)S(1)}, bf16[512,512]{0,1:T(8,128)(2,1)S(1)}, u32[]{:S(2)}, u32[]{:S(2)}) %collective-permute-start.12) | collective-permute-done | bytes 524320 | tf_op jit(solution)/shard_map/ppermute | solution.py:325
  247.2 2.6 multiply_reduce_fusion.2
  249.9 2.6 multiply_convert_fusion.2
  262.7 9.9 %collective-permute-done.18 = bf16[512,512]{0,1:T(8,128)(2,1)S(1)} collective-permute-done((bf16[512,512]{0,1:T(8,128)(2,1)S(1)}, bf16[512,512]{0,1:T(8,128)(2,1)S(1)}, u32[]{:S(2)}, u32[]{:S(2)}) %collective-permute-start.18) | collective-permute-done | bytes 524320 | tf_op jit(solution)/shard_map/ppermute | solution.py:325
  273.0 9.5 %collective-permute-done.14 = bf16[512,512]{0,1:T(8,128)(2,1)S(1)} collective-permute-done((bf16[512,512]{0,1:T(8,128)(2,1)S(1)}, bf16[512,512]{0,1:T(8,128)(2,1)S(1)}, u32[]{:S(2)}, u32[]{:S(2)}) %collective-permute-start.14) | collective-permute-done | bytes 524320 | tf_op jit(solution)/shard_map/ppermute | solution.py:325
  294.4 5.7 %collective-permute-done.15 = bf16[512,512]{0,1:T(8,128)(2,1)S(1)} collective-permute-done((bf16[512,512]{0,1:T(8,128)(2,1)S(1)}, bf16[512,512]{0,1:T(8,128)(2,1)S(1)}, u32[]{:S(2)}, u32[]{:S(2)}) %collective-permute-start.15) | collective-permute-done | bytes 524320 | tf_op jit(solution)/shard_map/ppermute | solution.py:325
  303.1 2.7 fusion.6
  305.8 4.4 multiply_reduce_fusion
  311.5 2.9 fusion.8
  314.4 2.7 multiply_reduce_fusion.1
  317.1 2.9 multiply_convert_fusion.1
  320.0 2.6 fusion.43
  325.6 2.0 multiply_convert_fusion
  338.5 2.7 fusion.48
  342.4 2.0 fusion.70
  344.4 2.6 fusion.47
  347.0 5.0 gather_fusion.1
  352.0 4.5 broadcast_select_fusion
  359.2 17.1 %before.1 = (f32[8,512,512]{2,1,0:T(8,128)}, f32[8,512,512]{2,1,0:T(8,128)}) custom-call(f32[8,512,512]{2,1,0:T(8,128)} %bitcast.441, f32[8,512,512]{2,1,0:T(8,128)} %bitcast.443), custom_call_target="tpu_custom_call" | custom-call | flops 12884901888 | bytes 33554432 | tf_op jit(solution)/shard_map/before/pallas_call | solution.py:69
  378.4 4.6 collective-permute-done.28
  389.0 2.0 select_convert_fusion.1
  394.5 2.0 copy.141
  396.6 2.4 collective-permute-done.17
  401.3 42.8 %reduce-scatter.2.cloned.1.call-done.g_ref = bf16[8,64,512]{2,1,0:T(8,128)(2,1)} async-done(((bf16[64,64,512]{2,1,0:T(8,128)(2,1)}), bf16[8,64,512]{2,1,0:T(8,128)(2,1)}) %reduce-scatter.2.cloned.1.call-update) | async-done | bytes 524304 | tf_op jit(solution)/shard_map/reduce_scatter | solution.py:599
  444.1 71.3 %after.1 = (f32[8,64,512]{2,1,0:T(8,128)}, f32[8,64,512]{2,1,0:T(8,128)}, f32[8,64,512]{2,1,0:T(8,128)}, f32[8,64,64]{2,1,0:T(8,128)}, f32[8,512,512]{2,1,0:T(8,...) custom-call(bf16[8,64,512]{2,1,0:T(8,128)(2,1)} %reduce-scatter.2.cloned.1.call-done.g_ref, ...), custom_call_target="tpu_custom_call" | custom-call | flops 12884901888 | bytes 50331648 | tf_op jit(solution)/shard_map/after/pallas_call | solution.py:279
  (627 shorter events, 116.5 us)
Async XLA Ops:
  7.2 79.7 %all-gather.2.cloned.1.call-start = ((), (), s32[]{:S(2)}) async-start(), calls=%async_computation.1 | async-start | bytes 4718592 | tf_op jit(solution)/shard_map/all_gather | solution.py:503
  9.3 434.8 %reduce-scatter.2.cloned.1.call-start = ((), (), s32[]{:S(2)}) async-start(), calls=%async_computation.2 | async-start | bytes 4718592 | tf_op jit(solution)/shard_map/reduce_scatter | solution.py:599
  9.6 82.1 %copy-start.109 = (bf16[1,256,512]{2,1,0:T(8,128)(2,1)S(1)}, bf16[1,256,512]{2,1,0:T(8,128)(2,1)}, u32[]{:S(2)}) copy-start(bf16[1,256,512]{2,1,0:T(8,128)(2,1)} %param.18) | copy-start | bytes 786436
  9.6 84.4 %copy-start.110 = (bf16[1,256,512]{2,1,0:T(8,128)(2,1)S(1)}, bf16[1,256,512]{2,1,0:T(8,128)(2,1)}, u32[]{:S(2)}) copy-start(bf16[1,256,512]{2,1,0:T(8,128)(2,1)} %param.17) | copy-start | bytes 786436
  9.6 85.2 %copy-start.111 = (bf16[1,256,512]{2,1,0:T(8,128)(2,1)S(1)}, bf16[1,256,512]{2,1,0:T(8,128)(2,1)}, u32[]{:S(2)}) copy-start(bf16[1,256,512]{2,1,0:T(8,128)(2,1)} %param.16) | copy-start | bytes 786436
  9.6 90.2 %copy-start.115 = (f32[2,5,512]{2,0,1:T(2,128)S(1)}, f32[2,5,512]{2,0,1:T(2,128)}, u32[]{:S(2)}) copy-start(f32[2,5,512]{2,0,1:T(2,128)} %param.29) | copy-start | bytes 61444
  91.7 12.6 %collective-permute-start.1 = (bf16[56,64,512]{2,1,0:T(8,128)(2,1)}, bf16[56,64,512]{2,1,0:T(8,128)(2,1)}, u32[]{:S(2)}, u32[]{:S(2)}) collective-permute-start(bf16[56,64,512]{2,1,0:T(8,128)(2,1)} %gather_fusion), channel_id=1, source_target_pairs={{0,1},{1,0},{2,3},{3,2},{4,5},{5,4},{6,7},{7,6},{8,9},{9,8},{10,11... | collective-permute-start | bytes 11010056 | tf_op jit(solution)/shard_map/ppermute | solution.py:312
  92.6 131.6 %collective-permute-start.11 = (bf16[256,512]{0,1:T(8,128)(2,1)}, bf16[256,512]{0,1:T(8,128)(2,1)}, u32[]{:S(2)}, u32[]{:S(2)}) collective-permute-start(bf16[256,512]{0,1:T(8,128)(2,1)} %bitcast.48), channel_id=1, source_target_pairs={{0,2},{1,3},{2,0},{3,1},{4,6},{5,7},{6,4},{7,5},{8,10},{9,11},{10,... | collective-permute-start | bytes 786440 | tf_op jit(solution)/shard_map/ppermute | solution.py:325
  94.2 30.7 %copy-start.69 = (bf16[1,256,512]{1,2,0:T(8,128)(2,1)}, bf16[1,256,512]{1,2,0:T(8,128)(2,1)S(1)}, u32[]{:S(2)}) copy-start(bf16[1,256,512]{1,2,0:T(8,128)(2,1)S(1)} %copy.116) | copy-start | bytes 786436
  94.2 19.9 %collective-permute-start = (bf16[256,512]{0,1:T(8,128)(2,1)S(1)}, bf16[256,512]{0,1:T(8,128)(2,1)S(1)}, u32[]{:S(2)}, u32[]{:S(2)}) collective-permute-start(bf16[256,512]{0,1:T(8,128)(2,1)S(1)} %bitcast.334), channel_id=1, source_target_pairs={{0,2},{1,3},{2,0},{3,1},{4,6},{5,7},{6,4},{7,5},{8,10},{9,11},{10,... | collective-permute-start | bytes 786440 | tf_op jit(solution)/shard_map/ppermute | solution.py:325
  94.9 28.9 %copy-start.72 = (bf16[1,256,512]{1,2,0:T(8,128)(2,1)}, bf16[1,256,512]{1,2,0:T(8,128)(2,1)S(1)}, u32[]{:S(2)}) copy-start(bf16[1,256,512]{1,2,0:T(8,128)(2,1)S(1)} %copy.119) | copy-start | bytes 786436
  95.0 17.8 %collective-permute-start.4 = (bf16[256,512]{0,1:T(8,128)(2,1)S(1)}, bf16[256,512]{0,1:T(8,128)(2,1)S(1)}, u32[]{:S(2)}, u32[]{:S(2)}) collective-permute-start(bf16[256,512]{0,1:T(8,128)(2,1)S(1)} %bitcast.341), channel_id=1, source_target_pairs={{0,2},{1,3},{2,0},{3,1},{4,6},{5,7},{6,4},{7,5},{8,10},{9,11},{10,... | collective-permute-start | bytes 786440 | tf_op jit(solution)/shard_map/ppermute | solution.py:325
  98.4 88.3 %copy-start.112 = (pred[1024]{0:T(1024)(128)(4,1)}, pred[1024]{0:T(1024)(128)(4,1)S(1)}, u32[]{:S(2)}) copy-start(pred[1024]{0:T(1024)(128)(4,1)S(1)} %get-tuple-element.211) | copy-start | bytes 3076
  100.5 52.0 %copy-start.153 = (f32[1,1,512]{2,0,1:T(1,128)}, f32[1,1,512]{2,0,1:T(1,128)S(1)}, u32[]{:S(2)}) copy-start(f32[1,1,512]{2,0,1:T(1,128)S(1)} %get-tuple-element.206) | copy-start | bytes 6148
  100.5 72.5 %copy-start.118 = (f32[1,1,512]{2,0,1:T(1,128)}, f32[1,1,512]{2,0,1:T(1,128)S(1)}, u32[]{:S(2)}) copy-start(f32[1,1,512]{2,0,1:T(1,128)S(1)} %get-tuple-element.207) | copy-start | bytes 6148
  103.2 20.6 %copy-start.43 = (bf16[2,64,512]{2,1,0:T(8,128)(2,1)}, bf16[2,64,512]{2,1,0:T(8,128)(2,1)S(1)}, u32[]{:S(2)}) copy-start(bf16[2,64,512]{2,1,0:T(8,128)(2,1)S(1)} %get-tuple-element.152) | copy-start | bytes 393220
  113.9 11.2 %collective-permute-start.5 = (bf16[512,512]{1,0:T(8,128)(2,1)S(1)}, bf16[512,512]{1,0:T(8,128)(2,1)S(1)}, u32[]{:S(2)}, u32[]{:S(2)}) collective-permute-start(bf16[512,512]{1,0:T(8,128)(2,1)S(1)} %convolution_convert_fusion.1), channel_id=1, source_target_pairs={{0,1},{1,0},{2,3},{3,2},{4,5},{5,4},{6,7},{7,6},{8,9},{9,8},{10,11... | collective-permute-start | bytes 1572872 | tf_op jit(solution)/shard_map/ppermute | solution.py:312
  116.3 9.7 %collective-permute-start.2 = (bf16[512,512]{1,0:T(8,128)(2,1)}, bf16[512,512]{1,0:T(8,128)(2,1)S(1)}, u32[]{:S(2)}, u32[]{:S(2)}) collective-permute-start(bf16[512,512]{1,0:T(8,128)(2,1)} %convolution_convert_fusion.2), channel_id=1, source_target_pairs={{0,1},{1,0},{2,3},{3,2},{4,5},{5,4},{6,7},{7,6},{8,9},{9,8},{10,11... | collective-permute-start | bytes 1572872 | tf_op jit(solution)/shard_map/ppermute | solution.py:312
  136.6 14.9 %collective-permute-start.6 = (bf16[512,512]{0,1:T(8,128)(2,1)S(1)}, bf16[512,512]{0,1:T(8,128)(2,1)S(1)}, u32[]{:S(2)}, u32[]{:S(2)}) collective-permute-start(bf16[512,512]{0,1:T(8,128)(2,1)S(1)} %fusion.38), channel_id=1, source_target_pairs={{0,2},{1,3},{2,0},{3,1},{4,6},{5,7},{6,4},{7,5},{8,10},{9,11},{10,... | collective-permute-start | bytes 1572872 | tf_op jit(solution)/shard_map/ppermute | solution.py:325
  146.3 15.9 %collective-permute-start.3 = (bf16[512,512]{0,1:T(8,128)(2,1)S(1)}, bf16[512,512]{0,1:T(8,128)(2,1)S(1)}, u32[]{:S(2)}, u32[]{:S(2)}) collective-permute-start(bf16[512,512]{0,1:T(8,128)(2,1)S(1)} %fusion.37), channel_id=1, source_target_pairs={{0,2},{1,3},{2,0},{3,1},{4,6},{5,7},{6,4},{7,5},{8,10},{9,11},{10,... | collective-permute-start | bytes 1572872 | tf_op jit(solution)/shard_map/ppermute | solution.py:325
  151.9 21.0 %copy-start.126 = (f32[512]{0:T(512)}, f32[512]{0:T(512)S(1)}, u32[]{:S(2)}) copy-start(f32[512]{0:T(512)S(1)} %fusion.137) | copy-start | bytes 6148
  160.3 12.6 %collective-permute-start.7 = (bf16[512,512]{0,1:T(8,128)(2,1)S(1)}, bf16[512,512]{0,1:T(8,128)(2,1)S(1)}, u32[]{:S(2)}, u32[]{:S(2)}) collective-permute-start(bf16[512,512]{0,1:T(8,128)(2,1)S(1)} %convolution_convert_fusion.6), channel_id=1, source_target_pairs={{0,2},{1,3},{2,0},{3,1},{4,6},{5,7},{6,4},{7,5},{8,10},{9,11},{10,... | collective-permute-start | bytes 1572872 | tf_op jit(solution)/shard_map/ppermute | solution.py:325
  174.9 2.0 collective-permute-start.8
  189.9 14.0 %collective-permute-start.9 = (bf16[512,512]{0,1:T(8,128)(2,1)S(1)}, bf16[512,512]{0,1:T(8,128)(2,1)S(1)}, u32[]{:S(2)}, u32[]{:S(2)}) collective-permute-start(bf16[512,512]{0,1:T(8,128)(2,1)S(1)} %fusion.39), channel_id=1, source_target_pairs={{0,2},{1,3},{2,0},{3,1},{4,6},{5,7},{6,4},{7,5},{8,10},{9,11},{10,... | collective-permute-start | bytes 1572872 | tf_op jit(solution)/shard_map/ppermute | solution.py:325
  210.6 13.2 %collective-permute-start.10 = (bf16[512,512]{0,1:T(8,128)(2,1)S(1)}, bf16[512,512]{0,1:T(8,128)(2,1)S(1)}, u32[]{:S(2)}, u32[]{:S(2)}) collective-permute-start(bf16[512,512]{0,1:T(8,128)(2,1)S(1)} %convolution_convert_fusion.5), channel_id=1, source_target_pairs={{0,2},{1,3},{2,0},{3,1},{4,6},{5,7},{6,4},{7,5},{8,10},{9,11},{10,... | collective-permute-start | bytes 1572872 | tf_op jit(solution)/shard_map/ppermute | solution.py:325
  212.2 102.2 %copy-start.117 = (f32[4,512]{1,0:T(4,128)}, f32[4,512]{1,0:T(4,128)S(1)}, u32[]{:S(2)}) copy-start(f32[4,512]{1,0:T(4,128)S(1)} %log_add_fusion.1) | copy-start | bytes 24580
  231.2 12.3 %collective-permute-start.12 = (bf16[512,512]{0,1:T(8,128)(2,1)S(1)}, bf16[512,512]{0,1:T(8,128)(2,1)S(1)}, u32[]{:S(2)}, u32[]{:S(2)}) collective-permute-start(bf16[512,512]{0,1:T(8,128)(2,1)S(1)} %convolution_convert_fusion.4), channel_id=1, source_target_pairs={{0,2},{1,3},{2,0},{3,1},{4,6},{5,7},{6,4},{7,5},{8,10},{9,11},{10,... | collective-permute-start | bytes 1572872 | tf_op jit(solution)/shard_map/ppermute | solution.py:325
  236.7 107.7 %collective-permute-start.25 = (bf16[16,64,512]{2,1,0:T(8,128)(2,1)}, bf16[16,64,512]{2,1,0:T(8,128)(2,1)}, u32[]{:S(2)}, u32[]{:S(2)}) collective-permute-start(bf16[16,64,512]{2,1,0:T(8,128)(2,1)} %pad_maximum_fusion.8), channel_id=1, source_target_pairs={{0,1},{1,0},{2,3},{3,2},{4,5},{5,4},{6,7},{7,6},{8,9},{9,8},{10,11... | collective-permute-start | bytes 3145736 | tf_op jit(solution)/shard_map/ppermute | solution.py:312
  254.9 4.3 collective-permute-start.13
  257.7 14.9 %collective-permute-start.18 = (bf16[512,512]{0,1:T(8,128)(2,1)S(1)}, bf16[512,512]{0,1:T(8,128)(2,1)S(1)}, u32[]{:S(2)}, u32[]{:S(2)}) collective-permute-start(bf16[512,512]{0,1:T(8,128)(2,1)S(1)} %fusion.40), channel_id=1, source_target_pairs={{0,2},{1,3},{2,0},{3,1},{4,6},{5,7},{6,4},{7,5},{8,10},{9,11},{10,... | collective-permute-start | bytes 1572872 | tf_op jit(solution)/shard_map/ppermute | solution.py:325
  261.1 81.2 %collective-permute-start.24 = (bf16[8,64,512]{2,1,0:T(8,128)(2,1)}, bf16[8,64,512]{2,1,0:T(8,128)(2,1)}, u32[]{:S(2)}, u32[]{:S(2)}) collective-permute-start(bf16[8,64,512]{2,1,0:T(8,128)(2,1)} %pad_maximum_fusion.11), channel_id=1, source_target_pairs={{0,1},{1,0},{2,3},{3,2},{4,5},{5,4},{6,7},{7,6},{8,9},{9,8},{10,11... | collective-permute-start | bytes 1572872 | tf_op jit(solution)/shard_map/ppermute | solution.py:312
  261.8 20.7 %copy-start.132 = (f32[512]{0:T(512)S(1)}, f32[512]{0:T(512)}, u32[]{:S(2)}) copy-start(f32[512]{0:T(512)} %copy-done.131) | copy-start | bytes 6148
  261.8 20.7 %copy-start.136 = (f32[1,1,512]{2,0,1:T(1,128)S(1)}, f32[1,1,512]{2,0,1:T(1,128)}, u32[]{:S(2)}) copy-start(f32[1,1,512]{2,0,1:T(1,128)} %get-tuple-element.205) | copy-start | bytes 6148
  261.9 20.7 %copy-start.138 = (f32[512]{0:T(512)S(1)}, f32[512]{0:T(512)}, u32[]{:S(2)}) copy-start(f32[512]{0:T(512)} %copy-done.137) | copy-start | bytes 6148
  261.9 20.7 %collective-permute-start.14 = (bf16[512,512]{0,1:T(8,128)(2,1)S(1)}, bf16[512,512]{0,1:T(8,128)(2,1)S(1)}, u32[]{:S(2)}, u32[]{:S(2)}) collective-permute-start(bf16[512,512]{0,1:T(8,128)(2,1)S(1)} %fusion.36), channel_id=1, source_target_pairs={{0,2},{1,3},{2,0},{3,1},{4,6},{5,7},{6,4},{7,5},{8,10},{9,11},{10,... | collective-permute-start | bytes 1572872 | tf_op jit(solution)/shard_map/ppermute | solution.py:325
  287.4 12.7 %collective-permute-start.15 = (bf16[512,512]{0,1:T(8,128)(2,1)S(1)}, bf16[512,512]{0,1:T(8,128)(2,1)S(1)}, u32[]{:S(2)}, u32[]{:S(2)}) collective-permute-start(bf16[512,512]{0,1:T(8,128)(2,1)S(1)} %convolution_convert_fusion.3), channel_id=1, source_target_pairs={{0,2},{1,3},{2,0},{3,1},{4,6},{5,7},{6,4},{7,5},{8,10},{9,11},{10,... | collective-permute-start | bytes 1572872 | tf_op jit(solution)/shard_map/ppermute | solution.py:325
  294.4 44.1 %collective-permute-start.22 = (bf16[16,64,512]{2,1,0:T(8,128)(2,1)}, bf16[16,64,512]{2,1,0:T(8,128)(2,1)}, u32[]{:S(2)}, u32[]{:S(2)}) collective-permute-start(bf16[16,64,512]{2,1,0:T(8,128)(2,1)} %pad_maximum_fusion.7), channel_id=1, source_target_pairs={{0,1},{1,0},{2,3},{3,2},{4,5},{5,4},{6,7},{7,6},{8,9},{9,8},{10,11... | collective-permute-start | bytes 3145736 | tf_op jit(solution)/shard_map/ppermute | solution.py:312
  329.1 4.3 collective-permute-start.16
  333.3 2.0 collective-permute-start.19
  334.5 2.4 collective-permute-start.21
  336.7 4.5 collective-permute-start.23
  357.3 1.3 collective-permute-start.26
  358.6 17.8 %collective-permute-start.27 = (f32[2,5,512]{2,1,0:T(8,128)S(1)}, f32[2,5,512]{2,1,0:T(8,128)S(1)}, u32[]{:S(2)}, u32[]{:S(2)}) collective-permute-start(f32[2,5,512]{2,1,0:T(8,128)S(1)} %fusion.155), channel_id=1, source_target_pairs={{0,4},{4,0},{8,12},{12,8},{16,20},{20,16},{24,28},{28,24},{1,5},{5... | collective-permute-start | bytes 61448 | tf_op jit(solution)/shard_map/ppermute | solution.py:368
  359.2 18.1 %copy-start.159 = (f32[1,1,512]{2,0,1:T(1,128)S(1)}, f32[1,1,512]{2,0,1:T(1,128)}, u32[]{:S(2)}) copy-start(f32[1,1,512]{2,0,1:T(1,128)} %get-tuple-element.200) | copy-start | bytes 6148
  376.4 6.6 %collective-permute-start.28 = (f32[2,5,512]{2,1,0:T(8,128)S(1)}, f32[2,5,512]{2,1,0:T(8,128)S(1)}, u32[]{:S(2)}, u32[]{:S(2)}) collective-permute-start(f32[2,5,512]{2,1,0:T(8,128)S(1)} %fusion.265), channel_id=1, source_target_pairs={{0,8},{4,12},{8,0},{12,4},{16,24},{20,28},{24,16},{28,20},{1,9},{5... | collective-permute-start | bytes 61448 | tf_op jit(solution)/shard_map/ppermute | solution.py:368
  383.0 8.6 %collective-permute-start.29 = (f32[2,5,512]{2,1,0:T(8,128)S(1)}, f32[2,5,512]{2,1,0:T(8,128)S(1)}, u32[]{:S(2)}, u32[]{:S(2)}) collective-permute-start(f32[2,5,512]{2,1,0:T(8,128)S(1)} %add.446), channel_id=1, source_target_pairs={{0,16},{4,20},{8,24},{12,28},{16,0},{20,4},{24,8},{28,12},{1,17},{... | collective-permute-start | bytes 61448 | tf_op jit(solution)/shard_map/ppermute | solution.py:368
  385.3 8.2 %collective-permute-start.20 = (bf16[256,512]{0,1:T(8,128)(2,1)S(1)}, bf16[256,512]{0,1:T(8,128)(2,1)S(1)}, u32[]{:S(2)}, u32[]{:S(2)}) collective-permute-start(bf16[256,512]{0,1:T(8,128)(2,1)S(1)} %select_convert_fusion), channel_id=1, source_target_pairs={{0,2},{1,3},{2,0},{3,1},{4,6},{5,7},{6,4},{7,5},{8,10},{9,11},{10,... | collective-permute-start | bytes 786440 | tf_op jit(solution)/shard_map/ppermute | solution.py:325
  391.1 7.9 %collective-permute-start.17 = (bf16[256,512]{0,1:T(8,128)(2,1)}, bf16[256,512]{0,1:T(8,128)(2,1)S(1)}, u32[]{:S(2)}, u32[]{:S(2)}) collective-permute-start(bf16[256,512]{0,1:T(8,128)(2,1)} %select_convert_fusion.1), channel_id=1, source_target_pairs={{0,2},{1,3},{2,0},{3,1},{4,6},{5,7},{6,4},{7,5},{8,10},{9,11},{10,... | collective-permute-start | bytes 786440 | tf_op jit(solution)/shard_map/ppermute | solution.py:325
  (173 other events, 712.7 us)
Sparse Core Ops, SparseCore 0:
  10.7 76.0 all-gather.1
  356.7 87.4 reduce-scatter.1

commit v3 on v2

--- a/solution.py
+++ b/solution.py
@@ -63,15 +63,16 @@
     m_ref[0, half:, half:] = mm3((ah[:, half:], al[:, half:]), (ah[:, half:], al[:, half:]), TN)
 
 
-def before(stat, basis):
-    n, w, _ = stat.shape
+def before(stat, basis, start, n):
+    w = stat.shape[1]
+    take = pl.BlockSpec((1, w, w), lambda i: (i + start, 0, 0))
     spec = pl.BlockSpec((1, w, w), lambda i: (i, 0, 0))
     return pl.pallas_call(
         before_kernel,
         grid=(n,),
-        in_specs=[spec, spec],
+        in_specs=[take, take],
         out_specs=[spec, spec],
-        out_shape=[jax.ShapeDtypeStruct(stat.shape, F32)] * 2,
+        out_shape=[jax.ShapeDtypeStruct((n, w, w), F32)] * 2,
         compiler_params=pltpu.CompilerParams(vmem_limit_bytes=60 << 20),
         cost_estimate=pl.CostEstimate(flops=n * 12 * w**3, bytes_accessed=n * 16 * w * w, transcendentals=0),
         name="before",
@@ -141,7 +142,7 @@
 
 
 def after_kernel(
-    g_ref, w_ref, m1_ref, m2_ref, l_ref, ql_ref, s_ref, q_ref, a_ref, m_ref,
+    g_ref, w_ref, m1_ref, m2_ref, l_ref, ql_ref, s_ref, q_ref, ae_ref, me_ref, al_ref, ml_ref,
     w_out, m1_out, m2_out, l_out, s_out, qln_out, q_out, c_out,
     gram, gram_left, x_left, dm, dw, pm, pw, um, uw,
 ):
@@ -169,7 +170,8 @@
     left = 0.95 * l_ref[0] + 0.05 * k
     l_out[0] = left
     s_out[0] = 0.95 * s_ref[0] + 0.05 * mm(g, g, TN)
-    a = a_ref[0]
+    early = step < n // 2
+    a = jnp.where(early, ae_ref[0], al_ref[0])
     a_parts = split(a)
     b = 0.05 * p
     bh, bl = split(b)
@@ -181,7 +183,7 @@
     blk = BLOCK
     for i in range(width // blk):
         lo = i * blk
-        gram[step, lo : lo + blk, lo:] = m_ref[0, lo : lo + blk, lo:] + mm(y[:, lo : lo + blk], z[:, lo:], TN)
+        gram[step, lo : lo + blk, lo:] = jnp.where(early, me_ref[0, lo : lo + blk, lo:], ml_ref[0, lo : lo + blk, lo:]) + mm(y[:, lo : lo + blk], z[:, lo:], TN)
     xl = mm3(left, ql, NN)
     x_left[step] = xl
     gl = mm3(xl, xl, TN)
@@ -270,8 +272,11 @@
         lax.fori_loop(0, n, finish, 0, unroll=min(n, 2))
 
 
-def after(grad, weight, m1, m2, left, ql, stat, q, a, m):
+def after(grad, weight, m1, m2, left, ql, stat, q, early, late):
     n, rows, width = weight.shape
+    half = n // 2
+    first = pl.BlockSpec((1, width, width), lambda i: (jnp.minimum(i, half - 1), 0, 0))
+    second = pl.BlockSpec((1, width, width), lambda i: (jnp.maximum(i - half, 0), 0, 0))
     wide = pl.BlockSpec((1, width, width), lambda i: (i, 0, 0))
     flat = pl.BlockSpec((1, rows, width), lambda i: (i, 0, 0))
     small = pl.BlockSpec((1, rows, rows), lambda i: (i, 0, 0))
@@ -279,7 +284,7 @@
     return pl.pallas_call(
         after_kernel,
         grid=(n,),
-        in_specs=[flat, flat, flat, flat, small, small, wide, wide, wide, wide],
+        in_specs=[flat, flat, flat, flat, small, small, wide, wide, first, first, second, second],
         out_specs=[
             flat, flat, flat, small, wide,
             pl.BlockSpec((n, rows, rows), lambda i: (0, 0, 0)),
@@ -304,7 +309,7 @@
         compiler_params=pltpu.CompilerParams(vmem_limit_bytes=62 << 20),
         cost_estimate=pl.CostEstimate(flops=n * 12 * width**3, bytes_accessed=n * 24 * width * width, transcendentals=0),
         name="after",
-    )(grad, weight, m1, m2, left, ql, stat, q, a, m)
+    )(grad, weight, m1, m2, left, ql, stat, q, *early, *late)
 
 
 def swap_core(values):
@@ -368,6 +373,94 @@
         values = values + lax.ppermute(values, "dp", [(i, i ^ bit) for i in range(count)])
         bit *= 2
     return values
+
+
+def shift(values, axis, pairs):
+    return lax.ppermute(values, axis, pairs)
+
+
+def gather_owners(own, beside):
+    count = lax.axis_size("dp")
+    if count != 8:
+        return lax.all_gather(own, "dp", axis=0, tiled=True), [make() for make in beside]
+    across = [(i, i ^ 1) for i in range(8)]
+    z = lax.axis_index("dp") // 2
+    even = (z & 1) == 0
+    ups, downs, far = [own], [own], []
+    made = []
+    for s in range(4):
+        if s == 0:
+            pay = own
+        elif s == 1:
+            pay = jnp.where(even, downs[1], ups[1])
+        elif s == 2:
+            pay = jnp.where(z == 0, downs[2], jnp.where(z == 1, downs[1], jnp.where(z == 2, ups[1], ups[2])))
+        else:
+            pay = jnp.where(z == 0, downs[3], jnp.where(z == 1, downs[2], jnp.where(z == 2, ups[2], ups[3])))
+        moved = [shift(pay, "dp", across)]
+        if s < 3:
+            moved.append(shift(ups[s], "dp", [(i, i + 2) for i in range(2 * s, 6)]))
+            moved.append(shift(downs[s], "dp", [(i, i - 2) for i in range(2, 8 - 2 * s)]))
+        extra = [beside[s]()] if s < len(beside) else []
+        moved, extra = lax.optimization_barrier((moved, extra))
+        made.extend(extra)
+        far.append(moved[0])
+        if s < 3:
+            ups.append(moved[1])
+            downs.append(moved[2])
+    far_rel = [
+        far[0],
+        jnp.where(z == 0, far[3], jnp.where(z == 1, far[1], jnp.where(z == 2, far[2], far[1]))),
+        jnp.where(z == 0, far[2], jnp.where(z == 1, far[3], jnp.where(z == 2, far[3], far[2]))),
+        jnp.where(z == 0, far[1], jnp.where(z == 1, far[2], jnp.where(z == 2, far[1], far[3]))),
+    ]
+    parts = [own, far_rel[0]]
+    for s in range(1, 4):
+        parts.append(ups[s] + downs[4 - s])
+        parts.append(far_rel[s])
+    return jnp.concatenate(parts, axis=0), made
+
+
+def owner_place(owner):
+    if lax.axis_size("dp") != 8:
+        return owner
+    me = lax.axis_index("dp")
+    return ((me // 2 - owner // 2) % 4) * 2 + ((me ^ owner) & 1)
+
+
+def sum_to_owner(blocks, block_of, capacity):
+    if lax.axis_size("dp") != 8:
+        return lax.psum_scatter(blocks[block_of], "dp", scatter_dimension=0, tiled=True)
+    me = lax.axis_index("dp")
+    z = me // 2
+    order = jnp.array([[3, 2, 1, 0], [3, 2, 0, 1], [0, 1, 3, 2], [0, 1, 2, 3]], jnp.int32)[z]
+    table = block_of.reshape(8, capacity)
+    give = blocks[table[order * 2 + ((me & 1) ^ 1)].reshape(-1)].reshape((4, capacity) + blocks.shape[1:])
+    keep = blocks[table[order * 2 + (me & 1)].reshape(-1)].reshape((4, capacity) + blocks.shape[1:])
+    across = [(i, i ^ 1) for i in range(8)]
+    def swapped(k):
+        return shift(give[k], "dp", across)
+
+    def total(k, other):
+        return keep[k].astype(F32) + other.astype(F32)
+
+    def send(part, other, direction, step):
+        part = (part if other is None else part + other.astype(F32)).astype(BF)
+        if direction > 0:
+            return shift(part, "dp", [(i, i + 2) for i in range(2 * step)])
+        return shift(part, "dp", [(i, i - 2) for i in range(8 - 2 * step, 8)])
+
+    first = total(0, swapped(0))
+    moved = lax.optimization_barrier((swapped(1), send(first, None, 1, 1), send(first, None, -1, 1)))
+    second = total(1, moved[0])
+    up = send(jnp.where(z == 0, second, first), moved[1], 1, 2)
+    down = send(jnp.where(z == 3, second, first), moved[2], -1, 2)
+    moved = lax.optimization_barrier((swapped(2), up, down))
+    third = total(2, moved[0])
+    up = send(jnp.where(z == 1, second, third), moved[1], 1, 3)
+    down = send(jnp.where(z == 2, second, third), moved[2], -1, 3)
+    moved = lax.optimization_barrier((swapped(3), up, down))
+    return (total(3, moved[0]) + moved[1].astype(F32) + moved[2].astype(F32)).astype(BF)
 
 
 def project(rows, matrix):
@@ -499,10 +592,18 @@
     block_rows = master.shape[2]
     width = master.shape[3]
 
-    product, gram = before(stat_right[0], basis_right[0])
-    gathered = lax.all_gather(master[0].astype(BF), "dp", axis=0, tiled=True)
+    half = max(capacity // 2, 1)
+    gathered, made = gather_owners(
+        master[0].astype(BF),
+        [
+            lambda: (before(stat_right[0], basis_right[0], 0, half), gather_chips(source[0])),
+            lambda: (before(stat_right[0], basis_right[0], half, capacity - half), gather_chips(target[0])),
+            lambda: gather_chips(out_grad[0]),
+        ],
+    )
+    (early, src), (late, tgt), cot = made
     slot_of = slot_positions(owners[0], capacity)
-    blocks = gathered[slot_of]
+    blocks = gathered[owner_place(slot_of // capacity) * capacity + slot_of % capacity]
     other_blocks = swap_core(blocks)
     extents = [head_count] * 4 + [col_count] * 2 + [head_count] * 8 + [col_count] * 2
     matrices = []
@@ -528,10 +629,6 @@
     enc_allowed = jnp.broadcast_to(key_pos[None, :] < src_size, (total_rows, 2 * total_rows))
     dec_allowed = (key_pos[None, :] <= own_pos[:, None]) & (key_pos[None, :] < tgt_size)
     keep_rows = (own_pos < tgt_size).astype(F32)[:, None]
-
-    src = gather_chips(source[0])
-    tgt = gather_chips(target[0])
-    cot = gather_chips(out_grad[0])
 
     branch_one, saved_one = attention_forward(src, src, matrices[0:4], enc_allowed, block_rows)
     z_one = src.astype(F32) + sum_chips(branch_one)
@@ -584,7 +681,9 @@
         return (jnp.concatenate(mine, axis=0) + other.astype(F32)).astype(BF)
 
     block_grad = jnp.concatenate(
-        [reduce_core(item) for item in (weights_one, weights_two, weights_three, weights_four, weights_five)], axis=0
+        [reduce_core(item) for item in (weights_one, weights_two, weights_three, weights_four, weights_five)]
+        + [jnp.zeros((1, block_rows, width), BF)],
+        axis=0,
     )
     norm_local = jnp.stack(
         [
@@ -594,9 +693,8 @@
     )
     held = slot_of[None, :] == jnp.arange(slot_count, dtype=jnp.int32)[:, None]
     block_of = jnp.sum(jnp.where(held, jnp.arange(slot_of.shape[0], dtype=jnp.int32)[None, :], 0), axis=1)
-    used = jnp.any(held, axis=1)
-    in_slots = jnp.where(used[:, None, None], block_grad[block_of], 0)
-    own_grad = lax.psum_scatter(in_slots, "dp", scatter_dimension=0, tiled=True)
+    block_of = jnp.where(jnp.any(held, axis=1), block_of, slot_of.shape[0])
+    own_grad = sum_to_owner(block_grad, block_of, capacity)
     norm_grad = sum_everywhere(norm_local)
     results = after(
         own_grad,
@@ -607,8 +705,8 @@
         basis_left[0],
         stat_right[0],
         basis_right[0],
-        product,
-        gram,
+        early,
+        late,
     )
     norm_one_new = 0.9 * norm_one + 0.1 * norm_grad
     norm_two_new = 0.999 * norm_two + 0.001 * norm_grad * norm_grad

time: 530 us -> 487 us (0.919)
  waiting for transfers between devices: 205 us -> 80.7 us
  starting transfers between devices: 21.5 us -> 68.6 us
  other arithmetic: 61.2 us -> 92.1 us
  local copies, waits for them, and re-layouts: 52.2 us -> 69 us
  between operations: 18.8 us -> 5.2 us
    all_gather x1 -> x0, waiting for transfers between devices: 77.2 us -> none  [per_device(): gathered = lax.all_gather(master[0].astype(BF), 'dp', axis=0, tiled=True)]
    reduce_scatter x1 -> x0, waiting for transfers between devices: 42.8 us -> none  [per_device(): own_grad = lax.psum_scatter(in_slots, 'dp', scatter_dimension=0, tiled=True)]
    ppermute x0 -> x20, starting transfers between devices: none -> 41.5 us  [shift(): return lax.ppermute(values, axis, pairs)]
    ppermute x0 -> x20, waiting for transfers between devices: none -> 21.6 us  [shift(): return lax.ppermute(values, axis, pairs)]
    ppermute x14, waiting for transfers between devices: 77.8 us -> 58.1 us  [swap_chip(): return lax.ppermute(values, 'tensor', [(i, i ^ bit) for i in range(count)])]
    unnamed x7 -> x13, other arithmetic: 6.66 us -> 18.4 us
    pallas_call x1 -> x2, Pallas kernels: 17.1 us -> 19.2 us  [before(): pl.pallas_call(before_kernel, grid=(n,), in_specs=[take, take], out_specs...]
    gather x2 -> x5, local copies, waits for them, and re-layouts: 9.85 us -> 11.7 us  [the longest x1 4.87 us: per_device(): gathered[owner_place(slot_of // capacity) * capacity + slot_of % capacity]]
  transfers between devices with their start and end apart: 32 -> 50, of which waited for: 17 -> 19; matrix products, arithmetic and copies ran while one was open for 28% -> 32% of each run, Pallas kernels for 3% -> 4%
where the time goes in v3:
time: 487 us; the launch traced here: 481 us
  other arithmetic  92.1 us (19%)
  Pallas kernels  91.4 us (19%)
  waiting for transfers between devices  80.7 us (17%)
  matrix products  73.9 us (15%)
  local copies, waits for them, and re-layouts  69 us (14%)
  starting transfers between devices  68.6 us (14%)
  between operations  5.2 us (1%)
    pallas_call x1, Pallas kernels, after(): pl.pallas_call(after_kernel, grid=(n,), in_specs=[flat, flat, flat, flat,...  72.1 us
    ppermute x14, waiting for transfers between devices, swap_chip(): return lax.ppermute(values, 'tensor', [(i, i ^ bit) for i in range(count)])  58.1 us
    ppermute x20, starting transfers between devices, shift(): return lax.ppermute(values, axis, pairs)  41.5 us
    dot_general x45, matrix products, mm(): return lax.dot_general(a, b, dims, preferred_element_type=F32)  38 us
    unnamed x373, local copies, waits for them, and re-layouts  25.1 us
    ppermute x20, waiting for transfers between devices, shift(): return lax.ppermute(values, axis, pairs)  21.6 us
    ppermute x14, starting transfers between devices, swap_chip(): return lax.ppermute(values, 'tensor', [(i, i ^ bit) for i in range(count)])  19.9 us
    pallas_call x2, Pallas kernels, before(): pl.pallas_call(before_kernel, grid=(n,), in_specs=[take, take], out_specs...  19.2 us
  transfers between devices with their start and end apart: 50, of which 19 were waited for; matrix products, arithmetic and copies ran while one was open for 32% of the time, Pallas kernels for 4%

profile of v3, /device:TPU:0, one launch (start us, length us, event | category | flops | bytes accessed | tf_op | source)
XLA Modules:
  0.0 480.9 jit_solution(8767083061512700178)
XLA Ops:
  0.7 2.2 constant_dynamic-update-slice_fusion.1
  4.1 5.6 %collective-permute-start.1 = (bf16[8,64,512]{2,1,0:T(8,128)(2,1)S(1)}, bf16[8,64,512]{2,1,0:T(8,128)(2,1)S(1)}, u32[]{:S(2)}, u32[]{:S(2)}) collective-permute-start(bf16[8,64,512]{2,1,0:T(8,128)(2,1)S(1)} %get-tuple-element.175), channel_id=1, source_target_pairs={{0,8},{4,12},{8,16},{12,20},{16,24},{20,28},{1,9},{5,13},{9,17},{1... | collective-permute-start | bytes 1572872 | tf_op jit(solution)/shard_map/ppermute | solution.py:379
  14.2 9.6 %before.2 = (f32[4,512,512]{2,1,0:T(8,128)}, f32[4,512,512]{2,1,0:T(8,128)}) custom-call(f32[8,512,512]{2,1,0:T(8,128)} %bitcast.462, f32[8,512,512]{2,1,0:T(8,128)} %bitcast.465), custom_call_target="tpu_custom_call" | custom-call | flops 6442450944 | bytes 16777216 | tf_op jit(solution)/shard_map/before/pallas_call | solution.py:70
  29.1 9.6 %before.3 = (f32[4,512,512]{2,1,0:T(8,128)}, f32[4,512,512]{2,1,0:T(8,128)}) custom-call(f32[8,512,512]{2,1,0:T(8,128)} %bitcast.463, f32[8,512,512]{2,1,0:T(8,128)} %bitcast.466), custom_call_target="tpu_custom_call" | custom-call | flops 6442450944 | bytes 16777216 | tf_op jit(solution)/shard_map/before/pallas_call | solution.py:70
  48.0 4.9 %collective-permute-done.11 = bf16[256,512]{0,1:T(8,128)(2,1)S(1)} collective-permute-done((bf16[256,512]{0,1:T(8,128)(2,1)S(1)}, bf16[256,512]{0,1:T(8,128)(2,1)S(1)}, u32[]{:S(2)}, u32[]{:S(2)}) %collective-permute-start.11) | collective-permute-done | bytes 262176 | tf_op jit(solution)/shard_map/ppermute | solution.py:330
  55.7 2.6 collective-permute-done.10
  58.4 2.6 select_select_fusion.2
  61.7 9.4 %collective-permute-done.12 = bf16[8,64,512]{2,1,0:T(8,128)(2,1)S(1)} collective-permute-done((bf16[8,64,512]{2,1,0:T(8,128)(2,1)S(1)}, bf16[8,64,512]{2,1,0:T(8,128)(2,1)S(1)}, u32[]{:S(2)}, u32[]{:S(2)}) %collective-permute-start.12) | collective-permute-done | bytes 524320 | tf_op jit(solution)/shard_map/ppermute | solution.py:379
  71.1 2.1 fusion.73
  79.1 4.9 %gather_fusion = bf16[56,64,512]{2,1,0:T(8,128)(2,1)} fusion(bf16[64,64,512]{2,1,0:T(8,128)(2,1)} %select_dynamic-update-slice_fusion, s32[1024]{0:T(1024)S(1)} %pad_clamp_fusion.4), kind=kCustom, calls=%fused_computation | custom fusion | bytes 7340256 | tf_op jit(solution)/shard_map/gather | solution.py:606
  90.7 2.3 fusion.193
  94.0 2.3 fusion.194
  99.7 2.5 fusion.192
  111.7 2.3 copy.91
  115.4 2.2 fusion.1
  118.8 2.5 fusion.42
  128.5 2.5 fusion.46
  132.0 4.5 collective-permute-done.17
  137.5 7.0 %multiply_convert_fusion.4 = (bf16[512,1024]{1,0:T(8,128)(2,1)S(1)}, f32[512,1024]{1,0:T(8,128)}, f32[512,1024]{1,0:T(8,128)}) fusion(bf16[1024,512]{1,0:T(8,128)(2,1)S(1)} %bitcast.357, f32[512,512]{0,1:T(8,128)S(1)} %get-tuple-element.173, f32[512]{0:T(512)S(1)} %bitcast.441, f32[512]{0:T(512)S(1)} %bitcast.416, f32[512]{0:T(512)S(1)} %fusion.142, ...), kind=kOutput, calls=%fused_computation.69 | convolution fusion | flops 572260352 | bytes 7348224 | tf_op jit(solution)/shard_map/dot_general | solution.py:47
  147.9 10.5 %collective-permute-done.18 = bf16[512,512]{0,1:T(8,128)(2,1)S(1)} collective-permute-done((bf16[512,512]{0,1:T(8,128)(2,1)S(1)}, bf16[512,512]{0,1:T(8,128)(2,1)S(1)}, u32[]{:S(2)}, u32[]{:S(2)}) %collective-permute-start.18) | collective-permute-done | bytes 524320 | tf_op jit(solution)/shard_map/ppermute | solution.py:330
  165.1 2.2 copy.95
  172.2 2.7 fusion.41
  184.7 5.0 %collective-permute-done.20 = bf16[512,512]{0,1:T(8,128)(2,1)} collective-permute-done((bf16[512,512]{0,1:T(8,128)(2,1)S(1)}, bf16[512,512]{0,1:T(8,128)(2,1)}, u32[]{:S(2)}, u32[]{:S(2)}) %collective-permute-start.20) | collective-permute-done | bytes 524320 | tf_op jit(solution)/shard_map/ppermute | solution.py:330
  191.4 5.3 %multiply_convert_fusion.3 = (bf16[512,1024]{1,0:T(8,128)(2,1)S(1)}, f32[512,1024]{1,0:T(8,128)S(1)}, f32[512,1024]{1,0:T(8,128)S(1)}) fusion(bf16[1024,512]{1,0:T(8,128)(2,1)S(1)} %bitcast.359, f32[512,512]{0,1:T(8,128)S(1)} %get-tuple-element.165, f32[512]{0:T(512)S(1)} %bitcast.444, f32[512]{0:T(512)S(1)} %bitcast.434, f32[512]{0:T(512)S(1)} %fusion.144, ...), kind=kOutput, calls=%fused_computation.56 | convolution fusion | flops 572260352 | bytes 7348224 | tf_op jit(solution)/shard_map/dot_general | solution.py:47
  200.4 10.3 %collective-permute-done.21 = bf16[512,512]{0,1:T(8,128)(2,1)S(1)} collective-permute-done((bf16[512,512]{0,1:T(8,128)(2,1)S(1)}, bf16[512,512]{0,1:T(8,128)(2,1)S(1)}, u32[]{:S(2)}, u32[]{:S(2)}) %collective-permute-start.21) | collective-permute-done | bytes 524320 | tf_op jit(solution)/shard_map/ppermute | solution.py:330
  224.4 2.4 pad_maximum_fusion.8
  226.9 2.7 collective-permute-done.22
  229.5 2.8 multiply_reduce_fusion.4
  233.6 5.0 %fusion.10 = f32[4,64,1024]{2,1,0:T(8,128)S(1)} fusion(bf16[512,4,64]{0,2,1:T(8,128)(2,1)S(1)} %bitcast.352, f32[4,512]{1,0:T(4,128)S(1)} %copy-done.116, f32[4,512,1024]{2,1,0:T(8,128)} %copy-done.2, pred[1024]{0:T(1024)(128)(4,1)S(1)} %copy-done.112), kind=kOutput, calls=%fused_computation.31 | convolution fusion | flops 276824064 | bytes 9708544 | tf_op jit(solution)/shard_map/hqk,qhe->khe/dot_general | solution.py:519
  238.6 2.7 multiply_reduce_fusion.2
  241.3 2.2 multiply_convert_fusion.2
  253.0 10.7 %collective-permute-done.28 = bf16[512,512]{0,1:T(8,128)(2,1)S(1)} collective-permute-done((bf16[512,512]{0,1:T(8,128)(2,1)S(1)}, bf16[512,512]{0,1:T(8,128)(2,1)S(1)}, u32[]{:S(2)}, u32[]{:S(2)}) %collective-permute-start.28) | collective-permute-done | bytes 524320 | tf_op jit(solution)/shard_map/ppermute | solution.py:330
  268.2 2.6 multiply_reduce_fusion
  280.7 4.1 collective-permute-done.24
  299.2 3.9 collective-permute-done.25
  307.9 3.1 multiply_reduce_fusion.1
  311.4 2.2 multiply_convert_fusion.1
  328.5 2.7 fusion.48
  334.5 2.6 fusion.47
  337.7 2.9 gather_fusion.4
  344.1 3.5 collective-permute-start.48
  351.1 2.9 gather_fusion.2
  358.3 6.5 %collective-permute-start.39 = (bf16[8,64,512]{2,1,0:T(8,128)(2,1)S(1)}, bf16[8,64,512]{2,1,0:T(8,128)(2,1)S(1)}, u32[]{:S(2)}, u32[]{:S(2)}) collective-permute-start(bf16[8,64,512]{2,1,0:T(8,128)(2,1)S(1)} %fusion.66), channel_id=1, source_target_pairs={{0,8},{4,12},{1,9},{5,13},{2,10},{6,14},{3,11},{7,15}} | collective-permute-start | bytes 1572872 | tf_op jit(solution)/shard_map/ppermute | solution.py:379
  368.7 4.9 %collective-permute-done.39 = bf16[8,64,512]{2,1,0:T(8,128)(2,1)S(1)} collective-permute-done((bf16[8,64,512]{2,1,0:T(8,128)(2,1)S(1)}, bf16[8,64,512]{2,1,0:T(8,128)(2,1)S(1)}, u32[]{:S(2)}, u32[]{:S(2)}) %collective-permute-start.39) | collective-permute-done | bytes 524320 | tf_op jit(solution)/shard_map/ppermute | solution.py:379
  375.8 5.0 %collective-permute-start.42 = (bf16[8,64,512]{2,1,0:T(8,128)(2,1)S(1)}, bf16[8,64,512]{2,1,0:T(8,128)(2,1)S(1)}, u32[]{:S(2)}, u32[]{:S(2)}) collective-permute-start(bf16[8,64,512]{2,1,0:T(8,128)(2,1)S(1)} %get-tuple-element.211), channel_id=1, source_target_pairs={{0,8},{4,12},{8,16},{12,20},{1,9},{5,13},{9,17},{13,21},{2,10},{6,... | collective-permute-start | bytes 1572872 | tf_op jit(solution)/shard_map/ppermute | solution.py:379
  391.7 6.1 %collective-permute-start.44 = (bf16[8,64,512]{2,1,0:T(8,128)(2,1)}, bf16[8,64,512]{2,1,0:T(8,128)(2,1)}, u32[]{:S(2)}, u32[]{:S(2)}) collective-permute-start(bf16[8,64,512]{2,1,0:T(8,128)(2,1)} %get-tuple-element.209), channel_id=1, source_target_pairs={{0,8},{4,12},{8,16},{12,20},{16,24},{20,28},{1,9},{5,13},{9,17},{1... | collective-permute-start | bytes 1572872 | tf_op jit(solution)/shard_map/ppermute | solution.py:379
  406.2 2.4 add_convert_fusion.2.g_ref
  408.6 72.1 %after.1 = (f32[8,64,512]{2,1,0:T(8,128)}, f32[8,64,512]{2,1,0:T(8,128)}, f32[8,64,512]{2,1,0:T(8,128)}, f32[8,64,64]{2,1,0:T(8,128)}, f32[8,512,512]{2,1,0:T(8,...) custom-call(bf16[8,64,512]{2,1,0:T(8,128)(2,1)} %add_convert_fusion.2.g_ref, ...), custom_call_target="tpu_custom_call" | custom-call | flops 12884901888 | bytes 50331648 | tf_op jit(solution)/shard_map/after/pallas_call | solution.py:284
  (697 shorter events, 202.8 us)
Async XLA Ops:
  2.9 22.1 %collective-permute-start.2 = (bf16[8,64,512]{2,1,0:T(8,128)(2,1)S(1)}, bf16[8,64,512]{2,1,0:T(8,128)(2,1)S(1)}, u32[]{:S(2)}, u32[]{:S(2)}) collective-permute-start(bf16[8,64,512]{2,1,0:T(8,128)(2,1)S(1)} %get-tuple-element.175), channel_id=1, source_target_pairs={{8,0},{12,4},{16,8},{20,12},{24,16},{28,20},{9,1},{13,5},{17,9},{2... | collective-permute-start | bytes 1572872 | tf_op jit(solution)/shard_map/ppermute | solution.py:379
  4.1 20.8 %collective-permute-start.1 = (bf16[8,64,512]{2,1,0:T(8,128)(2,1)S(1)}, bf16[8,64,512]{2,1,0:T(8,128)(2,1)S(1)}, u32[]{:S(2)}, u32[]{:S(2)}) collective-permute-start(bf16[8,64,512]{2,1,0:T(8,128)(2,1)S(1)} %get-tuple-element.175), channel_id=1, source_target_pairs={{0,8},{4,12},{8,16},{12,20},{16,24},{20,28},{1,9},{5,13},{9,17},{1... | collective-permute-start | bytes 1572872 | tf_op jit(solution)/shard_map/ppermute | solution.py:379
  9.7 15.2 %collective-permute-start = (bf16[8,64,512]{2,1,0:T(8,128)(2,1)S(1)}, bf16[8,64,512]{2,1,0:T(8,128)(2,1)S(1)}, u32[]{:S(2)}, u32[]{:S(2)}) collective-permute-start(bf16[8,64,512]{2,1,0:T(8,128)(2,1)S(1)} %get-tuple-element.175), channel_id=1, source_target_pairs={{0,4},{4,0},{8,12},{12,8},{16,20},{20,16},{24,28},{28,24},{1,5},{5... | collective-permute-start | bytes 1572872 | tf_op jit(solution)/shard_map/ppermute | solution.py:379
  11.9 26.8 %collective-permute-start.7 = (bf16[256,512]{0,1:T(8,128)(2,1)S(1)}, bf16[256,512]{0,1:T(8,128)(2,1)}, u32[]{:S(2)}, u32[]{:S(2)}) collective-permute-start(bf16[256,512]{0,1:T(8,128)(2,1)S(1)} %bitcast.371), channel_id=1, source_target_pairs={{0,2},{1,3},{2,0},{3,1},{4,6},{5,7},{6,4},{7,5},{8,10},{9,11},{10,... | collective-permute-start | bytes 786440 | tf_op jit(solution)/shard_map/ppermute | solution.py:330
  13.6 11.2 %collective-permute-start.3 = (bf16[256,512]{0,1:T(8,128)(2,1)S(1)}, bf16[256,512]{0,1:T(8,128)(2,1)S(1)}, u32[]{:S(2)}, u32[]{:S(2)}) collective-permute-start(bf16[256,512]{0,1:T(8,128)(2,1)S(1)} %bitcast.373), channel_id=1, source_target_pairs={{0,2},{1,3},{2,0},{3,1},{4,6},{5,7},{6,4},{7,5},{8,10},{9,11},{10,... | collective-permute-start | bytes 786440 | tf_op jit(solution)/shard_map/ppermute | solution.py:330
  25.9 15.1 %collective-permute-start.6 = (bf16[8,64,512]{2,1,0:T(8,128)(2,1)S(1)}, bf16[8,64,512]{2,1,0:T(8,128)(2,1)S(1)}, u32[]{:S(2)}, u32[]{:S(2)}) collective-permute-start(bf16[8,64,512]{2,1,0:T(8,128)(2,1)S(1)} %collective-permute-done.2), channel_id=1, source_target_pairs={{8,0},{12,4},{16,8},{20,12},{9,1},{13,5},{17,9},{21,13},{10,2},{14... | collective-permute-start | bytes 1572872 | tf_op jit(solution)/shard_map/ppermute | solution.py:379
  27.2 13.8 %collective-permute-start.5 = (bf16[8,64,512]{2,1,0:T(8,128)(2,1)S(1)}, bf16[8,64,512]{2,1,0:T(8,128)(2,1)S(1)}, u32[]{:S(2)}, u32[]{:S(2)}) collective-permute-start(bf16[8,64,512]{2,1,0:T(8,128)(2,1)S(1)} %collective-permute-done.1), channel_id=1, source_target_pairs={{8,16},{12,20},{16,24},{20,28},{9,17},{13,21},{17,25},{21,29},{10,... | collective-permute-start | bytes 1572872 | tf_op jit(solution)/shard_map/ppermute | solution.py:379
  28.7 12.2 %collective-permute-start.4 = (bf16[8,64,512]{2,1,0:T(8,128)(2,1)}, bf16[8,64,512]{2,1,0:T(8,128)(2,1)}, u32[]{:S(2)}, u32[]{:S(2)}) collective-permute-start(bf16[8,64,512]{2,1,0:T(8,128)(2,1)} %broadcast_select_fusion), channel_id=1, source_target_pairs={{0,4},{4,0},{8,12},{12,8},{16,20},{20,16},{24,28},{28,24},{1,5},{5... | collective-permute-start | bytes 1572872 | tf_op jit(solution)/shard_map/ppermute | solution.py:379
  41.8 13.9 %collective-permute-start.8 = (bf16[8,64,512]{2,1,0:T(8,128)(2,1)}, bf16[8,64,512]{2,1,0:T(8,128)(2,1)S(1)}, u32[]{:S(2)}, u32[]{:S(2)}) collective-permute-start(bf16[8,64,512]{2,1,0:T(8,128)(2,1)} %select_select_fusion.3), channel_id=1, source_target_pairs={{0,4},{4,0},{8,12},{12,8},{16,20},{20,16},{24,28},{28,24},{1,5},{5... | collective-permute-start | bytes 1572872 | tf_op jit(solution)/shard_map/ppermute | solution.py:379
  42.5 15.9 %collective-permute-start.10 = (bf16[8,64,512]{2,1,0:T(8,128)(2,1)S(1)}, bf16[8,64,512]{2,1,0:T(8,128)(2,1)}, u32[]{:S(2)}, u32[]{:S(2)}) collective-permute-start(bf16[8,64,512]{2,1,0:T(8,128)(2,1)S(1)} %collective-permute-done.6), channel_id=1, source_target_pairs={{8,0},{12,4},{9,1},{13,5},{10,2},{14,6},{11,3},{15,7}} | collective-permute-start | bytes 1572872 | tf_op jit(solution)/shard_map/ppermute | solution.py:379
  43.8 14.6 %collective-permute-start.9 = (bf16[8,64,512]{2,1,0:T(8,128)(2,1)S(1)}, bf16[8,64,512]{2,1,0:T(8,128)(2,1)}, u32[]{:S(2)}, u32[]{:S(2)}) collective-permute-start(bf16[8,64,512]{2,1,0:T(8,128)(2,1)S(1)} %collective-permute-done.5), channel_id=1, source_target_pairs={{16,24},{20,28},{17,25},{21,29},{18,26},{22,30},{19,27},{23,31}} | collective-permute-start | bytes 1572872 | tf_op jit(solution)/shard_map/ppermute | solution.py:379
  46.5 6.4 %collective-permute-start.11 = (bf16[256,512]{0,1:T(8,128)(2,1)S(1)}, bf16[256,512]{0,1:T(8,128)(2,1)S(1)}, u32[]{:S(2)}, u32[]{:S(2)}) collective-permute-start(bf16[256,512]{0,1:T(8,128)(2,1)S(1)} %bitcast.376), channel_id=1, source_target_pairs={{0,2},{1,3},{2,0},{3,1},{4,6},{5,7},{6,4},{7,5},{8,10},{9,11},{10,... | collective-permute-start | bytes 786440 | tf_op jit(solution)/shard_map/ppermute | solution.py:330
  61.0 10.1 %collective-permute-start.12 = (bf16[8,64,512]{2,1,0:T(8,128)(2,1)S(1)}, bf16[8,64,512]{2,1,0:T(8,128)(2,1)S(1)}, u32[]{:S(2)}, u32[]{:S(2)}) collective-permute-start(bf16[8,64,512]{2,1,0:T(8,128)(2,1)S(1)} %get-tuple-element.246), channel_id=1, source_target_pairs={{0,4},{4,0},{8,12},{12,8},{16,20},{20,16},{24,28},{28,24},{1,5},{5... | collective-permute-start | bytes 1572872 | tf_op jit(solution)/shard_map/ppermute | solution.py:379
  84.0 10.0 %collective-permute-start.13 = (bf16[56,64,512]{2,1,0:T(8,128)(2,1)}, bf16[56,64,512]{2,1,0:T(8,128)(2,1)}, u32[]{:S(2)}, u32[]{:S(2)}) collective-permute-start(bf16[56,64,512]{2,1,0:T(8,128)(2,1)} %gather_fusion), channel_id=1, source_target_pairs={{0,1},{1,0},{2,3},{3,2},{4,5},{5,4},{6,7},{7,6},{8,9},{9,8},{10,11... | collective-permute-start | bytes 11010056 | tf_op jit(solution)/shard_map/ppermute | solution.py:317
  96.8 9.4 %collective-permute-start.16 = (bf16[512,512]{1,0:T(8,128)(2,1)S(1)}, bf16[512,512]{1,0:T(8,128)(2,1)S(1)}, u32[]{:S(2)}, u32[]{:S(2)}) collective-permute-start(bf16[512,512]{1,0:T(8,128)(2,1)S(1)} %convolution_convert_fusion.1), channel_id=1, source_target_pairs={{0,1},{1,0},{2,3},{3,2},{4,5},{5,4},{6,7},{7,6},{8,9},{9,8},{10,11... | collective-permute-start | bytes 1572872 | tf_op jit(solution)/shard_map/ppermute | solution.py:317
  98.7 8.2 %collective-permute-start.14 = (bf16[512,512]{1,0:T(8,128)(2,1)}, bf16[512,512]{1,0:T(8,128)(2,1)}, u32[]{:S(2)}, u32[]{:S(2)}) collective-permute-start(bf16[512,512]{1,0:T(8,128)(2,1)} %convolution_convert_fusion.2), channel_id=1, source_target_pairs={{0,1},{1,0},{2,3},{3,2},{4,5},{5,4},{6,7},{7,6},{8,9},{9,8},{10,11... | collective-permute-start | bytes 1572872 | tf_op jit(solution)/shard_map/ppermute | solution.py:317
  121.7 14.8 %collective-permute-start.17 = (bf16[512,512]{0,1:T(8,128)(2,1)S(1)}, bf16[512,512]{0,1:T(8,128)(2,1)S(1)}, u32[]{:S(2)}, u32[]{:S(2)}) collective-permute-start(bf16[512,512]{0,1:T(8,128)(2,1)S(1)} %fusion.38), channel_id=1, source_target_pairs={{0,2},{1,3},{2,0},{3,1},{4,6},{5,7},{6,4},{7,5},{8,10},{9,11},{10,... | collective-permute-start | bytes 1572872 | tf_op jit(solution)/shard_map/ppermute | solution.py:330
  131.5 16.0 %collective-permute-start.15 = (bf16[512,512]{0,1:T(8,128)(2,1)S(1)}, bf16[512,512]{0,1:T(8,128)(2,1)S(1)}, u32[]{:S(2)}, u32[]{:S(2)}) collective-permute-start(bf16[512,512]{0,1:T(8,128)(2,1)S(1)} %fusion.37), channel_id=1, source_target_pairs={{0,2},{1,3},{2,0},{3,1},{4,6},{5,7},{6,4},{7,5},{8,10},{9,11},{10,... | collective-permute-start | bytes 1572872 | tf_op jit(solution)/shard_map/ppermute | solution.py:330
  145.2 13.2 %collective-permute-start.18 = (bf16[512,512]{0,1:T(8,128)(2,1)S(1)}, bf16[512,512]{0,1:T(8,128)(2,1)S(1)}, u32[]{:S(2)}, u32[]{:S(2)}) collective-permute-start(bf16[512,512]{0,1:T(8,128)(2,1)S(1)} %convolution_convert_fusion.6), channel_id=1, source_target_pairs={{0,2},{1,3},{2,0},{3,1},{4,6},{5,7},{6,4},{7,5},{8,10},{9,11},{10,... | collective-permute-start | bytes 1572872 | tf_op jit(solution)/shard_map/ppermute | solution.py:330
  175.5 14.1 %collective-permute-start.20 = (bf16[512,512]{0,1:T(8,128)(2,1)S(1)}, bf16[512,512]{0,1:T(8,128)(2,1)}, u32[]{:S(2)}, u32[]{:S(2)}) collective-permute-start(bf16[512,512]{0,1:T(8,128)(2,1)S(1)} %fusion.39), channel_id=1, source_target_pairs={{0,2},{1,3},{2,0},{3,1},{4,6},{5,7},{6,4},{7,5},{8,10},{9,11},{10,... | collective-permute-start | bytes 1572872 | tf_op jit(solution)/shard_map/ppermute | solution.py:330
  197.6 13.2 %collective-permute-start.21 = (bf16[512,512]{0,1:T(8,128)(2,1)S(1)}, bf16[512,512]{0,1:T(8,128)(2,1)S(1)}, u32[]{:S(2)}, u32[]{:S(2)}) collective-permute-start(bf16[512,512]{0,1:T(8,128)(2,1)S(1)} %convolution_convert_fusion.5), channel_id=1, source_target_pairs={{0,2},{1,3},{2,0},{3,1},{4,6},{5,7},{6,4},{7,5},{8,10},{9,11},{10,... | collective-permute-start | bytes 1572872 | tf_op jit(solution)/shard_map/ppermute | solution.py:330
  217.0 12.5 %collective-permute-start.22 = (bf16[512,512]{0,1:T(8,128)(2,1)}, bf16[512,512]{0,1:T(8,128)(2,1)}, u32[]{:S(2)}, u32[]{:S(2)}) collective-permute-start(bf16[512,512]{0,1:T(8,128)(2,1)} %convolution_convert_fusion.4), channel_id=1, source_target_pairs={{0,2},{1,3},{2,0},{3,1},{4,6},{5,7},{6,4},{7,5},{8,10},{9,11},{10,... | collective-permute-start | bytes 1572872 | tf_op jit(solution)/shard_map/ppermute | solution.py:330
  226.8 107.7 %collective-permute-start.35 = (bf16[16,64,512]{2,1,0:T(8,128)(2,1)}, bf16[16,64,512]{2,1,0:T(8,128)(2,1)}, u32[]{:S(2)}, u32[]{:S(2)}) collective-permute-start(bf16[16,64,512]{2,1,0:T(8,128)(2,1)} %pad_maximum_fusion.8), channel_id=1, source_target_pairs={{0,1},{1,0},{2,3},{3,2},{4,5},{5,4},{6,7},{7,6},{8,9},{9,8},{10,11... | collective-permute-start | bytes 3145736 | tf_op jit(solution)/shard_map/ppermute | solution.py:317
  245.9 5.7 %collective-permute-start.23 = (bf16[512,512]{0,1:T(8,128)(2,1)S(1)}, bf16[512,512]{0,1:T(8,128)(2,1)S(1)}, u32[]{:S(2)}, u32[]{:S(2)}) collective-permute-start(bf16[512,512]{0,1:T(8,128)(2,1)S(1)} %fusion.60), channel_id=1, source_target_pairs={{0,1},{1,0},{2,3},{3,2},{4,5},{5,4},{6,7},{7,6},{8,9},{9,8},{10,11... | collective-permute-start | bytes 1572872 | tf_op jit(solution)/shard_map/ppermute | solution.py:317
  250.0 13.6 %collective-permute-start.28 = (bf16[512,512]{0,1:T(8,128)(2,1)S(1)}, bf16[512,512]{0,1:T(8,128)(2,1)S(1)}, u32[]{:S(2)}, u32[]{:S(2)}) collective-permute-start(bf16[512,512]{0,1:T(8,128)(2,1)S(1)} %fusion.40), channel_id=1, source_target_pairs={{0,2},{1,3},{2,0},{3,1},{4,6},{5,7},{6,4},{7,5},{8,10},{9,11},{10,... | collective-permute-start | bytes 1572872 | tf_op jit(solution)/shard_map/ppermute | solution.py:330
  272.1 12.7 %collective-permute-start.24 = (bf16[512,512]{0,1:T(8,128)(2,1)S(1)}, bf16[512,512]{0,1:T(8,128)(2,1)S(1)}, u32[]{:S(2)}, u32[]{:S(2)}) collective-permute-start(bf16[512,512]{0,1:T(8,128)(2,1)S(1)} %fusion.36), channel_id=1, source_target_pairs={{0,2},{1,3},{2,0},{3,1},{4,6},{5,7},{6,4},{7,5},{8,10},{9,11},{10,... | collective-permute-start | bytes 1572872 | tf_op jit(solution)/shard_map/ppermute | solution.py:330
  279.1 53.1 %collective-permute-start.34 = (bf16[8,64,512]{2,1,0:T(8,128)(2,1)}, bf16[8,64,512]{2,1,0:T(8,128)(2,1)}, u32[]{:S(2)}, u32[]{:S(2)}) collective-permute-start(bf16[8,64,512]{2,1,0:T(8,128)(2,1)} %pad_maximum_fusion.11), channel_id=1, source_target_pairs={{0,1},{1,0},{2,3},{3,2},{4,5},{5,4},{6,7},{7,6},{8,9},{9,8},{10,11... | collective-permute-start | bytes 1572872 | tf_op jit(solution)/shard_map/ppermute | solution.py:317
  280.1 16.2 %collective-permute-start.29 = (bf16[512,512]{0,1:T(8,128)(2,1)S(1)}, bf16[512,512]{0,1:T(8,128)(2,1)S(1)}, u32[]{:S(2)}, u32[]{:S(2)}) collective-permute-start(bf16[512,512]{0,1:T(8,128)(2,1)S(1)} %fusion.58), channel_id=1, source_target_pairs={{0,1},{1,0},{2,3},{3,2},{4,5},{5,4},{6,7},{7,6},{8,9},{9,8},{10,11... | collective-permute-start | bytes 1572872 | tf_op jit(solution)/shard_map/ppermute | solution.py:317
  291.4 11.8 %collective-permute-start.25 = (bf16[512,512]{0,1:T(8,128)(2,1)S(1)}, bf16[512,512]{0,1:T(8,128)(2,1)S(1)}, u32[]{:S(2)}, u32[]{:S(2)}) collective-permute-start(bf16[512,512]{0,1:T(8,128)(2,1)S(1)} %convolution_convert_fusion.3), channel_id=1, source_target_pairs={{0,2},{1,3},{2,0},{3,1},{4,6},{5,7},{6,4},{7,5},{8,10},{9,11},{10,... | collective-permute-start | bytes 1572872 | tf_op jit(solution)/shard_map/ppermute | solution.py:330
  296.3 32.2 %collective-permute-start.32 = (bf16[16,64,512]{2,1,0:T(8,128)(2,1)}, bf16[16,64,512]{2,1,0:T(8,128)(2,1)}, u32[]{:S(2)}, u32[]{:S(2)}) collective-permute-start(bf16[16,64,512]{2,1,0:T(8,128)(2,1)} %pad_maximum_fusion.7), channel_id=1, source_target_pairs={{0,1},{1,0},{2,3},{3,2},{4,5},{5,4},{6,7},{7,6},{8,9},{9,8},{10,11... | collective-permute-start | bytes 3145736 | tf_op jit(solution)/shard_map/ppermute | solution.py:317
  314.6 2.7 collective-permute-start.26
  319.1 6.9 %collective-permute-start.31 = (bf16[8,64,512]{2,1,0:T(8,128)(2,1)}, bf16[8,64,512]{2,1,0:T(8,128)(2,1)}, u32[]{:S(2)}, u32[]{:S(2)}) collective-permute-start(bf16[8,64,512]{2,1,0:T(8,128)(2,1)} %pad_maximum_fusion.9), channel_id=1, source_target_pairs={{0,1},{1,0},{2,3},{3,2},{4,5},{5,4},{6,7},{7,6},{8,9},{9,8},{10,11... | collective-permute-start | bytes 1572872 | tf_op jit(solution)/shard_map/ppermute | solution.py:317
  325.4 5.8 %collective-permute-start.33 = (bf16[8,64,512]{2,1,0:T(8,128)(2,1)S(1)}, bf16[8,64,512]{2,1,0:T(8,128)(2,1)S(1)}, u32[]{:S(2)}, u32[]{:S(2)}) collective-permute-start(bf16[8,64,512]{2,1,0:T(8,128)(2,1)S(1)} %pad_maximum_fusion.10), channel_id=1, source_target_pairs={{0,1},{1,0},{2,3},{3,2},{4,5},{5,4},{6,7},{7,6},{8,9},{9,8},{10,11... | collective-permute-start | bytes 1572872 | tf_op jit(solution)/shard_map/ppermute | solution.py:317
  326.0 18.0 %collective-permute-start.47 = (f32[2,5,512]{2,1,0:T(8,128)S(1)}, f32[2,5,512]{2,1,0:T(8,128)S(1)}, u32[]{:S(2)}, u32[]{:S(2)}) collective-permute-start(f32[2,5,512]{2,1,0:T(8,128)S(1)} %fusion.168), channel_id=1, source_target_pairs={{0,4},{4,0},{8,12},{12,8},{16,20},{20,16},{24,28},{28,24},{1,5},{5... | collective-permute-start | bytes 61448 | tf_op jit(solution)/shard_map/ppermute | solution.py:373
  342.0 14.3 %collective-permute-start.38 = (bf16[8,64,512]{2,1,0:T(8,128)(2,1)}, bf16[8,64,512]{2,1,0:T(8,128)(2,1)}, u32[]{:S(2)}, u32[]{:S(2)}) collective-permute-start(bf16[8,64,512]{2,1,0:T(8,128)(2,1)} %get-tuple-element.212), channel_id=1, source_target_pairs={{0,4},{4,0},{8,12},{12,8},{16,20},{20,16},{24,28},{28,24},{1,5},{5... | collective-permute-start | bytes 1572872 | tf_op jit(solution)/shard_map/ppermute | solution.py:379
  344.1 5.8 %collective-permute-start.48 = (f32[2,5,512]{2,1,0:T(8,128)S(1)}, f32[2,5,512]{2,1,0:T(8,128)S(1)}, u32[]{:S(2)}, u32[]{:S(2)}) collective-permute-start(f32[2,5,512]{2,1,0:T(8,128)S(1)} %fusion.289), channel_id=1, source_target_pairs={{0,8},{4,12},{8,0},{12,4},{16,24},{20,28},{24,16},{28,20},{1,9},{5... | collective-permute-start | bytes 61448 | tf_op jit(solution)/shard_map/ppermute | solution.py:373
  348.4 43.3 %collective-permute-start.30 = (bf16[256,512]{0,1:T(8,128)(2,1)}, bf16[256,512]{0,1:T(8,128)(2,1)}, u32[]{:S(2)}, u32[]{:S(2)}) collective-permute-start(bf16[256,512]{0,1:T(8,128)(2,1)} %select_convert_fusion), channel_id=1, source_target_pairs={{0,2},{1,3},{2,0},{3,1},{4,6},{5,7},{6,4},{7,5},{8,10},{9,11},{10,... | collective-permute-start | bytes 786440 | tf_op jit(solution)/shard_map/ppermute | solution.py:330
  349.9 51.8 %collective-permute-start.49 = (f32[2,5,512]{2,1,0:T(8,128)S(1)}, f32[2,5,512]{2,1,0:T(8,128)S(1)}, u32[]{:S(2)}, u32[]{:S(2)}) collective-permute-start(f32[2,5,512]{2,1,0:T(8,128)S(1)} %add.632), channel_id=1, source_target_pairs={{0,16},{4,20},{8,24},{12,28},{16,0},{20,4},{24,8},{28,12},{1,17},{... | collective-permute-start | bytes 61448 | tf_op jit(solution)/shard_map/ppermute | solution.py:373
  354.0 12.9 %collective-permute-start.37 = (bf16[8,64,512]{2,1,0:T(8,128)(2,1)}, bf16[8,64,512]{2,1,0:T(8,128)(2,1)S(1)}, u32[]{:S(2)}, u32[]{:S(2)}) collective-permute-start(bf16[8,64,512]{2,1,0:T(8,128)(2,1)} %get-tuple-element.213), channel_id=1, source_target_pairs={{0,4},{4,0},{8,12},{12,8},{16,20},{20,16},{24,28},{28,24},{1,5},{5... | collective-permute-start | bytes 1572872 | tf_op jit(solution)/shard_map/ppermute | solution.py:379
  357.4 11.3 %collective-permute-start.40 = (bf16[8,64,512]{2,1,0:T(8,128)(2,1)S(1)}, bf16[8,64,512]{2,1,0:T(8,128)(2,1)S(1)}, u32[]{:S(2)}, u32[]{:S(2)}) collective-permute-start(bf16[8,64,512]{2,1,0:T(8,128)(2,1)S(1)} %fusion.66), channel_id=1, source_target_pairs={{24,16},{28,20},{25,17},{29,21},{26,18},{30,22},{27,19},{31,23}} | collective-permute-start | bytes 1572872 | tf_op jit(solution)/shard_map/ppermute | solution.py:379
  358.3 15.3 %collective-permute-start.39 = (bf16[8,64,512]{2,1,0:T(8,128)(2,1)S(1)}, bf16[8,64,512]{2,1,0:T(8,128)(2,1)S(1)}, u32[]{:S(2)}, u32[]{:S(2)}) collective-permute-start(bf16[8,64,512]{2,1,0:T(8,128)(2,1)S(1)} %fusion.66), channel_id=1, source_target_pairs={{0,8},{4,12},{1,9},{5,13},{2,10},{6,14},{3,11},{7,15}} | collective-permute-start | bytes 1572872 | tf_op jit(solution)/shard_map/ppermute | solution.py:379
  367.0 17.2 %collective-permute-start.41 = (bf16[8,64,512]{2,1,0:T(8,128)(2,1)S(1)}, bf16[8,64,512]{2,1,0:T(8,128)(2,1)S(1)}, u32[]{:S(2)}, u32[]{:S(2)}) collective-permute-start(bf16[8,64,512]{2,1,0:T(8,128)(2,1)S(1)} %copy-done.105), channel_id=1, source_target_pairs={{0,4},{4,0},{8,12},{12,8},{16,20},{20,16},{24,28},{28,24},{1,5},{5... | collective-permute-start | bytes 1572872 | tf_op jit(solution)/shard_map/ppermute | solution.py:379
  375.1 10.5 %collective-permute-start.43 = (bf16[8,64,512]{2,1,0:T(8,128)(2,1)S(1)}, bf16[8,64,512]{2,1,0:T(8,128)(2,1)S(1)}, u32[]{:S(2)}, u32[]{:S(2)}) collective-permute-start(bf16[8,64,512]{2,1,0:T(8,128)(2,1)S(1)} %get-tuple-element.210), channel_id=1, source_target_pairs={{16,8},{20,12},{24,16},{28,20},{17,9},{21,13},{25,17},{29,21},{18,... | collective-permute-start | bytes 1572872 | tf_op jit(solution)/shard_map/ppermute | solution.py:379
  375.8 13.0 %collective-permute-start.42 = (bf16[8,64,512]{2,1,0:T(8,128)(2,1)S(1)}, bf16[8,64,512]{2,1,0:T(8,128)(2,1)S(1)}, u32[]{:S(2)}, u32[]{:S(2)}) collective-permute-start(bf16[8,64,512]{2,1,0:T(8,128)(2,1)S(1)} %get-tuple-element.211), channel_id=1, source_target_pairs={{0,8},{4,12},{8,16},{12,20},{1,9},{5,13},{9,17},{13,21},{2,10},{6,... | collective-permute-start | bytes 1572872 | tf_op jit(solution)/shard_map/ppermute | solution.py:379
  384.2 19.5 %collective-permute-start.27 = (bf16[256,512]{0,1:T(8,128)(2,1)}, bf16[256,512]{0,1:T(8,128)(2,1)S(1)}, u32[]{:S(2)}, u32[]{:S(2)}) collective-permute-start(bf16[256,512]{0,1:T(8,128)(2,1)} %select_convert_fusion.1), channel_id=1, source_target_pairs={{0,2},{1,3},{2,0},{3,1},{4,6},{5,7},{6,4},{7,5},{8,10},{9,11},{10,... | collective-permute-start | bytes 786440 | tf_op jit(solution)/shard_map/ppermute | solution.py:330
  385.7 20.5 %collective-permute-start.36 = (bf16[8,64,512]{2,1,0:T(8,128)(2,1)}, bf16[8,64,512]{2,1,0:T(8,128)(2,1)}, u32[]{:S(2)}, u32[]{:S(2)}) collective-permute-start(bf16[8,64,512]{2,1,0:T(8,128)(2,1)} %get-tuple-element.214), channel_id=1, source_target_pairs={{0,4},{4,0},{8,12},{12,8},{16,20},{20,16},{24,28},{28,24},{1,5},{5... | collective-permute-start | bytes 1572872 | tf_op jit(solution)/shard_map/ppermute | solution.py:379
  390.3 15.9 %collective-permute-start.45 = (bf16[8,64,512]{2,1,0:T(8,128)(2,1)}, bf16[8,64,512]{2,1,0:T(8,128)(2,1)}, u32[]{:S(2)}, u32[]{:S(2)}) collective-permute-start(bf16[8,64,512]{2,1,0:T(8,128)(2,1)} %get-tuple-element.208), channel_id=1, source_target_pairs={{8,0},{12,4},{16,8},{20,12},{24,16},{28,20},{9,1},{13,5},{17,9},{2... | collective-permute-start | bytes 1572872 | tf_op jit(solution)/shard_map/ppermute | solution.py:379
  391.7 14.4 %collective-permute-start.44 = (bf16[8,64,512]{2,1,0:T(8,128)(2,1)}, bf16[8,64,512]{2,1,0:T(8,128)(2,1)}, u32[]{:S(2)}, u32[]{:S(2)}) collective-permute-start(bf16[8,64,512]{2,1,0:T(8,128)(2,1)} %get-tuple-element.209), channel_id=1, source_target_pairs={{0,8},{4,12},{8,16},{12,20},{16,24},{20,28},{1,9},{5,13},{9,17},{1... | collective-permute-start | bytes 1572872 | tf_op jit(solution)/shard_map/ppermute | solution.py:379
  (195 other events, 1424.6 us)

commit v4 on v3

--- a/solution.py
+++ b/solution.py
@@ -1,3 +1,6 @@
+import functools
+import math
+
 import jax
 import jax.numpy as jnp
 from jax import lax
@@ -72,11 +75,11 @@
         grid=(n,),
         in_specs=[take, take],
         out_specs=[spec, spec],
-        out_shape=[jax.ShapeDtypeStruct((n, w, w), F32)] * 2,
-        compiler_params=pltpu.CompilerParams(vmem_limit_bytes=60 << 20),
+        out_shape=[pltpu.HBM((n, w, w), F32)] * 2,
+        compiler_params=pltpu.CompilerParams(vmem_limit_bytes=24 << 20),
         cost_estimate=pl.CostEstimate(flops=n * 12 * w**3, bytes_accessed=n * 16 * w * w, transcendentals=0),
         name="before",
-    )(stat, basis)
+    )(pltpu.with_memory_space_constraint(stat, pltpu.HBM), pltpu.with_memory_space_constraint(basis, pltpu.HBM))
 
 
 PANEL = 16
@@ -151,43 +154,55 @@
     n = q_out.shape[0]
     width = g_ref.shape[2]
     rows = g_ref.shape[1]
-    g = g_ref[0]
-    q = split(q_ref[0])
-    ql = split(ql_ref[0])
-    p = mm(g, q[0], NN) + mm(g, q[1], NN)
-    turned = mm3(ql, p, TN)
-    first = 0.9 * m1_ref[0] + 0.1 * turned
-    second = 0.999 * m2_ref[0] + 0.001 * turned * turned
-    m1_out[0] = first
-    m2_out[0] = second
-    direction = first / FIX_ONE / (jnp.sqrt(second / FIX_TWO) + 1e-08)
-    update = mm3(ql, mm3(direction, q, NT), NN)
-    weight = w_ref[0]
-    weight = weight - rate_matrix * (update + 0.01 * weight)
-    w_out[0] = weight
-    c_out[0] = weight.astype(BF)
-    k = mm(g, g, NT)
-    left = 0.95 * l_ref[0] + 0.05 * k
-    l_out[0] = left
-    s_out[0] = 0.95 * s_ref[0] + 0.05 * mm(g, g, TN)
-    early = step < n // 2
-    a = jnp.where(early, ae_ref[0], al_ref[0])
-    a_parts = split(a)
-    b = 0.05 * p
-    bh, bl = split(b)
-    h = mm(g, a_parts[0], NN) + mm(g, a_parts[1], NN) + 0.5 * mm3(k, (bh, bl), NN)
-    q_out[step] = a + mm(jnp.concatenate([g, g], axis=0), jnp.concatenate([bh, bl], axis=0), TN)
-    hh, hl = split(h)
-    y = jnp.concatenate([hh, bh, hh, bh, hl, bl], axis=0)
-    z = jnp.concatenate([bh, hh, bl, hl, bh, hh], axis=0)
+    per = g_ref.shape[0]
     blk = BLOCK
-    for i in range(width // blk):
-        lo = i * blk
-        gram[step, lo : lo + blk, lo:] = jnp.where(early, me_ref[0, lo : lo + blk, lo:], ml_ref[0, lo : lo + blk, lo:]) + mm(y[:, lo : lo + blk], z[:, lo:], TN)
-    xl = mm3(left, ql, NN)
-    x_left[step] = xl
-    gl = mm3(xl, xl, TN)
-    gram_left[step] = gl
+
+    def one_slot(i, a_ref, m_ref):
+        slot = step * per + i
+        g = g_ref[i]
+        q = split(q_ref[i])
+        ql = split(ql_ref[i])
+        p = mm(g, q[0], NN) + mm(g, q[1], NN)
+        k = mm(g, g, NT)
+        a = a_ref[i]
+        a_parts = split(a)
+        b = 0.05 * p
+        bh, bl = split(b)
+        h = mm(g, a_parts[0], NN) + mm(g, a_parts[1], NN) + 0.5 * mm3(k, (bh, bl), NN)
+        q_out[slot] = a + mm(jnp.concatenate([g, g], axis=0), jnp.concatenate([bh, bl], axis=0), TN)
+        hh, hl = split(h)
+        y = jnp.concatenate([hh, bh, hh, bh, hl, bl], axis=0)
+        z = jnp.concatenate([bh, hh, bl, hl, bh, hh], axis=0)
+        for j in range(width // blk):
+            lo = j * blk
+            gram[slot, lo : lo + blk, lo:] = m_ref[i, lo : lo + blk, lo:] + mm(y[:, lo : lo + blk], z[:, lo:], TN)
+        left = 0.95 * l_ref[i] + 0.05 * k
+        l_out[i] = left
+        xl = mm3(left, ql, NN)
+        x_left[slot] = xl
+        gram_left[slot] = mm3(xl, xl, TN)
+        s_out[i] = 0.95 * s_ref[i] + 0.05 * mm(g, g, TN)
+        turned = mm3(ql, p, TN)
+        first = 0.9 * m1_ref[i] + 0.1 * turned
+        second = 0.999 * m2_ref[i] + 0.001 * turned * turned
+        m1_out[i] = first
+        m2_out[i] = second
+        direction = first / FIX_ONE / (jnp.sqrt(second / FIX_TWO) + 1e-08)
+        update = mm3(ql, mm3(direction, q, NT), NN)
+        weight = w_ref[i]
+        weight = weight - rate_matrix * (update + 0.01 * weight)
+        w_out[i] = weight
+        c_out[i] = weight.astype(BF)
+
+    @pl.when(step * per < n // 2)
+    def _():
+        for i in range(per):
+            one_slot(i, ae_ref, me_ref)
+
+    @pl.when(step * per >= n // 2)
+    def _():
+        for i in range(per):
+            one_slot(i, al_ref, ml_ref)
 
     @pl.when(step == count - 1)
     def _():
@@ -274,16 +289,17 @@
 
 def after(grad, weight, m1, m2, left, ql, stat, q, early, late):
     n, rows, width = weight.shape
-    half = n // 2
-    first = pl.BlockSpec((1, width, width), lambda i: (jnp.minimum(i, half - 1), 0, 0))
-    second = pl.BlockSpec((1, width, width), lambda i: (jnp.maximum(i - half, 0), 0, 0))
-    wide = pl.BlockSpec((1, width, width), lambda i: (i, 0, 0))
-    flat = pl.BlockSpec((1, rows, width), lambda i: (i, 0, 0))
-    small = pl.BlockSpec((1, rows, rows), lambda i: (i, 0, 0))
+    per = 2 if n % 4 == 0 else 1
+    half = n // 2 // per
+    first = pl.BlockSpec((per, width, width), lambda i: (jnp.minimum(i, half - 1), 0, 0))
+    second = pl.BlockSpec((per, width, width), lambda i: (jnp.maximum(i - half, 0), 0, 0))
+    wide = pl.BlockSpec((per, width, width), lambda i: (i, 0, 0))
+    flat = pl.BlockSpec((per, rows, width), lambda i: (i, 0, 0))
+    small = pl.BlockSpec((per, rows, rows), lambda i: (i, 0, 0))
     sd = jax.ShapeDtypeStruct
     return pl.pallas_call(
         after_kernel,
-        grid=(n,),
+        grid=(n // per,),
         in_specs=[flat, flat, flat, flat, small, small, wide, wide, first, first, second, second],
         out_specs=[
             flat, flat, flat, small, wide,
@@ -382,7 +398,7 @@
 def gather_owners(own, beside):
     count = lax.axis_size("dp")
     if count != 8:
-        return lax.all_gather(own, "dp", axis=0, tiled=True), [make() for make in beside]
+        return [lax.all_gather(own, "dp", axis=0, tiled=True)], [make() for make in beside]
     across = [(i, i ^ 1) for i in range(8)]
     z = lax.axis_index("dp") // 2
     even = (z & 1) == 0
@@ -408,36 +424,77 @@
         if s < 3:
             ups.append(moved[1])
             downs.append(moved[2])
-    far_rel = [
-        far[0],
-        jnp.where(z == 0, far[3], jnp.where(z == 1, far[1], jnp.where(z == 2, far[2], far[1]))),
-        jnp.where(z == 0, far[2], jnp.where(z == 1, far[3], jnp.where(z == 2, far[3], far[2]))),
-        jnp.where(z == 0, far[1], jnp.where(z == 1, far[2], jnp.where(z == 2, far[1], far[3]))),
-    ]
-    parts = [own, far_rel[0]]
-    for s in range(1, 4):
-        parts.append(ups[s] + downs[4 - s])
-        parts.append(far_rel[s])
-    return jnp.concatenate(parts, axis=0), made
-
-
-def owner_place(owner):
+    return [own] + ups[1:] + downs[1:] + far, made
+
+
+def owner_place(slot, capacity):
     if lax.axis_size("dp") != 8:
-        return owner
+        return jnp.zeros_like(slot), slot
+    owner = slot // capacity
     me = lax.axis_index("dp")
-    return ((me // 2 - owner // 2) % 4) * 2 + ((me ^ owner) & 1)
-
-
-def sum_to_owner(blocks, block_of, capacity):
+    away = me // 2 - owner // 2
+    near = jnp.where(away >= 0, away, 3 - away)
+    rounds = jnp.array([[0, 1, 2, 3], [1, 0, 2, 3], [3, 2, 0, 1], [3, 2, 1, 0]], jnp.int32)
+    far = 7 + rounds[me // 2][owner // 2]
+    return jnp.where(((me ^ owner) & 1) == 0, near, far), slot % capacity
+
+
+def collect(sources, which, row, counts):
+    block = sources[0].shape[1:]
+    total = sum(counts)
+
+    def kernel(which_ref, row_ref, *refs):
+        source_refs, out_refs = refs[: len(sources)], refs[len(sources) :]
+        first = 0
+        for out, count in zip(out_refs, counts):
+
+            def one(k, carry, out=out, first=first):
+                source_of, row_of = which_ref[first + k], row_ref[first + k]
+                for u, source in enumerate(source_refs):
+
+                    @pl.when(source_of == u)
+                    def _(source=source):
+                        out[k] = source[row_of]
+
+                return carry
+
+            lax.fori_loop(0, count, one, 0)
+            first += count
+
+    near = pl.BlockSpec(memory_space=pltpu.VMEM)
+    scalars = pl.BlockSpec(memory_space=pltpu.SMEM)
+    return pl.pallas_call(
+        kernel,
+        in_specs=[scalars, scalars] + [near] * len(sources),
+        out_specs=[near] * len(counts),
+        out_shape=[jax.ShapeDtypeStruct((count,) + block, sources[0].dtype) for count in counts],
+        compiler_params=pltpu.CompilerParams(vmem_limit_bytes=24 << 20),
+        cost_estimate=pl.CostEstimate(flops=0, bytes_accessed=2 * total * block[0] * block[1] * 2, transcendentals=0),
+        name="collect",
+    )(which, row, *sources)
+
+
+def sum_to_owner(layers, block_of, capacity):
+    starts, start = [], 0
+    for layer in layers:
+        starts.append(start)
+        start += layer.shape[0]
+    sources = list(layers) + [jnp.zeros((1,) + layers[0].shape[1:], layers[0].dtype)]
+    which = sum((block_of >= at).astype(jnp.int32) for at in starts[1:] + [start])
+    row = block_of - jnp.array(starts + [start], jnp.int32)[which]
     if lax.axis_size("dp") != 8:
-        return lax.psum_scatter(blocks[block_of], "dp", scatter_dimension=0, tiled=True)
+        (placed,) = collect(sources, which, row, [block_of.shape[0]])
+        return lax.psum_scatter(placed, "dp", scatter_dimension=0, tiled=True)
     me = lax.axis_index("dp")
     z = me // 2
     order = jnp.array([[3, 2, 1, 0], [3, 2, 0, 1], [0, 1, 3, 2], [0, 1, 2, 3]], jnp.int32)[z]
-    table = block_of.reshape(8, capacity)
-    give = blocks[table[order * 2 + ((me & 1) ^ 1)].reshape(-1)].reshape((4, capacity) + blocks.shape[1:])
-    keep = blocks[table[order * 2 + (me & 1)].reshape(-1)].reshape((4, capacity) + blocks.shape[1:])
+    units = jnp.concatenate([order * 2 + ((me & 1) ^ 1), order * 2 + (me & 1)])
+    which = which.reshape(8, capacity)[units].reshape(-1)
+    row = row.reshape(8, capacity)[units].reshape(-1)
+    give = collect(sources, which[: 4 * capacity], row[: 4 * capacity], [capacity] * 4)
+    keep = collect(sources, which[4 * capacity :], row[4 * capacity :], [capacity] * 4)
     across = [(i, i ^ 1) for i in range(8)]
+
     def swapped(k):
         return shift(give[k], "dp", across)
 
@@ -463,104 +520,251 @@
     return (total(3, moved[0]) + moved[1].astype(F32) + moved[2].astype(F32)).astype(BF)
 
 
-def project(rows, matrix):
-    return mm(rows, matrix, NT)
-
-
-def join_core(own, width):
-    other = swap_core(own)
-    half = width // 2
-    parts = []
-    for start in range(0, own.shape[1], width):
-        parts.append(other[:, start + half : start + width])
-        parts.append(other[:, start : start + half])
-    return jnp.concatenate([own, jnp.concatenate(parts, axis=1)], axis=0)
-
-
-def attention_scores(query, key, allowed):
-    scale = query.shape[-1] ** (-0.5)
-    scores = jnp.einsum("qhe,khe->hqk", query, key, preferred_element_type=F32) * scale
-    return jnp.where(allowed[None], scores, -1e30)
-
-
-def heads_of(rows, size):
-    return rows.reshape(rows.shape[0], -1, size)
-
-
-def attention_forward(query_rows, key_rows, weights, allowed, size):
-    w_query, w_key, w_value, w_out = weights
-    width = w_query.shape[0]
-    query = project(query_rows, w_query).astype(BF)
-    pair = project(key_rows, jnp.concatenate([w_key, w_value], axis=0)).astype(BF)
-    pair = join_core(pair, width)
-    key, value = pair[:, :width], pair[:, width:]
-    scores = attention_scores(heads_of(query, size), heads_of(key, size), allowed)
-    top = jnp.max(scores, axis=-1, keepdims=True)
-    powers = jnp.exp(scores - top)
-    total = jnp.sum(powers, axis=-1, keepdims=True)
-    chance = powers / total
-    log_total = top + jnp.log(total)
-    mixed = jnp.einsum("hqk,khe->qhe", chance.astype(BF), heads_of(value, size), preferred_element_type=F32)
-    mixed = mixed.astype(BF).reshape(query.shape)
-    return mm(mixed, w_out, NN), (query, key, value, log_total, mixed)
-
-
-def attention_backward(grad, saved, weights, query_rows, key_rows, allowed, size):
-    w_query, w_key, w_value, w_out = weights
-    query, key, value, log_total, mixed = saved
-    width = query.shape[1]
-    own = key_rows.shape[0]
-    grad_b = grad.astype(BF)
-    grad_mixed = heads_of(mm(grad_b, w_out, NT).astype(BF), size)
-    grad_out_w = mm(mixed, grad_b, TN)
-    query_h, key_h, value_h = heads_of(query, size), heads_of(key, size), heads_of(value, size)
-    scores = attention_scores(query_h, key_h, allowed)
-    chance = jnp.exp(scores - log_total)
-    grad_value = jnp.einsum("hqk,qhe->khe", chance.astype(BF), grad_mixed, preferred_element_type=F32)
-    grad_chance = jnp.einsum("qhe,khe->hqk", grad_mixed, value_h, preferred_element_type=F32)
-    inner = jnp.sum(chance * grad_chance, axis=-1, keepdims=True)
-    grad_score = (chance * (grad_chance - inner)).astype(BF)
+UNIT_ATTENTION = ((0, 0), (0, 1), (1, 2))
+UNIT_FEED = ((1, 0), (1, 3))
+
+
+def rows_of(ref):
+    return ref[...].reshape(-1, ref.shape[-1])
+
+
+def unit_spec(unit, blocks, like):
+    return pl.BlockSpec((blocks,) + like.shape[1:], lambda *i: (unit, 0, 0))
+
+
+def whole(like):
+    rank = len(like.shape)
+    return pl.BlockSpec(like.shape, lambda *i: (0,) * rank)
+
+
+def tall(like, size):
+    return pl.BlockSpec((size, like.shape[1]), lambda i: (i, 0))
+
+
+def call(kernel, grid, ins, in_specs, outs, out_specs, flops, limit, scratch=(), name=None):
+    moved = sum(math.prod(v.shape) * v.dtype.itemsize for v in list(ins) + list(outs))
+    return pl.pallas_call(
+        kernel,
+        grid=grid,
+        in_specs=in_specs,
+        out_specs=out_specs,
+        out_shape=outs,
+        scratch_shapes=list(scratch),
+        compiler_params=pltpu.CompilerParams(vmem_limit_bytes=limit << 20),
+        cost_estimate=pl.CostEstimate(flops=int(flops), bytes_accessed=int(moved), transcendentals=0),
+        name=name,
+    )(*ins)
+
+
+def row_block(count):
+    return count // 2 if count % 32 == 0 else count
+
+
+def pair_of(mine_ref, away_ref, group, value):
+    wide = mine_ref.shape[2] // 2
+    at = value * wide
+    return jnp.concatenate([mine_ref[group, :, at : at + wide], away_ref[1 - group, :, at : at + wide]], axis=0)
+
+
+def attend_kernel(
+    size, causal, rows_ref, pair_ref, away_ref, own_ref, other_ref, mask_ref, place_ref,
+    part_ref, e_ref, inverse_ref, mixed_ref, q_ref,
+):
+    wide = q_ref.shape[1] // 2
+    heads = wide // size
+    rows = rows_ref[...]
+    count = rows.shape[0]
+    lanes = lax.broadcasted_iota(jnp.int32, (count, wide), 1)
+    if causal:
+        allowed = place_ref[...] < mask_ref[...]
+    else:
+        one = (lanes == 0).astype(BF)
+    ones = jnp.ones((pair_ref.shape[1] * 2, wide), BF)
+    inverses = jnp.zeros((count, wide), F32)
+    part = None
+    for group, w_ref in enumerate((own_ref, other_ref)):
+        weight = rows_of(w_ref)
+        query = mm(rows, weight[:wide], NT).astype(BF)
+        q_ref[:, group * wide : group * wide + wide] = query
+        query = query.astype(F32) * size ** (-0.5)
+        key = pair_of(pair_ref, away_ref, group, 0)
+        if not causal:
+            key = jnp.concatenate([key, mask_ref[...]], axis=1)
+        value = jnp.concatenate([pair_of(pair_ref, away_ref, group, 1), ones], axis=1)
+        mixed = None
+        for h in range(heads):
+            here = (lanes >= h * size) & (lanes < h * size + size)
+            lhs = jnp.where(here, query, 0.0).astype(BF)
+            if causal:
+                scores = jnp.where(allowed, mm(lhs, key, NT), -1e30)
+            else:
+                scores = mm(jnp.concatenate([lhs, one], axis=1), key, NT)
+            powers = jnp.exp(scores - jnp.max(scores, axis=1, keepdims=True)).astype(BF)
+            e_ref[group * heads + h] = powers
+            got = mm(powers, value, NN)
+            inverse = 1.0 / got[:, wide:]
+            inverses = jnp.where(lanes == group * heads + h, inverse, inverses)
+            got = got[:, :wide] * inverse
+            mixed = got if h == 0 else jnp.where(here, got, mixed)
+        mixed = mixed.astype(BF)
+        mixed_ref[:, group * wide : group * wide + wide] = mixed
+        term = mm(mixed, weight[3 * wide :], NN)
+        part = term if part is None else part + term
+    inverse_ref[...] = inverses
+    part_ref[...] = part.astype(BF)
+
+
+def attend(rows, pair, away, weights, unit, causal, mask, place, size):
+    own, other, blocks = weights
+    count, width = rows.shape
+    wide = pair.shape[2] // 2
+    step = row_block(count)
+    heads = 2 * wide // size
+    spec = unit_spec(unit, blocks, own)
+    sd = jax.ShapeDtypeStruct
+    return call(
+        functools.partial(attend_kernel, size, causal),
+        (count // step,),
+        [rows, pair, away, own, other, mask, place],
+        [tall(rows, step), whole(pair), whole(away), spec, spec, tall(mask, step) if causal else whole(mask), whole(place)],
+        [
+            sd((count, width), BF), pltpu.HBM((heads, count, 2 * count), BF), sd((count, wide), F32),
+            sd((count, 2 * wide), BF), sd((count, 2 * wide), BF),
+        ],
+        [
+            pl.BlockSpec((step, width), lambda i: (i, 0)),
+            pl.BlockSpec((heads, step, 2 * count), lambda i: (0, i, 0)),
+            pl.BlockSpec((step, wide), lambda i: (i, 0)),
+            pl.BlockSpec((step, 2 * wide), lambda i: (i, 0)),
+            pl.BlockSpec((step, 2 * wide), lambda i: (i, 0)),
+        ],
+        16 * heads * count * count * size,
+        32,
+        name="attend",
+    )
+
+
+def attend_back_kernel(
+    size, g_ref, e_ref, inverse_ref, mixed_ref, q_ref, pair_ref, away_ref, own_ref, other_ref,
+    dq_ref, rows_ref, mine_ref, give_ref, total,
+):
+    step = pl.program_id(0)
+    wide = q_ref.shape[1] // 2
+    heads = wide // size
+    count = pair_ref.shape[1]
     scale = size ** (-0.5)
-    grad_query = jnp.einsum("hqk,khe->qhe", grad_score, key_h, preferred_element_type=F32) * scale
-    grad_key = jnp.einsum("hqk,qhe->khe", grad_score, query_h, preferred_element_type=F32) * scale
-    grad_query = grad_query.astype(BF).reshape(query.shape)
-    both = jnp.concatenate([grad_key.reshape(key.shape), grad_value.reshape(key.shape)], axis=1)
-    half = width // 2
-    away = both[own:].astype(BF)
-    away = swap_core(away)
-    away = jnp.concatenate(
-        [away[:, half:width], away[:, :half], away[:, width + half :], away[:, width : width + half]], axis=1
+    lanes = lax.broadcasted_iota(jnp.int32, (q_ref.shape[0], wide), 1)
+    grad = g_ref[...]
+
+    @pl.when(step == 0)
+    def _():
+        total[...] = jnp.zeros_like(total)
+
+    rows = None
+    for group, w_ref in enumerate((own_ref, other_ref)):
+        weight = rows_of(w_ref)
+        cols = slice(group * wide, group * wide + wide)
+        key = pair_of(pair_ref, away_ref, group, 0)
+        value = pair_of(pair_ref, away_ref, group, 1)
+        back = mm(grad, weight[3 * wide :], NT).astype(BF).astype(F32)
+        inner = back * mixed_ref[:, cols].astype(F32)
+        inverses = [inverse_ref[:, group * heads + h : group * heads + h + 1] for h in range(heads)]
+        spread = jnp.broadcast_to(inverses[0], back.shape)
+        for h in range(1, heads):
+            spread = jnp.where(lanes >= h * size, inverses[h], spread)
+        back = back * spread
+        inner = inner * spread
+        back_t = back.T.astype(BF)
+        query_t = (q_ref[:, cols].astype(F32) * scale).T.astype(BF)
+        dq = None
+        for h in range(heads):
+            here = (lanes >= h * size) & (lanes < h * size + size)
+            powers = e_ref[group * heads + h]
+            level = jnp.sum(jnp.where(here, inner, 0.0), axis=1, keepdims=True)
+            slope = mm(jnp.where(here, back, 0.0).astype(BF), value, NT)
+            ds = (powers.astype(F32) * (slope - level)).astype(BF)
+            got = mm(ds, key, NN)
+            dq = got if h == 0 else jnp.where(here, got, dq)
+            k_at = group * 2 * wide + h * size
+            v_at = k_at + wide
+            total[k_at : k_at + size, :] += mm(query_t[h * size : h * size + size], ds, NN)
+            total[v_at : v_at + size, :] += mm(back_t[h * size : h * size + size], powers, NN)
+        dq = (dq * scale).astype(BF)
+        dq_ref[:, cols] = dq
+        term = mm(dq, weight[:wide], NN)
+        rows = term if rows is None else rows + term
+    rows_ref[...] = rows.astype(rows_ref.dtype)
+
+    @pl.when(step == pl.num_programs(0) - 1)
+    def _():
+        mine_ref[...] = total[:, :count]
+        give_ref[: 2 * wide, :] = total[2 * wide :, count:].astype(BF)
+        give_ref[2 * wide :, :] = total[: 2 * wide, count:].astype(BF)
+
+
+def attend_back(grad, powers, inverse, mixed, query, pair, away, weights, unit, size, kind):
+    own, other, blocks = weights
+    count, width = grad.shape
+    wide = inverse.shape[1]
+    step = row_block(count)
+    heads = 2 * wide // size
+    spec = unit_spec(unit, blocks, own)
+    sd = jax.ShapeDtypeStruct
+    flat = sd((4 * wide, count), F32)
+    return call(
+        functools.partial(attend_back_kernel, size),
+        (count // step,),
+        [grad, powers, inverse, mixed, query, pair, away, own, other],
+        [
+            tall(grad, step), pl.BlockSpec((heads, step, 2 * count), lambda i: (0, i, 0)), tall(inverse, step),
+            tall(mixed, step), tall(query, step), whole(pair), whole(away), spec, spec,
+        ],
+        [sd((count, 2 * wide), BF), sd((count, width), kind), flat, sd(flat.shape, BF)],
+        [
+            pl.BlockSpec((step, 2 * wide), lambda i: (i, 0)),
+            pl.BlockSpec((step, width), lambda i: (i, 0)),
+            whole(flat),
+            whole(flat),
+        ],
+        32 * heads * count * count * size,
+        32,
+        scratch=[pltpu.VMEM((4 * wide, 2 * count), F32)],
+        name="attend_back",
     )
-    both = (both[:own] + away.astype(F32)).astype(BF)
-    grad_key, grad_value = both[:, :width], both[:, width:]
-    grads = [
-        mm(grad_query, query_rows, TN),
-        mm(grad_key, key_rows, TN),
-        mm(grad_value, key_rows, TN),
-        grad_out_w,
-    ]
-    part_query = mm(grad_query, w_query, NN)
-    part_key = mm(grad_key, w_key, NN) + mm(grad_value, w_value, NN)
-    return grads, part_query, part_key
-
-
-def gelu(values):
-    return jax.nn.gelu(values, approximate=False)
-
-
-def feed_forward(rows, w_in, w_down):
-    hidden = project(rows, w_in)
-    active = gelu(hidden).astype(BF)
-    return mm(active, w_down, NN), (hidden, active)
-
-
-def feed_backward(grad, saved, w_in, w_down, rows):
-    hidden, active = saved
-    grad_b = grad.astype(BF)
-    grad_active = mm(grad_b, w_down, NT)
-    grad_hidden = jax.vjp(gelu, hidden)[1](grad_active)[0].astype(BF)
-    grads = [mm(grad_hidden, rows, TN), mm(active, grad_b, TN)]
-    return grads, mm(grad_hidden, w_in, NN)
+
+
+def feed_kernel(rows_ref, own_in, other_in, own_out, other_out, part_ref, active_ref, slope_ref):
+    rows = rows_ref[...]
+    size = active_ref.shape[1] // 2
+    part = None
+    for group, (w_in, w_out) in enumerate(((own_in, own_out), (other_in, other_out))):
+        u = mm(rows, rows_of(w_in), NT)
+        phi = 0.5 + 0.5 * lax.erf(u * 0.5**0.5)
+        active = (u * phi).astype(BF)
+        active_ref[:, group * size : group * size + size] = active
+        slope_ref[:, group * size : group * size + size] = (
+            phi + u * (jnp.exp(-0.5 * u * u) * 0.3989422804014327)
+        ).astype(BF)
+        term = mm(active, rows_of(w_out), NN)
+        part = term if part is None else part + term
+    part_ref[...] = part.astype(BF)
+
+
+def feed(rows, weights, unit):
+    own, other, blocks = weights
+    count, width = rows.shape
+    step = row_block(count)
+    size = 2 * blocks * own.shape[1]
+    first, second = unit_spec(unit, blocks, own), unit_spec(unit + 1, blocks, own)
+    sd = jax.ShapeDtypeStruct
+    return call(
+        feed_kernel, (count // step,), [rows, own, other, own, other], [tall(rows, step), first, first, second, second],
+        [sd((count, width), BF), sd((count, size), BF), sd((count, size), BF)],
+        [pl.BlockSpec((step, w), lambda i: (i, 0)) for w in (width, size, size)],
+        4 * count * width * size,
+        20,
+        name="feed",
+    )
 
 
 def per_device(
@@ -593,7 +797,7 @@
     width = master.shape[3]
 
     half = max(capacity // 2, 1)
-    gathered, made = gather_owners(
+    sources, made = gather_owners(
         master[0].astype(BF),
         [
             lambda: (before(stat_right[0], basis_right[0], 0, half), gather_chips(source[0])),
@@ -603,18 +807,12 @@
     )
     (early, src), (late, tgt), cot = made
     slot_of = slot_positions(owners[0], capacity)
-    blocks = gathered[owner_place(slot_of // capacity) * capacity + slot_of % capacity]
-    other_blocks = swap_core(blocks)
-    extents = [head_count] * 4 + [col_count] * 2 + [head_count] * 8 + [col_count] * 2
-    matrices = []
-    offset = 0
-    for extent in extents:
-        matrices.append(
-            jnp.concatenate([blocks[offset : offset + extent], other_blocks[offset : offset + extent]], axis=0).reshape(
-                2 * extent * block_rows, width
-            )
-        )
-        offset += extent
+    which, row = owner_place(slot_of, capacity)
+    order = [j for unit in (0, 3, 1, 2, 4, 5, 6) for j in range(unit * col_count, (unit + 1) * col_count)]
+    order = jnp.array(order, jnp.int32)
+    blocks = collect(sources, which[order], row[order], [2 * col_count, 5 * col_count])
+    weights = [(part, swap_core(part), col_count) for part in blocks]
+    wide = head_count * block_rows
 
     chips = tensor_count // 2
     local = lax.iota(jnp.int32, row_count * chips)
@@ -626,65 +824,108 @@
     src_size = src_len[0]
     tgt_size = tgt_len[0]
     total_rows = local.shape[0]
-    enc_allowed = jnp.broadcast_to(key_pos[None, :] < src_size, (total_rows, 2 * total_rows))
-    dec_allowed = (key_pos[None, :] <= own_pos[:, None]) & (key_pos[None, :] < tgt_size)
+    place = key_pos[None, :]
+    first_lane = lax.iota(jnp.int32, wide)[None, :] == 0
+    enc_mask = jnp.where((key_pos[:, None] >= src_size) & first_lane, -1e30, 0.0).astype(BF)
+    dec_mask = jnp.minimum(own_pos + 1, tgt_size)[:, None]
     keep_rows = (own_pos < tgt_size).astype(F32)[:, None]
 
-    branch_one, saved_one = attention_forward(src, src, matrices[0:4], enc_allowed, block_rows)
+    def matrices(place_of, start, stop):
+        part, unit = place_of
+        at = unit * col_count
+        return [w[at + start : at + stop].reshape(-1, width) for w in weights[part][:2]]
+
+    def attention(query_rows, key_rows, unit, causal):
+        pair = jnp.stack([mm(key_rows, w, NT).astype(BF) for w in matrices(unit, head_count, 3 * head_count)])
+        away = swap_core(pair)
+        mask = dec_mask if causal else enc_mask
+        part, *saved = attend(query_rows, pair, away, weights[unit[0]], unit[1], causal, mask, place, block_rows)
+        return part, saved + [pair, away]
+
+    def halves(first, second):
+        half = first.shape[1] // 2
+        return mm(first[:, :half], second, TN), mm(first[:, half:], second, TN)
+
+    def attention_back(grad, saved, query_rows, key_rows, unit, together):
+        powers, inverse, mixed, query, pair, away = saved
+        grad_b = grad.astype(BF)
+        dq, query_part, mine, give = attend_back(
+            grad_b, powers, inverse, mixed, query, pair, away, weights[unit[0]], unit[1], block_rows, F32 if together else BF
+        )
+        both = (mine + swap_core(give).astype(F32)).astype(BF)
+        parts = [both[: 2 * wide], both[2 * wide :]]
+        key_part = sum(mm(p, w, TN) for p, w in zip(parts, matrices(unit, head_count, 3 * head_count)))
+        if together:
+            key_part = key_part + query_part
+        grad_q = halves(dq, query_rows)
+        grad_o = halves(mixed, grad_b)
+        grads = [[grad_q[at], mm(parts[at], key_rows, NN), grad_o[at]] for at in range(2)]
+        return grads, query_part, key_part
+
+    def feeding(rows, unit):
+        part, active, slope = feed(rows, weights[unit[0]], unit[1])
+        return part, (active, slope)
+
+    def feeding_back(grad, saved, rows, unit):
+        active, slope = saved
+        grad_b = grad.astype(BF)
+        half = active.shape[1] // 2
+        grads, part = [], 0.0
+        for at, w_in, w_out in zip(range(2), matrices(unit, 0, col_count), matrices((unit[0], unit[1] + 1), 0, col_count)):
+            cols = slice(at * half, at * half + half)
+            du = (mm(grad_b, w_out, NT) * slope[:, cols].astype(F32)).astype(BF)
+            part = part + mm(du, w_in, NN)
+            grads.append([mm(du, rows, TN), mm(active[:, cols], grad_b, TN)])
+        return grads, part
+
+    one, three, four = UNIT_ATTENTION
+    two, five = UNIT_FEED
+    branch_one, saved_one = attention(src, src, one, False)
     z_one = src.astype(F32) + sum_chips(branch_one)
     h_one, pull_one = jax.vjp(layer_norm, z_one, gains[0], shifts[0])
     h_one_b = h_one.astype(BF)
-    branch_two, saved_two = feed_forward(h_one_b, matrices[4], matrices[5])
+    branch_two, saved_two = feeding(h_one_b, two)
     z_two = h_one + sum_chips(branch_two)
     encoded, pull_two = jax.vjp(layer_norm, z_two, gains[1], shifts[1])
     encoded_b = encoded.astype(BF)
-    branch_three, saved_three = attention_forward(tgt, tgt, matrices[6:10], dec_allowed, block_rows)
+    branch_three, saved_three = attention(tgt, tgt, three, True)
     z_three = tgt.astype(F32) + sum_chips(branch_three)
     g_one, pull_three = jax.vjp(layer_norm, z_three, gains[2], shifts[2])
     g_one_b = g_one.astype(BF)
-    branch_four, saved_four = attention_forward(g_one_b, encoded_b, matrices[10:14], enc_allowed, block_rows)
+    branch_four, saved_four = attention(g_one_b, encoded_b, four, False)
     z_four = g_one + sum_chips(branch_four)
     g_two, pull_four = jax.vjp(layer_norm, z_four, gains[3], shifts[3])
     g_two_b = g_two.astype(BF)
-    branch_five, saved_five = feed_forward(g_two_b, matrices[14], matrices[15])
+    branch_five, saved_five = feeding(g_two_b, five)
     z_five = g_two + sum_chips(branch_five)
     normed, pull_five = jax.vjp(layer_norm, z_five, gains[4], shifts[4])
     decoded = own_rows((normed * keep_rows).astype(BF))
 
     grad_z_five, gain_five, shift_five = pull_five(cot.astype(F32) * keep_rows)
-    weights_five, rows_five = feed_backward(grad_z_five, saved_five, matrices[14], matrices[15], g_two_b)
+    weights_five, rows_five = feeding_back(grad_z_five, saved_five, g_two_b, five)
     grad_z_four, gain_four, shift_four = pull_four(grad_z_five + sum_chips(rows_five))
-    weights_four, query_four, key_four = attention_backward(
-        grad_z_four, saved_four, matrices[10:14], g_one_b, encoded_b, enc_allowed, block_rows
-    )
+    weights_four, query_four, key_four = attention_back(grad_z_four, saved_four, g_one_b, encoded_b, four, False)
     grad_encoded = sum_chips(key_four)
-    grad_z_three, gain_three, shift_three = pull_three(grad_z_four + sum_chips(query_four))
-    weights_three, query_three, key_three = attention_backward(
-        grad_z_three, saved_three, matrices[6:10], tgt, tgt, dec_allowed, block_rows
-    )
-    tgt_grad = own_rows(grad_z_three) + sum_chips_own(query_three + key_three)
+    query_four, weights_four = lax.optimization_barrier((query_four, weights_four))
+    query_sum = sum_chips(query_four)
     grad_z_two, gain_two, shift_two = pull_two(grad_encoded)
-    weights_two, rows_two = feed_backward(grad_z_two, saved_two, matrices[4], matrices[5], h_one_b)
-    grad_z_one, gain_one, shift_one = pull_one(grad_z_two + sum_chips(rows_two))
-    weights_one, query_one, key_one = attention_backward(
-        grad_z_one, saved_one, matrices[0:4], src, src, enc_allowed, block_rows
-    )
-    src_grad = own_rows(grad_z_one) + sum_chips_own(query_one + key_one)
+    weights_two, rows_two = feeding_back(grad_z_two, saved_two, h_one_b, two)
+    query_sum, rows_two = lax.optimization_barrier((query_sum, rows_two.astype(BF)))
+    sum_two = sum_chips(rows_two)
+    grad_z_three, gain_three, shift_three = pull_three(grad_z_four + query_sum)
+    weights_three, _, rows_three = attention_back(grad_z_three, saved_three, tgt, tgt, three, True)
+    sum_two, rows_three = lax.optimization_barrier((sum_two, rows_three))
+    tgt_grad = own_rows(grad_z_three) + sum_chips_own(rows_three)
+    grad_z_one, gain_one, shift_one = pull_one(grad_z_two + sum_two)
+    weights_one, _, rows_one = attention_back(grad_z_one, saved_one, src, src, one, True)
+    src_grad = own_rows(grad_z_one) + sum_chips_own(rows_one)
 
     def reduce_core(grads):
-        mine, away = [], []
-        for item in grads:
-            half = item.shape[0] // 2
-            mine.append(item[:half].reshape(-1, block_rows, width))
-            away.append(item[half:].reshape(-1, block_rows, width))
-        other = swap_core(jnp.concatenate(away, axis=0).astype(BF))
-        return (jnp.concatenate(mine, axis=0) + other.astype(F32)).astype(BF)
-
-    block_grad = jnp.concatenate(
-        [reduce_core(item) for item in (weights_one, weights_two, weights_three, weights_four, weights_five)]
-        + [jnp.zeros((1, block_rows, width), BF)],
-        axis=0,
-    )
+        mine, give = [jnp.concatenate(part, axis=0) for part in grads]
+        total = mine + swap_core(give.astype(BF)).astype(F32)
+        return total.astype(BF).reshape(-1, block_rows, width)
+
+    layers = [reduce_core(item) for item in (weights_one, weights_two, weights_three, weights_four, weights_five)]
     norm_local = jnp.stack(
         [
             jnp.stack([gain_one, gain_two, gain_three, gain_four, gain_five]),
@@ -694,7 +935,7 @@
     held = slot_of[None, :] == jnp.arange(slot_count, dtype=jnp.int32)[:, None]
     block_of = jnp.sum(jnp.where(held, jnp.arange(slot_of.shape[0], dtype=jnp.int32)[None, :], 0), axis=1)
     block_of = jnp.where(jnp.any(held, axis=1), block_of, slot_of.shape[0])
-    own_grad = sum_to_owner(block_grad, block_of, capacity)
+    own_grad = sum_to_owner(layers, block_of, capacity)
     norm_grad = sum_everywhere(norm_local)
     results = after(
         own_grad,

time: 487 us -> 432 us (0.89)
  matrix products: 73.9 us -> 22.3 us
  Pallas kernels: 91.4 us -> 141 us
  other arithmetic: 92.1 us -> 45.1 us
  waiting for transfers between devices: 80.7 us -> 123 us
  local copies, waits for them, and re-layouts: 69 us -> 35.2 us
  starting transfers between devices: 68.6 us -> 56.7 us
    pallas_call x1 -> x12, Pallas kernels: 72.1 us -> 121 us  [the longest x1 70.8 us: after(): pl.pallas_call(after_kernel, grid=(n // per,), in_specs=[flat, flat, flat...]
    dot_general x18 -> x0, matrix products: 35.9 us -> none  [the longest x3 8.57 us: attention_backward(): jnp.einsum('hqk,qhe->khe', chance.astype(BF), grad_mixed, preferred_eleme...]
    slice x63 -> x12, local copies, waits for them, and re-layouts: 26.2 us -> 0.87 us  [the longest x6 0.53 us: matrices(): w[at + start:at + stop].reshape(-1, width)]
    unnamed x13 -> x0, other arithmetic: 18.4 us -> none
    concatenate x21 -> x6, other arithmetic: 20.3 us -> 2.74 us  [the longest x5 2.02 us: reduce_core(): mine, give = [jnp.concatenate(part, axis=0) for part in grads]]
    dot_general x45 -> x46, matrix products: 38 us -> 22.3 us  [mm(): return lax.dot_general(a, b, dims, preferred_element_type=F32)]
    ppermute x20, waiting for transfers between devices: 21.6 us -> 37.2 us  [shift(): return lax.ppermute(values, axis, pairs)]
    ppermute x14, waiting for transfers between devices: 58.1 us -> 70.1 us  [swap_chip(): return lax.ppermute(values, 'tensor', [(i, i ^ bit) for i in range(count)])]
  transfers between devices with their start and end apart: 50 -> 51, of which waited for: 19 -> 22; matrix products, arithmetic and copies ran while one was open for 32% -> 15% of each run, Pallas kernels for 4% -> 13%
where the time goes in v4:
time: 432 us; the launch traced here: 427 us
  Pallas kernels  141 us (33%)
  waiting for transfers between devices  123 us (28%)
  starting transfers between devices  56.7 us (13%)
  other arithmetic  45.1 us (10%)
  local copies, waits for them, and re-layouts  35.2 us (8%)
  matrix products  22.3 us (5%)
    pallas_call x1, Pallas kernels, after(): pl.pallas_call(after_kernel, grid=(n // per,), in_specs=[flat, flat, flat...  70.8 us
    ppermute x14, waiting for transfers between devices, swap_chip(): return lax.ppermute(values, 'tensor', [(i, i ^ bit) for i in range(count)])  70.1 us
    pallas_call x8, Pallas kernels, call(): pl.pallas_call(kernel, grid=grid, in_specs=in_specs, out_specs=out_specs,...  41.9 us
    ppermute x20, waiting for transfers between devices, shift(): return lax.ppermute(values, axis, pairs)  37.2 us
    ppermute x20, starting transfers between devices, shift(): return lax.ppermute(values, axis, pairs)  36.2 us
    unnamed x239, local copies, waits for them, and re-layouts  27 us
    dot_general x46, matrix products, mm(): return lax.dot_general(a, b, dims, preferred_element_type=F32)  22.3 us
    pallas_call x2, Pallas kernels, before(): pl.pallas_call(before_kernel, grid=(n,), in_specs=[take, take], out_specs...  19.3 us
  transfers between devices with their start and end apart: 51, of which 22 were waited for; matrix products, arithmetic and copies ran while one was open for 15% of the time, Pallas kernels for 13%

profile of v4, /device:TPU:0, one launch (start us, length us, event | category | flops | bytes accessed | tf_op | source)
XLA Modules:
  0.0 426.6 jit_solution(17485345077177336381)
XLA Ops:
  2.0 3.0 collective-permute-start
  5.0 3.5 collective-permute-start.1
  11.9 9.6 %before.2 = (f32[4,512,512]{2,1,0:T(8,128)}, f32[4,512,512]{2,1,0:T(8,128)}) custom-call(f32[8,512,512]{2,1,0:T(8,128)} %bitcast.266, f32[8,512,512]{2,1,0:T(8,128)} %bitcast.269), custom_call_target="tpu_custom_call" | custom-call | flops 6442450944 | bytes 16777216 | tf_op jit(solution)/shard_map/before/pallas_call | solution.py:73
  27.5 9.6 %before.3 = (f32[4,512,512]{2,1,0:T(8,128)}, f32[4,512,512]{2,1,0:T(8,128)}) custom-call(f32[8,512,512]{2,1,0:T(8,128)} %bitcast.267, f32[8,512,512]{2,1,0:T(8,128)} %bitcast.270), custom_call_target="tpu_custom_call" | custom-call | flops 6442450944 | bytes 16777216 | tf_op jit(solution)/shard_map/before/pallas_call | solution.py:73
  38.1 2.0 maximum_select_fusion.1.rows_ref
  42.9 1.8 collective-permute-start.10
  46.6 2.6 and_select_fusion
  52.1 2.2 maximum_select_fusion.2
  54.3 2.5 collective-permute-done.8.refs_9_
  56.8 1.9 collective-permute-done.10.refs_6_
  59.8 1.6 collective-permute-start.12
  61.5 9.2 %collective-permute-done.12.refs_10_ = bf16[8,64,512]{2,1,0:T(8,128)(2,1)S(1)} collective-permute-done((bf16[8,64,512]{2,1,0:T(8,128)(2,1)S(1)}, bf16[8,64,512]{2,1,0:T(8,128)(2,1)S(1)}, u32[]{:S(2)}, u32[]{:S(2)}) %collective-permute-start.12) | collective-permute-done | bytes 524320 | tf_op jit(solution)/shard_map/ppermute | solution.py:395
  80.1 4.9 %collect.3 = (bf16[16,64,512]{2,1,0:T(8,128)(2,1)S(1)}, bf16[40,64,512]{2,1,0:T(8,128)(2,1)S(1)}) custom-call(s32[56]{0:T(128)S(1)} %gather_fusion, s32[56]{0:T(128)S(1)} %gather_fusion.1, bf16[8,64,512]{2,1,0:T(8,128)(2,1)S(1)} %copy-done.27, bf16[8,64,512]{2,1,0:T(8,128)(2,1)S(1)} %copy-done.14, bf16[8,64,512]{2,1,0:T(8,128)(2,1)S(1)} %copy-done.18, ...), custom_call_target="tpu_custom_call" | custom-call | bytes 7340032 | tf_op jit(solution)/shard_map/collect/pallas_call | solution.py:466
  89.7 2.5 collective-permute-done.16.away_ref
  92.2 6.2 %attend.4 = (bf16[512,512]{1,0:T(8,128)(2,1)S(1)}, bf16[4,512,1024]{2,1,0:T(8,128)(2,1)}, f32[512,128]{1,0:T(8,128)S(1)}, bf16[512,256]{1,0:T(8,128)(2,1)S(1)}, bf16[512,256]{1,0:T(8,128)(2,1)S(1)}) custom-call(bf16[512,512]{1,0:T(8,128)(2,1)S(1)} %maximum_select_fusion.rows_ref, bf16[2,512,256]{2,1,0:T(8,128)(2,1)S(1)} %pad_maximum_fusion.3.pair_ref, ...), custom_call_target="tpu_custom_call" | custom-call | flops 1073741824 | bytes 9441280 | tf_op jit(solution)/shard_map/attend/pallas_call | solution.py:546
  101.0 6.6 %attend.3 = (bf16[512,512]{1,0:T(8,128)(2,1)}, bf16[4,512,1024]{2,1,0:T(8,128)(2,1)}, f32[512,128]{1,0:T(8,128)S(1)}, bf16[512,256]{1,0:T(8,128)(2,1)S(1)}, bf16[512,256]{1,0:T(8,128)(2,1)S(1)}) custom-call(bf16[512,512]{1,0:T(8,128)(2,1)S(1)} %copy-done.3, bf16[2,512,256]{2,1,0:T(8,128)(2,1)S(1)} %pad_maximum_fusion.2.pair_ref, ...), custom_call_target="tpu_custom_call" | custom-call | flops 1073741824 | bytes 9181184 | tf_op jit(solution)/shard_map/attend/pallas_call | solution.py:546
  109.2 5.4 %collective-permute-done.17 = bf16[512,512]{1,0:T(8,128)(2,1)S(1)} collective-permute-done((bf16[512,512]{1,0:T(8,128)(2,1)S(1)}, bf16[512,512]{1,0:T(8,128)(2,1)S(1)}, u32[]{:S(2)}, u32[]{:S(2)}) %collective-permute-start.17) | collective-permute-done | bytes 524320 | tf_op jit(solution)/shard_map/ppermute | solution.py:346
  115.8 2.7 feed.2
  121.7 4.2 collective-permute-done.15
  125.9 1.6 fusion.134
  127.6 8.7 %collective-permute-done.19 = bf16[512,512]{1,0:T(8,128)(2,1)} collective-permute-done((bf16[512,512]{1,0:T(8,128)(2,1)}, bf16[512,512]{1,0:T(8,128)(2,1)}, u32[]{:S(2)}, u32[]{:S(2)}) %collective-permute-start.19) | collective-permute-done | bytes 524320 | tf_op jit(solution)/shard_map/ppermute | solution.py:346
  136.3 1.6 fusion.132
  141.3 6.4 %attend.5 = (bf16[512,512]{1,0:T(8,128)(2,1)}, bf16[4,512,1024]{2,1,0:T(8,128)(2,1)}, f32[512,128]{1,0:T(8,128)S(1)}, bf16[512,256]{1,0:T(8,128)(2,1)S(1)}, bf16[512,256]{1,0:T(8,128)(2,1)S(1)}) custom-call(bf16[512,512]{1,0:T(8,128)(2,1)S(1)} %fusion.21.rows_ref, bf16[2,512,256]{2,1,0:T(8,128)(2,1)S(1)} %pad_maximum_fusion.4.pair_ref, ...), custom_call_target="tpu_custom_call" | custom-call | flops 1073741824 | bytes 12587008 | tf_op jit(solution)/shard_map/attend/pallas_call | solution.py:546
  152.1 12.1 %collective-permute-done.21 = bf16[512,512]{1,0:T(8,128)(2,1)} collective-permute-done((bf16[512,512]{1,0:T(8,128)(2,1)}, bf16[512,512]{1,0:T(8,128)(2,1)}, u32[]{:S(2)}, u32[]{:S(2)}) %collective-permute-start.21) | collective-permute-done | bytes 524320 | tf_op jit(solution)/shard_map/ppermute | solution.py:346
  164.2 2.0 fusion.131
  167.9 1.9 feed.3
  170.9 12.2 %collective-permute-done.22 = bf16[512,512]{1,0:T(8,128)(2,1)S(1)} collective-permute-done((bf16[512,512]{1,0:T(8,128)(2,1)S(1)}, bf16[512,512]{1,0:T(8,128)(2,1)S(1)}, u32[]{:S(2)}, u32[]{:S(2)}) %collective-permute-start.22) | collective-permute-done | bytes 524320 | tf_op jit(solution)/shard_map/ppermute | solution.py:346
  184.1 2.1 fusion.129
  190.9 10.0 %collective-permute-done.23 = bf16[512,512]{1,0:T(8,128)(2,1)S(1)} collective-permute-done((bf16[512,512]{1,0:T(8,128)(2,1)S(1)}, bf16[512,512]{1,0:T(8,128)(2,1)S(1)}, u32[]{:S(2)}, u32[]{:S(2)}) %collective-permute-start.23) | collective-permute-done | bytes 524320 | tf_op jit(solution)/shard_map/ppermute | solution.py:346
  204.5 5.8 %attend_back.3 = (bf16[512,256]{1,0:T(8,128)(2,1)S(1)}, bf16[512,512]{1,0:T(8,128)(2,1)S(1)}, f32[512,512]{1,0:T(8,128)S(1)}, bf16[512,512]{1,0:T(8,128)(2,1)S(1)}) custom-call(bf16[512,512]{1,0:T(8,128)(2,1)S(1)} %add_convert_fusion.10.g_ref, bf16[4,512,1024]{2,1,0:T(8,128)(2,1)S(1)} %copy-done.23, f32[512,128]{1,0:T(8,128)S(1)} %copy-done.67, ...), custom_call_target="tpu_custom_call" | custom-call | flops 2147483648 | bytes 14155776 | tf_op jit(solution)/shard_map/attend_back/pallas_call | solution.py:546
  214.5 1.6 collective-permute-start.26
  216.3 11.9 %collective-permute-done.25 = bf16[512,512]{1,0:T(8,128)(2,1)S(1)} collective-permute-done((bf16[512,512]{1,0:T(8,128)(2,1)S(1)}, bf16[512,512]{1,0:T(8,128)(2,1)S(1)}, u32[]{:S(2)}, u32[]{:S(2)}) %collective-permute-start.25) | collective-permute-done | bytes 524320 | tf_op jit(solution)/shard_map/ppermute | solution.py:346
  233.4 5.6 %collective-permute-done.26 = bf16[512,512]{1,0:T(8,128)(2,1)S(1)} collective-permute-done((bf16[512,512]{1,0:T(8,128)(2,1)S(1)}, bf16[512,512]{1,0:T(8,128)(2,1)S(1)}, u32[]{:S(2)}, u32[]{:S(2)}) %collective-permute-start.26) | collective-permute-done | bytes 524320 | tf_op jit(solution)/shard_map/ppermute | solution.py:346
  243.8 6.0 %attend_back.4 = (bf16[512,256]{1,0:T(8,128)(2,1)S(1)}, f32[512,512]{1,0:T(8,128)S(1)}, f32[512,512]{1,0:T(8,128)S(1)}, bf16[512,512]{1,0:T(8,128)(2,1)S(1)}) custom-call(bf16[512,512]{1,0:T(8,128)(2,1)S(1)} %get-tuple-element.265.g_ref, bf16[4,512,1024]{2,1,0:T(8,128)(2,1)S(1)} %copy-done.25, f32[512,128]{1,0:T(8,128)S(1)} %copy-done.63, ...), custom_call_target="tpu_custom_call" | custom-call | flops 2147483648 | bytes 11534336 | tf_op jit(solution)/shard_map/attend_back/pallas_call | solution.py:546
  263.2 6.3 %attend_back.5 = (bf16[512,256]{1,0:T(8,128)(2,1)S(1)}, f32[512,512]{1,0:T(8,128)S(1)}, f32[512,512]{1,0:T(8,128)S(1)}, bf16[512,512]{1,0:T(8,128)(2,1)}) custom-call(bf16[512,512]{1,0:T(8,128)(2,1)S(1)} %get-tuple-element.260.g_ref, bf16[4,512,1024]{2,1,0:T(8,128)(2,1)S(1)} %copy-done.24, f32[512,128]{1,0:T(8,128)S(1)} %copy-done.59, ...), custom_call_target="tpu_custom_call" | custom-call | flops 2147483648 | bytes 11534336 | tf_op jit(solution)/shard_map/attend_back/pallas_call | solution.py:546
  279.9 1.6 fusion
  283.3 1.9 collect.5
  290.2 1.9 collect.4
  292.1 7.9 %collective-permute-done.39 = bf16[8,64,512]{2,1,0:T(8,128)(2,1)S(1)} collective-permute-done((bf16[8,64,512]{2,1,0:T(8,128)(2,1)S(1)}, bf16[8,64,512]{2,1,0:T(8,128)(2,1)S(1)}, u32[]{:S(2)}, u32[]{:S(2)}) %collective-permute-start.39) | collective-permute-done | bytes 524320 | tf_op jit(solution)/shard_map/ppermute | solution.py:395
  300.2 5.2 %collective-permute-start.40 = (bf16[8,64,512]{2,1,0:T(8,128)(2,1)S(1)}, bf16[8,64,512]{2,1,0:T(8,128)(2,1)S(1)}, u32[]{:S(2)}, u32[]{:S(2)}) collective-permute-start(bf16[8,64,512]{2,1,0:T(8,128)(2,1)S(1)} %fusion.20), channel_id=1, source_target_pairs={{0,8},{4,12},{1,9},{5,13},{2,10},{6,14},{3,11},{7,15}} | collective-permute-start | bytes 1572872 | tf_op jit(solution)/shard_map/ppermute | solution.py:395
  307.2 9.5 %collective-permute-done.49 = f32[2,5,512]{2,1,0:T(8,128)S(1)} collective-permute-done((f32[2,5,512]{2,1,0:T(8,128)S(1)}, f32[2,5,512]{2,1,0:T(8,128)S(1)}, u32[]{:S(2)}, u32[]{:S(2)}) %collective-permute-start.49) | collective-permute-done | bytes 20512 | tf_op jit(solution)/shard_map/ppermute | solution.py:389
  316.7 4.4 %collective-permute-start.50 = (f32[2,5,512]{2,1,0:T(8,128)S(1)}, f32[2,5,512]{2,1,0:T(8,128)S(1)}, u32[]{:S(2)}, u32[]{:S(2)}) collective-permute-start(f32[2,5,512]{2,1,0:T(8,128)S(1)} %add.653), channel_id=1, source_target_pairs={{0,16},{4,20},{8,24},{12,28},{16,0},{20,4},{24,8},{28,12},{1,17},{... | collective-permute-start | bytes 61448 | tf_op jit(solution)/shard_map/ppermute | solution.py:389
  321.4 1.6 collective-permute-start.42
  326.1 7.2 %collective-permute-done.42 = bf16[8,64,512]{2,1,0:T(8,128)(2,1)S(1)} collective-permute-done((bf16[8,64,512]{2,1,0:T(8,128)(2,1)S(1)}, bf16[8,64,512]{2,1,0:T(8,128)(2,1)S(1)}, u32[]{:S(2)}, u32[]{:S(2)}) %collective-permute-start.42) | collective-permute-done | bytes 524320 | tf_op jit(solution)/shard_map/ppermute | solution.py:395
  336.3 5.8 %collective-permute-start.45 = (bf16[8,64,512]{2,1,0:T(8,128)(2,1)S(1)}, bf16[8,64,512]{2,1,0:T(8,128)(2,1)S(1)}, u32[]{:S(2)}, u32[]{:S(2)}) collective-permute-start(bf16[8,64,512]{2,1,0:T(8,128)(2,1)S(1)} %get-tuple-element.296), channel_id=1, source_target_pairs={{0,8},{4,12},{8,16},{12,20},{16,24},{20,28},{1,9},{5,13},{9,17},{1... | collective-permute-start | bytes 1572872 | tf_op jit(solution)/shard_map/ppermute | solution.py:395
  347.4 2.9 collective-permute-done.45
  350.3 4.2 collective-permute-done.46
  355.6 70.8 %after.1 = (f32[8,64,512]{2,1,0:T(8,128)}, f32[8,64,512]{2,1,0:T(8,128)}, f32[8,64,512]{2,1,0:T(8,128)}, f32[8,64,64]{2,1,0:T(8,128)}, f32[8,512,512]{2,1,0:T(8,...) custom-call(bf16[8,64,512]{2,1,0:T(8,128)(2,1)} %add_convert_fusion.g_ref, ...), custom_call_target="tpu_custom_call" | custom-call | flops 12884901888 | bytes 50331648 | tf_op jit(solution)/shard_map/after/pallas_call | solution.py:300
  (480 shorter events, 119.7 us)
Async XLA Ops:
  2.0 21.4 %collective-permute-start = (bf16[8,64,512]{2,1,0:T(8,128)(2,1)S(1)}, bf16[8,64,512]{2,1,0:T(8,128)(2,1)S(1)}, u32[]{:S(2)}, u32[]{:S(2)}) collective-permute-start(bf16[8,64,512]{2,1,0:T(8,128)(2,1)S(1)} %bitcast_convert_fusion.refs_0_), channel_id=1, source_target_pairs={{0,4},{4,0},{8,12},{12,8},{16,20},{20,16},{24,28},{28,24},{1,5},{5... | collective-permute-start | bytes 1572872 | tf_op jit(solution)/shard_map/ppermute | solution.py:395
  5.0 19.2 %collective-permute-start.1 = (bf16[8,64,512]{2,1,0:T(8,128)(2,1)S(1)}, bf16[8,64,512]{2,1,0:T(8,128)(2,1)S(1)}, u32[]{:S(2)}, u32[]{:S(2)}) collective-permute-start(bf16[8,64,512]{2,1,0:T(8,128)(2,1)S(1)} %bitcast_convert_fusion.refs_0_), channel_id=1, source_target_pairs={{0,8},{4,12},{8,16},{12,20},{16,24},{20,28},{1,9},{5,13},{9,17},{1... | collective-permute-start | bytes 1572872 | tf_op jit(solution)/shard_map/ppermute | solution.py:395
  8.5 15.6 %collective-permute-start.2 = (bf16[8,64,512]{2,1,0:T(8,128)(2,1)S(1)}, bf16[8,64,512]{2,1,0:T(8,128)(2,1)S(1)}, u32[]{:S(2)}, u32[]{:S(2)}) collective-permute-start(bf16[8,64,512]{2,1,0:T(8,128)(2,1)S(1)} %bitcast_convert_fusion.refs_0_), channel_id=1, source_target_pairs={{8,0},{12,4},{16,8},{20,12},{24,16},{28,20},{9,1},{13,5},{17,9},{2... | collective-permute-start | bytes 1572872 | tf_op jit(solution)/shard_map/ppermute | solution.py:395
  9.8 11.7 %collective-permute-start.3 = (bf16[256,512]{1,0:T(8,128)(2,1)}, bf16[256,512]{1,0:T(8,128)(2,1)S(1)}, u32[]{:S(2)}, u32[]{:S(2)}) collective-permute-start(bf16[256,512]{1,0:T(8,128)(2,1)} %bitcast.219), channel_id=1, source_target_pairs={{0,2},{1,3},{2,0},{3,1},{4,6},{5,7},{6,4},{7,5},{8,10},{9,11},{10,... | collective-permute-start | bytes 786440 | tf_op jit(solution)/shard_map/ppermute | solution.py:346
  11.4 26.7 %collective-permute-start.7 = (bf16[256,512]{1,0:T(8,128)(2,1)}, bf16[256,512]{1,0:T(8,128)(2,1)}, u32[]{:S(2)}, u32[]{:S(2)}) collective-permute-start(bf16[256,512]{1,0:T(8,128)(2,1)} %bitcast.221), channel_id=1, source_target_pairs={{0,2},{1,3},{2,0},{3,1},{4,6},{5,7},{6,4},{7,5},{8,10},{9,11},{10,... | collective-permute-start | bytes 786440 | tf_op jit(solution)/shard_map/ppermute | solution.py:346
  21.5 30.6 %collective-permute-start.11 = (bf16[256,512]{1,0:T(8,128)(2,1)}, bf16[256,512]{1,0:T(8,128)(2,1)}, u32[]{:S(2)}, u32[]{:S(2)}) collective-permute-start(bf16[256,512]{1,0:T(8,128)(2,1)} %bitcast.13), channel_id=1, source_target_pairs={{0,2},{1,3},{2,0},{3,1},{4,6},{5,7},{6,4},{7,5},{8,10},{9,11},{10,... | collective-permute-start | bytes 786440 | tf_op jit(solution)/shard_map/ppermute | solution.py:346
  24.2 16.7 %collective-permute-start.5 = (bf16[8,64,512]{2,1,0:T(8,128)(2,1)S(1)}, bf16[8,64,512]{2,1,0:T(8,128)(2,1)S(1)}, u32[]{:S(2)}, u32[]{:S(2)}) collective-permute-start(bf16[8,64,512]{2,1,0:T(8,128)(2,1)S(1)} %collective-permute-done.1.refs_1_), channel_id=1, source_target_pairs={{8,16},{12,20},{16,24},{20,28},{9,17},{13,21},{17,25},{21,29},{10,... | collective-permute-start | bytes 1572872 | tf_op jit(solution)/shard_map/ppermute | solution.py:395
  24.9 17.3 %collective-permute-start.6 = (bf16[8,64,512]{2,1,0:T(8,128)(2,1)S(1)}, bf16[8,64,512]{2,1,0:T(8,128)(2,1)S(1)}, u32[]{:S(2)}, u32[]{:S(2)}) collective-permute-start(bf16[8,64,512]{2,1,0:T(8,128)(2,1)S(1)} %collective-permute-done.2.refs_4_), channel_id=1, source_target_pairs={{8,0},{12,4},{16,8},{20,12},{9,1},{13,5},{17,9},{21,13},{10,2},{14... | collective-permute-start | bytes 1572872 | tf_op jit(solution)/shard_map/ppermute | solution.py:395
  27.0 13.0 %collective-permute-start.4 = (bf16[8,64,512]{2,1,0:T(8,128)(2,1)}, bf16[8,64,512]{2,1,0:T(8,128)(2,1)S(1)}, u32[]{:S(2)}, u32[]{:S(2)}) collective-permute-start(bf16[8,64,512]{2,1,0:T(8,128)(2,1)} %broadcast_select_fusion), channel_id=1, source_target_pairs={{0,4},{4,0},{8,12},{12,8},{16,20},{20,16},{24,28},{28,24},{1,5},{5... | collective-permute-start | bytes 1572872 | tf_op jit(solution)/shard_map/ppermute | solution.py:395
  42.2 14.6 %collective-permute-start.9 = (bf16[8,64,512]{2,1,0:T(8,128)(2,1)S(1)}, bf16[8,64,512]{2,1,0:T(8,128)(2,1)S(1)}, u32[]{:S(2)}, u32[]{:S(2)}) collective-permute-start(bf16[8,64,512]{2,1,0:T(8,128)(2,1)S(1)} %collective-permute-done.5.refs_2_), channel_id=1, source_target_pairs={{16,24},{20,28},{17,25},{21,29},{18,26},{22,30},{19,27},{23,31}} | collective-permute-start | bytes 1572872 | tf_op jit(solution)/shard_map/ppermute | solution.py:395
  42.9 15.8 %collective-permute-start.10 = (bf16[8,64,512]{2,1,0:T(8,128)(2,1)S(1)}, bf16[8,64,512]{2,1,0:T(8,128)(2,1)}, u32[]{:S(2)}, u32[]{:S(2)}) collective-permute-start(bf16[8,64,512]{2,1,0:T(8,128)(2,1)S(1)} %collective-permute-done.6.refs_5_), channel_id=1, source_target_pairs={{8,0},{12,4},{9,1},{13,5},{10,2},{14,6},{11,3},{15,7}} | collective-permute-start | bytes 1572872 | tf_op jit(solution)/shard_map/ppermute | solution.py:395
  45.5 11.3 %collective-permute-start.8 = (bf16[8,64,512]{2,1,0:T(8,128)(2,1)}, bf16[8,64,512]{2,1,0:T(8,128)(2,1)S(1)}, u32[]{:S(2)}, u32[]{:S(2)}) collective-permute-start(bf16[8,64,512]{2,1,0:T(8,128)(2,1)} %select_select_fusion.1), channel_id=1, source_target_pairs={{0,4},{4,0},{8,12},{12,8},{16,20},{20,16},{24,28},{28,24},{1,5},{5... | collective-permute-start | bytes 1572872 | tf_op jit(solution)/shard_map/ppermute | solution.py:395
  59.8 10.8 %collective-permute-start.12 = (bf16[8,64,512]{2,1,0:T(8,128)(2,1)S(1)}, bf16[8,64,512]{2,1,0:T(8,128)(2,1)S(1)}, u32[]{:S(2)}, u32[]{:S(2)}) collective-permute-start(bf16[8,64,512]{2,1,0:T(8,128)(2,1)S(1)} %select_select_fusion), channel_id=1, source_target_pairs={{0,4},{4,0},{8,12},{12,8},{16,20},{20,16},{24,28},{28,24},{1,5},{5... | collective-permute-start | bytes 1572872 | tf_op jit(solution)/shard_map/ppermute | solution.py:395
  85.0 2.7 collective-permute-start.13
  85.6 30.3 %collective-permute-start.18 = (bf16[40,64,512]{2,1,0:T(8,128)(2,1)S(1)}, bf16[40,64,512]{2,1,0:T(8,128)(2,1)S(1)}, u32[]{:S(2)}, u32[]{:S(2)}) collective-permute-start(bf16[40,64,512]{2,1,0:T(8,128)(2,1)S(1)} %get-tuple-element.123.own_in.own_out.own_ref), channel_id=1, source_target_pairs={{0,1},{1,0},{2,3},{3,2},{4,5},{5,4},{6,7},{7,6},{8,9},{9,8},{10,11... | collective-permute-start | bytes 7864328 | tf_op jit(solution)/shard_map/ppermute | solution.py:333
  88.2 4.0 collective-permute-start.16
  89.2 11.7 %collective-permute-start.14 = (bf16[2,512,256]{2,1,0:T(8,128)(2,1)S(1)}, bf16[2,512,256]{2,1,0:T(8,128)(2,1)S(1)}, u32[]{:S(2)}, u32[]{:S(2)}) collective-permute-start(bf16[2,512,256]{2,1,0:T(8,128)(2,1)S(1)} %pad_maximum_fusion.2.pair_ref), channel_id=1, source_target_pairs={{0,1},{1,0},{2,3},{3,2},{4,5},{5,4},{6,7},{7,6},{8,9},{9,8},{10,11... | collective-permute-start | bytes 1572872 | tf_op jit(solution)/shard_map/ppermute | solution.py:333
  99.8 14.8 %collective-permute-start.17 = (bf16[512,512]{1,0:T(8,128)(2,1)S(1)}, bf16[512,512]{1,0:T(8,128)(2,1)S(1)}, u32[]{:S(2)}, u32[]{:S(2)}) collective-permute-start(bf16[512,512]{1,0:T(8,128)(2,1)S(1)} %get-tuple-element.122), channel_id=1, source_target_pairs={{0,2},{1,3},{2,0},{3,1},{4,6},{5,7},{6,4},{7,5},{8,10},{9,11},{10,... | collective-permute-start | bytes 1572872 | tf_op jit(solution)/shard_map/ppermute | solution.py:346
  107.6 18.3 %collective-permute-start.15 = (bf16[512,512]{1,0:T(8,128)(2,1)}, bf16[512,512]{1,0:T(8,128)(2,1)}, u32[]{:S(2)}, u32[]{:S(2)}) collective-permute-start(bf16[512,512]{1,0:T(8,128)(2,1)} %get-tuple-element.120), channel_id=1, source_target_pairs={{0,2},{1,3},{2,0},{3,1},{4,6},{5,7},{6,4},{7,5},{8,10},{9,11},{10,... | collective-permute-start | bytes 1572872 | tf_op jit(solution)/shard_map/ppermute | solution.py:346
  120.5 15.9 %collective-permute-start.19 = (bf16[512,512]{1,0:T(8,128)(2,1)}, bf16[512,512]{1,0:T(8,128)(2,1)}, u32[]{:S(2)}, u32[]{:S(2)}) collective-permute-start(bf16[512,512]{1,0:T(8,128)(2,1)} %get-tuple-element.124), channel_id=1, source_target_pairs={{0,2},{1,3},{2,0},{3,1},{4,6},{5,7},{6,4},{7,5},{8,10},{9,11},{10,... | collective-permute-start | bytes 1572872 | tf_op jit(solution)/shard_map/ppermute | solution.py:346
  149.9 14.3 %collective-permute-start.21 = (bf16[512,512]{1,0:T(8,128)(2,1)}, bf16[512,512]{1,0:T(8,128)(2,1)}, u32[]{:S(2)}, u32[]{:S(2)}) collective-permute-start(bf16[512,512]{1,0:T(8,128)(2,1)} %get-tuple-element.125), channel_id=1, source_target_pairs={{0,2},{1,3},{2,0},{3,1},{4,6},{5,7},{6,4},{7,5},{8,10},{9,11},{10,... | collective-permute-start | bytes 1572872 | tf_op jit(solution)/shard_map/ppermute | solution.py:346
  169.8 13.2 %collective-permute-start.22 = (bf16[512,512]{1,0:T(8,128)(2,1)S(1)}, bf16[512,512]{1,0:T(8,128)(2,1)S(1)}, u32[]{:S(2)}, u32[]{:S(2)}) collective-permute-start(bf16[512,512]{1,0:T(8,128)(2,1)S(1)} %get-tuple-element.126), channel_id=1, source_target_pairs={{0,2},{1,3},{2,0},{3,1},{4,6},{5,7},{6,4},{7,5},{8,10},{9,11},{10,... | collective-permute-start | bytes 1572872 | tf_op jit(solution)/shard_map/ppermute | solution.py:346
  188.7 12.3 %collective-permute-start.23 = (bf16[512,512]{1,0:T(8,128)(2,1)S(1)}, bf16[512,512]{1,0:T(8,128)(2,1)S(1)}, u32[]{:S(2)}, u32[]{:S(2)}) collective-permute-start(bf16[512,512]{1,0:T(8,128)(2,1)S(1)} %fusion.6), channel_id=1, source_target_pairs={{0,2},{1,3},{2,0},{3,1},{4,6},{5,7},{6,4},{7,5},{8,10},{9,11},{10,... | collective-permute-start | bytes 1572872 | tf_op jit(solution)/shard_map/ppermute | solution.py:346
  189.8 21.6 %collective-permute-start.36 = (bf16[1024,512]{1,0:T(8,128)(2,1)S(1)}, bf16[1024,512]{1,0:T(8,128)(2,1)S(1)}, u32[]{:S(2)}, u32[]{:S(2)}) collective-permute-start(bf16[1024,512]{1,0:T(8,128)(2,1)S(1)} %pad_maximum_fusion.1), channel_id=1, source_target_pairs={{0,1},{1,0},{2,3},{3,2},{4,5},{5,4},{6,7},{7,6},{8,9},{9,8},{10,11... | collective-permute-start | bytes 3145736 | tf_op jit(solution)/shard_map/ppermute | solution.py:333
  213.4 14.8 %collective-permute-start.25 = (bf16[512,512]{1,0:T(8,128)(2,1)S(1)}, bf16[512,512]{1,0:T(8,128)(2,1)S(1)}, u32[]{:S(2)}, u32[]{:S(2)}) collective-permute-start(bf16[512,512]{1,0:T(8,128)(2,1)S(1)} %fusion.4), channel_id=1, source_target_pairs={{0,2},{1,3},{2,0},{3,1},{4,6},{5,7},{6,4},{7,5},{8,10},{9,11},{10,... | collective-permute-start | bytes 1572872 | tf_op jit(solution)/shard_map/ppermute | solution.py:346
  214.5 24.4 %collective-permute-start.26 = (bf16[512,512]{1,0:T(8,128)(2,1)S(1)}, bf16[512,512]{1,0:T(8,128)(2,1)S(1)}, u32[]{:S(2)}, u32[]{:S(2)}) collective-permute-start(bf16[512,512]{1,0:T(8,128)(2,1)S(1)} %get-tuple-element.137), channel_id=1, source_target_pairs={{0,2},{1,3},{2,0},{3,1},{4,6},{5,7},{6,4},{7,5},{8,10},{9,11},{10,... | collective-permute-start | bytes 1572872 | tf_op jit(solution)/shard_map/ppermute | solution.py:346
  216.2 38.2 %collective-permute-start.35 = (bf16[512,512]{1,0:T(8,128)(2,1)S(1)}, bf16[512,512]{1,0:T(8,128)(2,1)S(1)}, u32[]{:S(2)}, u32[]{:S(2)}) collective-permute-start(bf16[512,512]{1,0:T(8,128)(2,1)S(1)} %pad_maximum_fusion.7), channel_id=1, source_target_pairs={{0,1},{1,0},{2,3},{3,2},{4,5},{5,4},{6,7},{7,6},{8,9},{9,8},{10,11... | collective-permute-start | bytes 1572872 | tf_op jit(solution)/shard_map/ppermute | solution.py:333
  242.5 16.0 %collective-permute-start.27 = (bf16[512,512]{1,0:T(8,128)(2,1)S(1)}, bf16[512,512]{1,0:T(8,128)(2,1)S(1)}, u32[]{:S(2)}, u32[]{:S(2)}) collective-permute-start(bf16[512,512]{1,0:T(8,128)(2,1)S(1)} %fusion.8), channel_id=1, source_target_pairs={{0,2},{1,3},{2,0},{3,1},{4,6},{5,7},{6,4},{7,5},{8,10},{9,11},{10,... | collective-permute-start | bytes 1572872 | tf_op jit(solution)/shard_map/ppermute | solution.py:346
  249.8 6.4 %collective-permute-start.28 = (bf16[512,512]{1,0:T(8,128)(2,1)S(1)}, bf16[512,512]{1,0:T(8,128)(2,1)S(1)}, u32[]{:S(2)}, u32[]{:S(2)}) collective-permute-start(bf16[512,512]{1,0:T(8,128)(2,1)S(1)} %get-tuple-element.146), channel_id=1, source_target_pairs={{0,1},{1,0},{2,3},{3,2},{4,5},{5,4},{6,7},{7,6},{8,9},{9,8},{10,11... | collective-permute-start | bytes 1572872 | tf_op jit(solution)/shard_map/ppermute | solution.py:333
  251.4 28.4 %collective-permute-start.33 = (bf16[1024,512]{1,0:T(8,128)(2,1)}, bf16[1024,512]{1,0:T(8,128)(2,1)}, u32[]{:S(2)}, u32[]{:S(2)}) collective-permute-start(bf16[1024,512]{1,0:T(8,128)(2,1)} %pad_maximum_fusion), channel_id=1, source_target_pairs={{0,1},{1,0},{2,3},{3,2},{4,5},{5,4},{6,7},{7,6},{8,9},{9,8},{10,11... | collective-permute-start | bytes 3145736 | tf_op jit(solution)/shard_map/ppermute | solution.py:333
  271.5 6.6 %collective-permute-start.29 = (bf16[512,512]{1,0:T(8,128)(2,1)}, bf16[512,512]{1,0:T(8,128)(2,1)}, u32[]{:S(2)}, u32[]{:S(2)}) collective-permute-start(bf16[512,512]{1,0:T(8,128)(2,1)} %get-tuple-element.154), channel_id=1, source_target_pairs={{0,1},{1,0},{2,3},{3,2},{4,5},{5,4},{6,7},{7,6},{8,9},{9,8},{10,11... | collective-permute-start | bytes 1572872 | tf_op jit(solution)/shard_map/ppermute | solution.py:333
  273.3 8.2 %collective-permute-start.34 = (bf16[512,512]{1,0:T(8,128)(2,1)}, bf16[512,512]{1,0:T(8,128)(2,1)}, u32[]{:S(2)}, u32[]{:S(2)}) collective-permute-start(bf16[512,512]{1,0:T(8,128)(2,1)} %pad_maximum_fusion.6), channel_id=1, source_target_pairs={{0,1},{1,0},{2,3},{3,2},{4,5},{5,4},{6,7},{7,6},{8,9},{9,8},{10,11... | collective-permute-start | bytes 1572872 | tf_op jit(solution)/shard_map/ppermute | solution.py:333
  279.8 3.3 collective-permute-start.32
  285.2 14.8 %collective-permute-start.39 = (bf16[8,64,512]{2,1,0:T(8,128)(2,1)S(1)}, bf16[8,64,512]{2,1,0:T(8,128)(2,1)S(1)}, u32[]{:S(2)}, u32[]{:S(2)}) collective-permute-start(bf16[8,64,512]{2,1,0:T(8,128)(2,1)S(1)} %get-tuple-element.172), channel_id=1, source_target_pairs={{0,4},{4,0},{8,12},{12,8},{16,20},{20,16},{24,28},{28,24},{1,5},{5... | collective-permute-start | bytes 1572872 | tf_op jit(solution)/shard_map/ppermute | solution.py:395
  288.1 18.0 %collective-permute-start.48 = (f32[2,5,512]{2,1,0:T(8,128)S(1)}, f32[2,5,512]{2,1,0:T(8,128)S(1)}, u32[]{:S(2)}, u32[]{:S(2)}) collective-permute-start(f32[2,5,512]{2,1,0:T(8,128)S(1)} %fusion.115), channel_id=1, source_target_pairs={{0,4},{4,0},{8,12},{12,8},{16,20},{20,16},{24,28},{28,24},{1,5},{5... | collective-permute-start | bytes 61448 | tf_op jit(solution)/shard_map/ppermute | solution.py:389
  288.7 32.7 %collective-permute-start.38 = (bf16[8,64,512]{2,1,0:T(8,128)(2,1)S(1)}, bf16[8,64,512]{2,1,0:T(8,128)(2,1)S(1)}, u32[]{:S(2)}, u32[]{:S(2)}) collective-permute-start(bf16[8,64,512]{2,1,0:T(8,128)(2,1)S(1)} %get-tuple-element.170), channel_id=1, source_target_pairs={{0,4},{4,0},{8,12},{12,8},{16,20},{20,16},{24,28},{28,24},{1,5},{5... | collective-permute-start | bytes 1572872 | tf_op jit(solution)/shard_map/ppermute | solution.py:395
  300.2 22.8 %collective-permute-start.40 = (bf16[8,64,512]{2,1,0:T(8,128)(2,1)S(1)}, bf16[8,64,512]{2,1,0:T(8,128)(2,1)S(1)}, u32[]{:S(2)}, u32[]{:S(2)}) collective-permute-start(bf16[8,64,512]{2,1,0:T(8,128)(2,1)S(1)} %fusion.20), channel_id=1, source_target_pairs={{0,8},{4,12},{1,9},{5,13},{2,10},{6,14},{3,11},{7,15}} | collective-permute-start | bytes 1572872 | tf_op jit(solution)/shard_map/ppermute | solution.py:395
  305.4 17.6 %collective-permute-start.41 = (bf16[8,64,512]{2,1,0:T(8,128)(2,1)S(1)}, bf16[8,64,512]{2,1,0:T(8,128)(2,1)S(1)}, u32[]{:S(2)}, u32[]{:S(2)}) collective-permute-start(bf16[8,64,512]{2,1,0:T(8,128)(2,1)S(1)} %fusion.20), channel_id=1, source_target_pairs={{24,16},{28,20},{25,17},{29,21},{26,18},{30,22},{27,19},{31,23}} | collective-permute-start | bytes 1572872 | tf_op jit(solution)/shard_map/ppermute | solution.py:395
  306.1 10.5 %collective-permute-start.49 = (f32[2,5,512]{2,1,0:T(8,128)S(1)}, f32[2,5,512]{2,1,0:T(8,128)S(1)}, u32[]{:S(2)}, u32[]{:S(2)}) collective-permute-start(f32[2,5,512]{2,1,0:T(8,128)S(1)} %fusion.205), channel_id=1, source_target_pairs={{0,8},{4,12},{8,0},{12,4},{16,24},{20,28},{24,16},{28,20},{1,9},{5... | collective-permute-start | bytes 61448 | tf_op jit(solution)/shard_map/ppermute | solution.py:389
  306.3 39.1 %collective-permute-start.31 = (bf16[256,512]{1,0:T(8,128)(2,1)S(1)}, bf16[256,512]{1,0:T(8,128)(2,1)S(1)}, u32[]{:S(2)}, u32[]{:S(2)}) collective-permute-start(bf16[256,512]{1,0:T(8,128)(2,1)S(1)} %select_convert_fusion), channel_id=1, source_target_pairs={{0,2},{1,3},{2,0},{3,1},{4,6},{5,7},{6,4},{7,5},{8,10},{9,11},{10,... | collective-permute-start | bytes 786440 | tf_op jit(solution)/shard_map/ppermute | solution.py:346
  316.7 25.5 %collective-permute-start.50 = (f32[2,5,512]{2,1,0:T(8,128)S(1)}, f32[2,5,512]{2,1,0:T(8,128)S(1)}, u32[]{:S(2)}, u32[]{:S(2)}) collective-permute-start(f32[2,5,512]{2,1,0:T(8,128)S(1)} %add.653), channel_id=1, source_target_pairs={{0,16},{4,20},{8,24},{12,28},{16,0},{20,4},{24,8},{28,12},{1,17},{... | collective-permute-start | bytes 61448 | tf_op jit(solution)/shard_map/ppermute | solution.py:389
  321.4 12.0 %collective-permute-start.42 = (bf16[8,64,512]{2,1,0:T(8,128)(2,1)S(1)}, bf16[8,64,512]{2,1,0:T(8,128)(2,1)S(1)}, u32[]{:S(2)}, u32[]{:S(2)}) collective-permute-start(bf16[8,64,512]{2,1,0:T(8,128)(2,1)S(1)} %get-tuple-element.175), channel_id=1, source_target_pairs={{0,4},{4,0},{8,12},{12,8},{16,20},{20,16},{24,28},{28,24},{1,5},{5... | collective-permute-start | bytes 1572872 | tf_op jit(solution)/shard_map/ppermute | solution.py:395
  323.5 10.7 %collective-permute-start.43 = (bf16[8,64,512]{2,1,0:T(8,128)(2,1)S(1)}, bf16[8,64,512]{2,1,0:T(8,128)(2,1)S(1)}, u32[]{:S(2)}, u32[]{:S(2)}) collective-permute-start(bf16[8,64,512]{2,1,0:T(8,128)(2,1)S(1)} %get-tuple-element.298), channel_id=1, source_target_pairs={{0,8},{4,12},{8,16},{12,20},{1,9},{5,13},{9,17},{13,21},{2,10},{6,... | collective-permute-start | bytes 1572872 | tf_op jit(solution)/shard_map/ppermute | solution.py:395
  325.0 10.7 %collective-permute-start.44 = (bf16[8,64,512]{2,1,0:T(8,128)(2,1)S(1)}, bf16[8,64,512]{2,1,0:T(8,128)(2,1)S(1)}, u32[]{:S(2)}, u32[]{:S(2)}) collective-permute-start(bf16[8,64,512]{2,1,0:T(8,128)(2,1)S(1)} %get-tuple-element.297), channel_id=1, source_target_pairs={{16,8},{20,12},{24,16},{28,20},{17,9},{21,13},{25,17},{29,21},{18,... | collective-permute-start | bytes 1572872 | tf_op jit(solution)/shard_map/ppermute | solution.py:395
  333.4 13.1 %collective-permute-start.30 = (bf16[256,512]{1,0:T(8,128)(2,1)S(1)}, bf16[256,512]{1,0:T(8,128)(2,1)S(1)}, u32[]{:S(2)}, u32[]{:S(2)}) collective-permute-start(bf16[256,512]{1,0:T(8,128)(2,1)S(1)} %select_convert_fusion.1), channel_id=1, source_target_pairs={{0,2},{1,3},{2,0},{3,1},{4,6},{5,7},{6,4},{7,5},{8,10},{9,11},{10,... | collective-permute-start | bytes 786440 | tf_op jit(solution)/shard_map/ppermute | solution.py:346
  334.2 13.2 %collective-permute-start.37 = (bf16[8,64,512]{2,1,0:T(8,128)(2,1)S(1)}, bf16[8,64,512]{2,1,0:T(8,128)(2,1)S(1)}, u32[]{:S(2)}, u32[]{:S(2)}) collective-permute-start(bf16[8,64,512]{2,1,0:T(8,128)(2,1)S(1)} %get-tuple-element.168), channel_id=1, source_target_pairs={{0,4},{4,0},{8,12},{12,8},{16,20},{20,16},{24,28},{28,24},{1,5},{5... | collective-permute-start | bytes 1572872 | tf_op jit(solution)/shard_map/ppermute | solution.py:395
  336.3 14.0 %collective-permute-start.45 = (bf16[8,64,512]{2,1,0:T(8,128)(2,1)S(1)}, bf16[8,64,512]{2,1,0:T(8,128)(2,1)S(1)}, u32[]{:S(2)}, u32[]{:S(2)}) collective-permute-start(bf16[8,64,512]{2,1,0:T(8,128)(2,1)S(1)} %get-tuple-element.296), channel_id=1, source_target_pairs={{0,8},{4,12},{8,16},{12,20},{16,24},{20,28},{1,9},{5,13},{9,17},{1... | collective-permute-start | bytes 1572872 | tf_op jit(solution)/shard_map/ppermute | solution.py:395
  342.2 12.3 %collective-permute-start.46 = (bf16[8,64,512]{2,1,0:T(8,128)(2,1)S(1)}, bf16[8,64,512]{2,1,0:T(8,128)(2,1)S(1)}, u32[]{:S(2)}, u32[]{:S(2)}) collective-permute-start(bf16[8,64,512]{2,1,0:T(8,128)(2,1)S(1)} %get-tuple-element.295), channel_id=1, source_target_pairs={{8,0},{12,4},{16,8},{20,12},{24,16},{28,20},{9,1},{13,5},{17,9},{2... | collective-permute-start | bytes 1572872 | tf_op jit(solution)/shard_map/ppermute | solution.py:395
  (121 other events, 727.6 us)

commit v5 on v4

--- a/solution.py
+++ b/solution.py
@@ -363,6 +363,15 @@
     return part.astype(F32)
 
 
+def other_chips(part):
+    part, got = part.astype(BF), None
+    for bit in chip_bits():
+        moved = swap_chip(part, bit).astype(F32)
+        got = moved if got is None else got + moved
+        part = part if bit == chip_bits()[-1] else (part.astype(F32) + moved).astype(BF)
+    return jnp.zeros(part.shape, F32) if got is None else got
+
+
 def own_rows(values):
     chips = lax.axis_size("tensor") // 2
     count = values.shape[0] // chips
@@ -893,17 +902,47 @@
     g_one, pull_three = jax.vjp(layer_norm, z_three, gains[2], shifts[2])
     g_one_b = g_one.astype(BF)
     branch_four, saved_four = attention(g_one_b, encoded_b, four, False)
-    z_four = g_one + sum_chips(branch_four)
-    g_two, pull_four = jax.vjp(layer_norm, z_four, gains[3], shifts[3])
-    g_two_b = g_two.astype(BF)
-    branch_five, saved_five = feeding(g_two_b, five)
-    z_five = g_two + sum_chips(branch_five)
-    normed, pull_five = jax.vjp(layer_norm, z_five, gains[4], shifts[4])
-    decoded = own_rows((normed * keep_rows).astype(BF))
-
-    grad_z_five, gain_five, shift_five = pull_five(cot.astype(F32) * keep_rows)
-    weights_five, rows_five = feeding_back(grad_z_five, saved_five, g_two_b, five)
-    grad_z_four, gain_four, shift_four = pull_four(grad_z_five + sum_chips(rows_five))
+    count = total_rows // 2
+    chunks = [slice(0, count), slice(count, total_rows)]
+    hold = lax.optimization_barrier
+    got_four = [other_chips(branch_four[at]) for at in chunks]
+    fours, rows_fives, saves, terms, got_fives = [], [], [], [], []
+    for k, at in enumerate(chunks):
+        if k:
+            got_four[k], terms[0] = hold((got_four[k], terms[0]))
+        total = branch_four[at].astype(F32) + got_four[k]
+        g_two, pull = jax.vjp(layer_norm, g_one[at] + total, gains[3], shifts[3])
+        g_two_b = g_two.astype(BF)
+        branch_five, saved_five = feeding(g_two_b, five)
+        fours.append((g_two, pull))
+        rows_fives.append(g_two_b)
+        saves.append(saved_five)
+        terms.append(branch_five)
+        got_fives.append(other_chips(branch_five))
+    got_fives[0], terms[1] = hold((got_fives[0], terms[1]))
+    normed, grads_five, parts_five, weights_fives, got_back = [], [], [], [], []
+    gain_five, shift_five = 0.0, 0.0
+    for k, at in enumerate(chunks):
+        if k:
+            got_fives[k], parts_five[0] = hold((got_fives[k], parts_five[0]))
+        total = terms[k].astype(F32) + got_fives[k]
+        values, pull = jax.vjp(layer_norm, fours[k][0] + total, gains[4], shifts[4])
+        normed.append(values)
+        grad, gain, shift = pull(cot[at].astype(F32) * keep_rows[at])
+        gain_five, shift_five = gain_five + gain, shift_five + shift
+        weights_term, part = feeding_back(grad, saves[k], rows_fives[k], five)
+        part = part.astype(BF)
+        grads_five.append(grad)
+        parts_five.append(part)
+        weights_fives.append(weights_term)
+        got_back.append(other_chips(part))
+    got_back[0], parts_five[1] = hold((got_back[0], parts_five[1]))
+    decoded = own_rows((jnp.concatenate(normed, axis=0) * keep_rows).astype(BF))
+    back_five = [part.astype(F32) + got for part, got in zip(parts_five, got_back)]
+    weights_five = [[p + q for p, q in zip(x, y)] for x, y in zip(*weights_fives)]
+    back_four = [fours[k][1](grads_five[k] + back_five[k]) for k in range(2)]
+    grad_z_four = jnp.concatenate([item[0] for item in back_four], axis=0)
+    gain_four, shift_four = (back_four[0][i] + back_four[1][i] for i in (1, 2))
     weights_four, query_four, key_four = attention_back(grad_z_four, saved_four, g_one_b, encoded_b, four, False)
     grad_encoded = sum_chips(key_four)
     query_four, weights_four = lax.optimization_barrier((query_four, weights_four))

time: 432 us -> 412 us (0.954)
  local copies, waits for them, and re-layouts: 35.2 us -> 19.4 us
  waiting for transfers between devices: 123 us -> 116 us
    unnamed x239 -> x91, local copies, waits for them, and re-layouts: 27 us -> 9.78 us
    ppermute x14 -> x17, waiting for transfers between devices: 70.1 us -> 53.5 us  [swap_chip(): return lax.ppermute(values, 'tensor', [(i, i ^ bit) for i in range(count)])]
    ppermute x20, waiting for transfers between devices: 37.2 us -> 47.9 us  [shift(): return lax.ppermute(values, axis, pairs)]
    ppermute x20, starting transfers between devices: 36.2 us -> 30.3 us  [shift(): return lax.ppermute(values, axis, pairs)]
    ppermute x14 -> x17, starting transfers between devices: 12.5 us -> 17.1 us  [swap_chip(): return lax.ppermute(values, 'tensor', [(i, i ^ bit) for i in range(count)])]
    reduce_sum x10 -> x13, other arithmetic: 9.93 us -> 5.78 us  [layer_norm(): center = values - jnp.mean(values, axis=-1, keepdims=True)]
    dot_general x46 -> x54, matrix products: 22.3 us -> 23.4 us  [mm(): return lax.dot_general(a, b, dims, preferred_element_type=F32)]
    pallas_call x8 -> x9, Pallas kernels: 41.9 us -> 42.5 us  [call(): pl.pallas_call(kernel, grid=grid, in_specs=in_specs, out_specs=out_specs,...]
  transfers between devices with their start and end apart: 51 -> 54, of which waited for: 22 -> 23; matrix products, arithmetic and copies ran while one was open for 15% -> 18% of each run, Pallas kernels for 13% -> 14%
where the time goes in v5:
time: 412 us; the launch traced here: 406 us
  Pallas kernels  142 us (34%)
  waiting for transfers between devices  116 us (28%)
  starting transfers between devices  55.2 us (13%)
  other arithmetic  46.2 us (11%)
  matrix products  23.4 us (6%)
  local copies, waits for them, and re-layouts  19.4 us (5%)
    pallas_call x1, Pallas kernels, after(): pl.pallas_call(after_kernel, grid=(n // per,), in_specs=[flat, flat, flat...  70.8 us
    ppermute x17, waiting for transfers between devices, swap_chip(): return lax.ppermute(values, 'tensor', [(i, i ^ bit) for i in range(count)])  53.5 us
    ppermute x20, waiting for transfers between devices, shift(): return lax.ppermute(values, axis, pairs)  47.9 us
    pallas_call x9, Pallas kernels, call(): pl.pallas_call(kernel, grid=grid, in_specs=in_specs, out_specs=out_specs,...  42.5 us
    ppermute x20, starting transfers between devices, shift(): return lax.ppermute(values, axis, pairs)  30.3 us
    dot_general x54, matrix products, mm(): return lax.dot_general(a, b, dims, preferred_element_type=F32)  23.4 us
    pallas_call x2, Pallas kernels, before(): pl.pallas_call(before_kernel, grid=(n,), in_specs=[take, take], out_specs...  19.4 us
    ppermute x17, starting transfers between devices, swap_chip(): return lax.ppermute(values, 'tensor', [(i, i ^ bit) for i in range(count)])  17.1 us
  transfers between devices with their start and end apart: 54, of which 23 were waited for; matrix products, arithmetic and copies ran while one was open for 18% of the time, Pallas kernels for 14%

profile of v5, /device:TPU:0, one launch (start us, length us, event | category | flops | bytes accessed | tf_op | source)
XLA Modules:
  0.0 406.0 jit_solution(10683807901809118105)
XLA Ops:
  2.0 3.0 collective-permute-start
  5.0 3.5 collective-permute-start.1
  9.8 1.6 collective-permute-start.3
  11.9 9.7 %before.2 = (f32[4,512,512]{2,1,0:T(8,128)}, f32[4,512,512]{2,1,0:T(8,128)}) custom-call(f32[8,512,512]{2,1,0:T(8,128)} %bitcast.286, f32[8,512,512]{2,1,0:T(8,128)} %bitcast.289), custom_call_target="tpu_custom_call" | custom-call | flops 6442450944 | bytes 16777216 | tf_op jit(solution)/shard_map/before/pallas_call | solution.py:73
  21.6 9.7 %before.3 = (f32[4,512,512]{2,1,0:T(8,128)}, f32[4,512,512]{2,1,0:T(8,128)}) custom-call(f32[8,512,512]{2,1,0:T(8,128)} %bitcast.287, f32[8,512,512]{2,1,0:T(8,128)} %bitcast.290), custom_call_target="tpu_custom_call" | custom-call | flops 6442450944 | bytes 16777216 | tf_op jit(solution)/shard_map/before/pallas_call | solution.py:73
  31.7 1.6 collective-permute-start.11
  40.2 9.6 %collective-permute-done.4.refs_8_ = bf16[8,64,512]{2,1,0:T(8,128)(2,1)} collective-permute-done((bf16[8,64,512]{2,1,0:T(8,128)(2,1)}, bf16[8,64,512]{2,1,0:T(8,128)(2,1)}, u32[]{:S(2)}, u32[]{:S(2)}) %collective-permute-start.4) | collective-permute-done | bytes 524320 | tf_op jit(solution)/shard_map/ppermute | solution.py:404
  49.7 2.5 collective-permute-done.6.refs_5_
  56.4 2.6 and_select_fusion
  62.7 2.2 maximum_select_fusion.2
  64.8 2.6 collective-permute-done.8.refs_9_
  67.4 2.1 select_select_fusion
  71.0 9.1 %collective-permute-done.12.refs_10_ = bf16[8,64,512]{2,1,0:T(8,128)(2,1)} collective-permute-done((bf16[8,64,512]{2,1,0:T(8,128)(2,1)}, bf16[8,64,512]{2,1,0:T(8,128)(2,1)}, u32[]{:S(2)}, u32[]{:S(2)}) %collective-permute-start.12) | collective-permute-done | bytes 524320 | tf_op jit(solution)/shard_map/ppermute | solution.py:404
  82.1 5.7 %collect.3 = (bf16[16,64,512]{2,1,0:T(8,128)(2,1)S(1)}, bf16[40,64,512]{2,1,0:T(8,128)(2,1)S(1)}) custom-call(s32[56]{0:T(128)S(1)} %gather_fusion, s32[56]{0:T(128)S(1)} %gather_fusion.1, bf16[8,64,512]{2,1,0:T(8,128)(2,1)S(1)} %copy-done.4, bf16[8,64,512]{2,1,0:T(8,128)(2,1)S(1)} %collective-permute-done.1.refs_1_, ...), custom_call_target="tpu_custom_call" | custom-call | bytes 7340032 | tf_op jit(solution)/shard_map/collect/pallas_call | solution.py:475
  92.5 2.6 collective-permute-done.16.away_ref
  95.1 6.2 %attend.4 = (bf16[512,512]{1,0:T(8,128)(2,1)S(1)}, bf16[4,512,1024]{2,1,0:T(8,128)(2,1)}, f32[512,128]{1,0:T(8,128)S(1)}, bf16[512,256]{1,0:T(8,128)(2,1)S(1)}, bf16[512,256]{1,0:T(8,128)(2,1)S(1)}) custom-call(bf16[512,512]{1,0:T(8,128)(2,1)S(1)} %maximum_select_fusion.rows_ref, bf16[2,512,256]{2,1,0:T(8,128)(2,1)S(1)} %pad_maximum_fusion.4.pair_ref, ...), custom_call_target="tpu_custom_call" | custom-call | flops 1073741824 | bytes 9441280 | tf_op jit(solution)/shard_map/attend/pallas_call | solution.py:555
  102.6 6.5 %attend.3 = (bf16[512,512]{1,0:T(8,128)(2,1)S(1)}, bf16[4,512,1024]{2,1,0:T(8,128)(2,1)}, f32[512,128]{1,0:T(8,128)S(1)}, bf16[512,256]{1,0:T(8,128)(2,1)S(1)}, bf16[512,256]{1,0:T(8,128)(2,1)S(1)}) custom-call(bf16[512,512]{1,0:T(8,128)(2,1)S(1)} %maximum_select_fusion.1.rows_ref, bf16[2,512,256]{2,1,0:T(8,128)(2,1)S(1)} %pad_maximum_fusion.3.pair_ref, ...), custom_call_target="tpu_custom_call" | custom-call | flops 1073741824 | bytes 9181184 | tf_op jit(solution)/shard_map/attend/pallas_call | solution.py:555
  110.5 5.6 %collective-permute-done.17 = bf16[512,512]{1,0:T(8,128)(2,1)S(1)} collective-permute-done((bf16[512,512]{1,0:T(8,128)(2,1)S(1)}, bf16[512,512]{1,0:T(8,128)(2,1)S(1)}, u32[]{:S(2)}, u32[]{:S(2)}) %collective-permute-start.17) | collective-permute-done | bytes 524320 | tf_op jit(solution)/shard_map/ppermute | solution.py:346
  116.9 2.0 feed.3
  120.7 6.6 %collective-permute-done.15 = bf16[512,512]{1,0:T(8,128)(2,1)S(1)} collective-permute-done((bf16[512,512]{1,0:T(8,128)(2,1)S(1)}, bf16[512,512]{1,0:T(8,128)(2,1)S(1)}, u32[]{:S(2)}, u32[]{:S(2)}) %collective-permute-start.15) | collective-permute-done | bytes 524320 | tf_op jit(solution)/shard_map/ppermute | solution.py:346
  127.6 10.1 %collective-permute-done.19 = bf16[512,512]{1,0:T(8,128)(2,1)S(1)} collective-permute-done((bf16[512,512]{1,0:T(8,128)(2,1)S(1)}, bf16[512,512]{1,0:T(8,128)(2,1)S(1)}, u32[]{:S(2)}, u32[]{:S(2)}) %collective-permute-start.19) | collective-permute-done | bytes 524320 | tf_op jit(solution)/shard_map/ppermute | solution.py:346
  141.4 6.6 %attend.5 = (bf16[512,512]{1,0:T(8,128)(2,1)S(1)}, bf16[4,512,1024]{2,1,0:T(8,128)(2,1)}, f32[512,128]{1,0:T(8,128)S(1)}, bf16[512,256]{1,0:T(8,128)(2,1)S(1)}, bf16[512,256]{1,0:T(8,128)(2,1)S(1)}) custom-call(bf16[512,512]{1,0:T(8,128)(2,1)S(1)} %get-tuple-element.320.rows_ref, bf16[2,512,256]{2,1,0:T(8,128)(2,1)S(1)} %pad_maximum_fusion.5.pair_ref, ...), custom_call_target="tpu_custom_call" | custom-call | flops 1073741824 | bytes 12587008 | tf_op jit(solution)/shard_map/attend/pallas_call | solution.py:555
  151.4 5.9 %collective-permute-done.21 = bf16[256,512]{1,0:T(8,128)(2,1)S(1)} collective-permute-done((bf16[256,512]{1,0:T(8,128)(2,1)S(1)}, bf16[256,512]{1,0:T(8,128)(2,1)S(1)}, u32[]{:S(2)}, u32[]{:S(2)}) %collective-permute-start.21) | collective-permute-done | bytes 262176 | tf_op jit(solution)/shard_map/ppermute | solution.py:346
  157.8 1.6 feed.4
  160.1 2.8 collective-permute-done.22
  163.5 1.6 feed.5
  165.8 3.0 collective-permute-done.23
  182.6 2.4 collective-permute-done.26
  186.7 1.6 copy-done
  188.3 5.7 %attend_back.3 = (bf16[512,256]{1,0:T(8,128)(2,1)S(1)}, bf16[512,512]{1,0:T(8,128)(2,1)S(1)}, f32[512,512]{1,0:T(8,128)S(1)}, bf16[512,512]{1,0:T(8,128)(2,1)S(1)}) custom-call(bf16[512,512]{1,0:T(8,128)(2,1)S(1)} %fusion.26.g_ref, bf16[4,512,1024]{2,1,0:T(8,128)(2,1)S(1)} %copy-done, f32[512,128]{1,0:T(8,128)S(1)} %get-tuple-element.151.inverse_ref, ...), custom_call_target="tpu_custom_call" | custom-call | flops 2147483648 | bytes 14155776 | tf_op jit(solution)/shard_map/attend_back/pallas_call | solution.py:555
  199.7 1.6 fusion.1
  201.3 10.3 %collective-permute-done.28 = bf16[512,512]{1,0:T(8,128)(2,1)S(1)} collective-permute-done((bf16[512,512]{1,0:T(8,128)(2,1)S(1)}, bf16[512,512]{1,0:T(8,128)(2,1)S(1)}, u32[]{:S(2)}, u32[]{:S(2)}) %collective-permute-start.28) | collective-permute-done | bytes 524320 | tf_op jit(solution)/shard_map/ppermute | solution.py:346
  216.3 6.2 %collective-permute-done.29 = bf16[512,512]{1,0:T(8,128)(2,1)S(1)} collective-permute-done((bf16[512,512]{1,0:T(8,128)(2,1)S(1)}, bf16[512,512]{1,0:T(8,128)(2,1)S(1)}, u32[]{:S(2)}, u32[]{:S(2)}) %collective-permute-start.29) | collective-permute-done | bytes 524320 | tf_op jit(solution)/shard_map/ppermute | solution.py:346
  227.1 5.9 %attend_back.4 = (bf16[512,256]{1,0:T(8,128)(2,1)S(1)}, f32[512,512]{1,0:T(8,128)S(1)}, f32[512,512]{1,0:T(8,128)S(1)}, bf16[512,512]{1,0:T(8,128)(2,1)S(1)}) custom-call(bf16[512,512]{1,0:T(8,128)(2,1)S(1)} %get-tuple-element.291.g_ref, bf16[4,512,1024]{2,1,0:T(8,128)(2,1)S(1)} %copy-done.2, f32[512,128]{1,0:T(8,128)S(1)} %get-tuple-element.163.inverse_ref, ...), custom_call_target="tpu_custom_call" | custom-call | flops 2147483648 | bytes 11534336 | tf_op jit(solution)/shard_map/attend_back/pallas_call | solution.py:555
  245.7 6.3 %attend_back.5 = (bf16[512,256]{1,0:T(8,128)(2,1)S(1)}, f32[512,512]{1,0:T(8,128)S(1)}, f32[512,512]{1,0:T(8,128)S(1)}, bf16[512,512]{1,0:T(8,128)(2,1)}) custom-call(bf16[512,512]{1,0:T(8,128)(2,1)S(1)} %get-tuple-element.286.g_ref, bf16[4,512,1024]{2,1,0:T(8,128)(2,1)S(1)} %copy-done.1, f32[512,128]{1,0:T(8,128)S(1)} %get-tuple-element.171.inverse_ref, ...), custom_call_target="tpu_custom_call" | custom-call | flops 2147483648 | bytes 11534336 | tf_op jit(solution)/shard_map/attend_back/pallas_call | solution.py:555
  262.0 1.6 fusion
  265.5 1.9 collect.5
  269.3 1.6 collective-permute-start.51
  271.4 1.9 collect.4
  273.3 8.9 %collective-permute-done.42 = bf16[8,64,512]{2,1,0:T(8,128)(2,1)S(1)} collective-permute-done((bf16[8,64,512]{2,1,0:T(8,128)(2,1)S(1)}, bf16[8,64,512]{2,1,0:T(8,128)(2,1)S(1)}, u32[]{:S(2)}, u32[]{:S(2)}) %collective-permute-start.42) | collective-permute-done | bytes 524320 | tf_op jit(solution)/shard_map/ppermute | solution.py:404
  282.4 4.8 %collective-permute-start.43 = (bf16[8,64,512]{2,1,0:T(8,128)(2,1)S(1)}, bf16[8,64,512]{2,1,0:T(8,128)(2,1)S(1)}, u32[]{:S(2)}, u32[]{:S(2)}) collective-permute-start(bf16[8,64,512]{2,1,0:T(8,128)(2,1)S(1)} %fusion.22), channel_id=1, source_target_pairs={{0,8},{4,12},{1,9},{5,13},{2,10},{6,14},{3,11},{7,15}} | collective-permute-start | bytes 1572872 | tf_op jit(solution)/shard_map/ppermute | solution.py:404
  289.5 8.8 %collective-permute-done.52 = f32[2,5,512]{2,1,0:T(8,128)S(1)} collective-permute-done((f32[2,5,512]{2,1,0:T(8,128)S(1)}, f32[2,5,512]{2,1,0:T(8,128)S(1)}, u32[]{:S(2)}, u32[]{:S(2)}) %collective-permute-start.52) | collective-permute-done | bytes 20512 | tf_op jit(solution)/shard_map/ppermute | solution.py:398
  298.4 3.2 collective-permute-start.53
  305.6 8.2 %collective-permute-done.45 = bf16[8,64,512]{2,1,0:T(8,128)(2,1)S(1)} collective-permute-done((bf16[8,64,512]{2,1,0:T(8,128)(2,1)S(1)}, bf16[8,64,512]{2,1,0:T(8,128)(2,1)S(1)}, u32[]{:S(2)}, u32[]{:S(2)}) %collective-permute-start.45) | collective-permute-done | bytes 524320 | tf_op jit(solution)/shard_map/ppermute | solution.py:404
  316.3 5.3 %collective-permute-start.48 = (bf16[8,64,512]{2,1,0:T(8,128)(2,1)S(1)}, bf16[8,64,512]{2,1,0:T(8,128)(2,1)S(1)}, u32[]{:S(2)}, u32[]{:S(2)}) collective-permute-start(bf16[8,64,512]{2,1,0:T(8,128)(2,1)S(1)} %get-tuple-element.333), channel_id=1, source_target_pairs={{0,8},{4,12},{8,16},{12,20},{16,24},{20,28},{1,9},{5,13},{9,17},{1... | collective-permute-start | bytes 1572872 | tf_op jit(solution)/shard_map/ppermute | solution.py:404
  326.8 2.8 collective-permute-done.48
  329.7 4.2 %collective-permute-done.49 = bf16[8,64,512]{2,1,0:T(8,128)(2,1)S(1)} collective-permute-done((bf16[8,64,512]{2,1,0:T(8,128)(2,1)S(1)}, bf16[8,64,512]{2,1,0:T(8,128)(2,1)S(1)}, u32[]{:S(2)}, u32[]{:S(2)}) %collective-permute-start.49) | collective-permute-done | bytes 524320 | tf_op jit(solution)/shard_map/ppermute | solution.py:404
  334.9 70.8 %after.1 = (f32[8,64,512]{2,1,0:T(8,128)}, f32[8,64,512]{2,1,0:T(8,128)}, f32[8,64,512]{2,1,0:T(8,128)}, f32[8,64,64]{2,1,0:T(8,128)}, f32[8,512,512]{2,1,0:T(8,...) custom-call(bf16[8,64,512]{2,1,0:T(8,128)(2,1)} %add_convert_fusion.g_ref, ...), custom_call_target="tpu_custom_call" | custom-call | flops 12884901888 | bytes 50331648 | tf_op jit(solution)/shard_map/after/pallas_call | solution.py:300
  (376 shorter events, 111.6 us)
Async XLA Ops:
  2.0 31.5 %collective-permute-start = (bf16[8,64,512]{2,1,0:T(8,128)(2,1)S(1)}, bf16[8,64,512]{2,1,0:T(8,128)(2,1)S(1)}, u32[]{:S(2)}, u32[]{:S(2)}) collective-permute-start(bf16[8,64,512]{2,1,0:T(8,128)(2,1)S(1)} %bitcast_convert_fusion.refs_0_), channel_id=1, source_target_pairs={{0,4},{4,0},{8,12},{12,8},{16,20},{20,16},{24,28},{28,24},{1,5},{5... | collective-permute-start | bytes 1572872 | tf_op jit(solution)/shard_map/ppermute | solution.py:404
  5.0 29.3 %collective-permute-start.1 = (bf16[8,64,512]{2,1,0:T(8,128)(2,1)S(1)}, bf16[8,64,512]{2,1,0:T(8,128)(2,1)S(1)}, u32[]{:S(2)}, u32[]{:S(2)}) collective-permute-start(bf16[8,64,512]{2,1,0:T(8,128)(2,1)S(1)} %bitcast_convert_fusion.refs_0_), channel_id=1, source_target_pairs={{0,8},{4,12},{8,16},{12,20},{16,24},{20,28},{1,9},{5,13},{9,17},{1... | collective-permute-start | bytes 1572872 | tf_op jit(solution)/shard_map/ppermute | solution.py:404
  8.5 25.8 %collective-permute-start.2 = (bf16[8,64,512]{2,1,0:T(8,128)(2,1)S(1)}, bf16[8,64,512]{2,1,0:T(8,128)(2,1)S(1)}, u32[]{:S(2)}, u32[]{:S(2)}) collective-permute-start(bf16[8,64,512]{2,1,0:T(8,128)(2,1)S(1)} %bitcast_convert_fusion.refs_0_), channel_id=1, source_target_pairs={{8,0},{12,4},{16,8},{20,12},{24,16},{28,20},{9,1},{13,5},{17,9},{2... | collective-permute-start | bytes 1572872 | tf_op jit(solution)/shard_map/ppermute | solution.py:404
  9.8 21.9 %collective-permute-start.3 = (bf16[256,512]{1,0:T(8,128)(2,1)}, bf16[256,512]{1,0:T(8,128)(2,1)S(1)}, u32[]{:S(2)}, u32[]{:S(2)}) collective-permute-start(bf16[256,512]{1,0:T(8,128)(2,1)} %bitcast.235), channel_id=1, source_target_pairs={{0,2},{1,3},{2,0},{3,1},{4,6},{5,7},{6,4},{7,5},{8,10},{9,11},{10,... | collective-permute-start | bytes 786440 | tf_op jit(solution)/shard_map/ppermute | solution.py:346
  11.4 27.6 %collective-permute-start.7 = (bf16[256,512]{1,0:T(8,128)(2,1)}, bf16[256,512]{1,0:T(8,128)(2,1)}, u32[]{:S(2)}, u32[]{:S(2)}) collective-permute-start(bf16[256,512]{1,0:T(8,128)(2,1)} %bitcast.237), channel_id=1, source_target_pairs={{0,2},{1,3},{2,0},{3,1},{4,6},{5,7},{6,4},{7,5},{8,10},{9,11},{10,... | collective-permute-start | bytes 786440 | tf_op jit(solution)/shard_map/ppermute | solution.py:346
  31.7 31.0 %collective-permute-start.11 = (bf16[256,512]{1,0:T(8,128)(2,1)}, bf16[256,512]{1,0:T(8,128)(2,1)}, u32[]{:S(2)}, u32[]{:S(2)}) collective-permute-start(bf16[256,512]{1,0:T(8,128)(2,1)} %bitcast.13), channel_id=1, source_target_pairs={{0,2},{1,3},{2,0},{3,1},{4,6},{5,7},{6,4},{7,5},{8,10},{9,11},{10,... | collective-permute-start | bytes 786440 | tf_op jit(solution)/shard_map/ppermute | solution.py:346
  34.3 15.4 %collective-permute-start.5 = (bf16[8,64,512]{2,1,0:T(8,128)(2,1)S(1)}, bf16[8,64,512]{2,1,0:T(8,128)(2,1)S(1)}, u32[]{:S(2)}, u32[]{:S(2)}) collective-permute-start(bf16[8,64,512]{2,1,0:T(8,128)(2,1)S(1)} %collective-permute-done.1.refs_1_), channel_id=1, source_target_pairs={{8,16},{12,20},{16,24},{20,28},{9,17},{13,21},{17,25},{21,29},{10,... | collective-permute-start | bytes 1572872 | tf_op jit(solution)/shard_map/ppermute | solution.py:404
  35.0 17.3 %collective-permute-start.6 = (bf16[8,64,512]{2,1,0:T(8,128)(2,1)S(1)}, bf16[8,64,512]{2,1,0:T(8,128)(2,1)S(1)}, u32[]{:S(2)}, u32[]{:S(2)}) collective-permute-start(bf16[8,64,512]{2,1,0:T(8,128)(2,1)S(1)} %collective-permute-done.2.refs_4_), channel_id=1, source_target_pairs={{8,0},{12,4},{16,8},{20,12},{9,1},{13,5},{17,9},{21,13},{10,2},{14... | collective-permute-start | bytes 1572872 | tf_op jit(solution)/shard_map/ppermute | solution.py:404
  37.2 12.6 %collective-permute-start.4 = (bf16[8,64,512]{2,1,0:T(8,128)(2,1)}, bf16[8,64,512]{2,1,0:T(8,128)(2,1)}, u32[]{:S(2)}, u32[]{:S(2)}) collective-permute-start(bf16[8,64,512]{2,1,0:T(8,128)(2,1)} %broadcast_select_fusion), channel_id=1, source_target_pairs={{0,4},{4,0},{8,12},{12,8},{16,20},{20,16},{24,28},{28,24},{1,5},{5... | collective-permute-start | bytes 1572872 | tf_op jit(solution)/shard_map/ppermute | solution.py:404
  52.3 15.1 %collective-permute-start.9 = (bf16[8,64,512]{2,1,0:T(8,128)(2,1)S(1)}, bf16[8,64,512]{2,1,0:T(8,128)(2,1)}, u32[]{:S(2)}, u32[]{:S(2)}) collective-permute-start(bf16[8,64,512]{2,1,0:T(8,128)(2,1)S(1)} %collective-permute-done.5.refs_2_), channel_id=1, source_target_pairs={{16,24},{20,28},{17,25},{21,29},{18,26},{22,30},{19,27},{23,31}} | collective-permute-start | bytes 1572872 | tf_op jit(solution)/shard_map/ppermute | solution.py:404
  53.7 13.7 %collective-permute-start.10 = (bf16[8,64,512]{2,1,0:T(8,128)(2,1)S(1)}, bf16[8,64,512]{2,1,0:T(8,128)(2,1)}, u32[]{:S(2)}, u32[]{:S(2)}) collective-permute-start(bf16[8,64,512]{2,1,0:T(8,128)(2,1)S(1)} %collective-permute-done.6.refs_5_), channel_id=1, source_target_pairs={{8,0},{12,4},{9,1},{13,5},{10,2},{14,6},{11,3},{15,7}} | collective-permute-start | bytes 1572872 | tf_op jit(solution)/shard_map/ppermute | solution.py:404
  55.9 11.5 %collective-permute-start.8 = (bf16[8,64,512]{2,1,0:T(8,128)(2,1)}, bf16[8,64,512]{2,1,0:T(8,128)(2,1)}, u32[]{:S(2)}, u32[]{:S(2)}) collective-permute-start(bf16[8,64,512]{2,1,0:T(8,128)(2,1)} %select_select_fusion.1), channel_id=1, source_target_pairs={{0,4},{4,0},{8,12},{12,8},{16,20},{20,16},{24,28},{28,24},{1,5},{5... | collective-permute-start | bytes 1572872 | tf_op jit(solution)/shard_map/ppermute | solution.py:404
  69.5 10.6 %collective-permute-start.12 = (bf16[8,64,512]{2,1,0:T(8,128)(2,1)}, bf16[8,64,512]{2,1,0:T(8,128)(2,1)}, u32[]{:S(2)}, u32[]{:S(2)}) collective-permute-start(bf16[8,64,512]{2,1,0:T(8,128)(2,1)} %select_select_fusion), channel_id=1, source_target_pairs={{0,4},{4,0},{8,12},{12,8},{16,20},{20,16},{24,28},{28,24},{1,5},{5... | collective-permute-start | bytes 1572872 | tf_op jit(solution)/shard_map/ppermute | solution.py:404
  88.3 28.6 %collective-permute-start.18 = (bf16[40,64,512]{2,1,0:T(8,128)(2,1)S(1)}, bf16[40,64,512]{2,1,0:T(8,128)(2,1)S(1)}, u32[]{:S(2)}, u32[]{:S(2)}) collective-permute-start(bf16[40,64,512]{2,1,0:T(8,128)(2,1)S(1)} %get-tuple-element.134.own_in.own_out.own_ref), channel_id=1, source_target_pairs={{0,1},{1,0},{2,3},{3,2},{4,5},{5,4},{6,7},{7,6},{8,9},{9,8},{10,11... | collective-permute-start | bytes 7864328 | tf_op jit(solution)/shard_map/ppermute | solution.py:333
  92.0 10.5 %collective-permute-start.14 = (bf16[2,512,256]{2,1,0:T(8,128)(2,1)S(1)}, bf16[2,512,256]{2,1,0:T(8,128)(2,1)S(1)}, u32[]{:S(2)}, u32[]{:S(2)}) collective-permute-start(bf16[2,512,256]{2,1,0:T(8,128)(2,1)S(1)} %pad_maximum_fusion.3.pair_ref), channel_id=1, source_target_pairs={{0,1},{1,0},{2,3},{3,2},{4,5},{5,4},{6,7},{7,6},{8,9},{9,8},{10,11... | collective-permute-start | bytes 1572872 | tf_op jit(solution)/shard_map/ppermute | solution.py:333
  101.3 14.8 %collective-permute-start.17 = (bf16[512,512]{1,0:T(8,128)(2,1)S(1)}, bf16[512,512]{1,0:T(8,128)(2,1)S(1)}, u32[]{:S(2)}, u32[]{:S(2)}) collective-permute-start(bf16[512,512]{1,0:T(8,128)(2,1)S(1)} %get-tuple-element.133), channel_id=1, source_target_pairs={{0,2},{1,3},{2,0},{3,1},{4,6},{5,7},{6,4},{7,5},{8,10},{9,11},{10,... | collective-permute-start | bytes 1572872 | tf_op jit(solution)/shard_map/ppermute | solution.py:346
  109.1 18.2 %collective-permute-start.15 = (bf16[512,512]{1,0:T(8,128)(2,1)S(1)}, bf16[512,512]{1,0:T(8,128)(2,1)S(1)}, u32[]{:S(2)}, u32[]{:S(2)}) collective-permute-start(bf16[512,512]{1,0:T(8,128)(2,1)S(1)} %get-tuple-element.131), channel_id=1, source_target_pairs={{0,2},{1,3},{2,0},{3,1},{4,6},{5,7},{6,4},{7,5},{8,10},{9,11},{10,... | collective-permute-start | bytes 1572872 | tf_op jit(solution)/shard_map/ppermute | solution.py:346
  118.9 18.9 %collective-permute-start.19 = (bf16[512,512]{1,0:T(8,128)(2,1)S(1)}, bf16[512,512]{1,0:T(8,128)(2,1)S(1)}, u32[]{:S(2)}, u32[]{:S(2)}) collective-permute-start(bf16[512,512]{1,0:T(8,128)(2,1)S(1)} %get-tuple-element.135), channel_id=1, source_target_pairs={{0,2},{1,3},{2,0},{3,1},{4,6},{5,7},{6,4},{7,5},{8,10},{9,11},{10,... | collective-permute-start | bytes 1572872 | tf_op jit(solution)/shard_map/ppermute | solution.py:346
  148.1 9.2 %collective-permute-start.21 = (bf16[256,512]{1,0:T(8,128)(2,1)S(1)}, bf16[256,512]{1,0:T(8,128)(2,1)S(1)}, u32[]{:S(2)}, u32[]{:S(2)}) collective-permute-start(bf16[256,512]{1,0:T(8,128)(2,1)S(1)} %get-tuple-element.342), channel_id=1, source_target_pairs={{0,2},{1,3},{2,0},{3,1},{4,6},{5,7},{6,4},{7,5},{8,10},{9,11},{10,... | collective-permute-start | bytes 786440 | tf_op jit(solution)/shard_map/ppermute | solution.py:346
  149.9 12.9 %collective-permute-start.22 = (bf16[256,512]{1,0:T(8,128)(2,1)S(1)}, bf16[256,512]{1,0:T(8,128)(2,1)S(1)}, u32[]{:S(2)}, u32[]{:S(2)}) collective-permute-start(bf16[256,512]{1,0:T(8,128)(2,1)S(1)} %get-tuple-element.343), channel_id=1, source_target_pairs={{0,2},{1,3},{2,0},{3,1},{4,6},{5,7},{6,4},{7,5},{8,10},{9,11},{10,... | collective-permute-start | bytes 786440 | tf_op jit(solution)/shard_map/ppermute | solution.py:346
  159.4 9.3 %collective-permute-start.23 = (bf16[256,512]{1,0:T(8,128)(2,1)S(1)}, bf16[256,512]{1,0:T(8,128)(2,1)S(1)}, u32[]{:S(2)}, u32[]{:S(2)}) collective-permute-start(bf16[256,512]{1,0:T(8,128)(2,1)S(1)} %get-tuple-element.138), channel_id=1, source_target_pairs={{0,2},{1,3},{2,0},{3,1},{4,6},{5,7},{6,4},{7,5},{8,10},{9,11},{10,... | collective-permute-start | bytes 786440 | tf_op jit(solution)/shard_map/ppermute | solution.py:346
  165.1 8.6 %collective-permute-start.24 = (bf16[256,512]{1,0:T(8,128)(2,1)S(1)}, bf16[256,512]{1,0:T(8,128)(2,1)S(1)}, u32[]{:S(2)}, u32[]{:S(2)}) collective-permute-start(bf16[256,512]{1,0:T(8,128)(2,1)S(1)} %get-tuple-element.142), channel_id=1, source_target_pairs={{0,2},{1,3},{2,0},{3,1},{4,6},{5,7},{6,4},{7,5},{8,10},{9,11},{10,... | collective-permute-start | bytes 786440 | tf_op jit(solution)/shard_map/ppermute | solution.py:346
  172.1 10.4 %collective-permute-start.25 = (bf16[256,512]{1,0:T(8,128)(2,1)S(1)}, bf16[256,512]{1,0:T(8,128)(2,1)S(1)}, u32[]{:S(2)}, u32[]{:S(2)}) collective-permute-start(bf16[256,512]{1,0:T(8,128)(2,1)S(1)} %fusion.10), channel_id=1, source_target_pairs={{0,2},{1,3},{2,0},{3,1},{4,6},{5,7},{6,4},{7,5},{8,10},{9,11},{10,... | collective-permute-start | bytes 786440 | tf_op jit(solution)/shard_map/ppermute | solution.py:346
  178.1 6.9 %collective-permute-start.26 = (bf16[256,512]{1,0:T(8,128)(2,1)S(1)}, bf16[256,512]{1,0:T(8,128)(2,1)S(1)}, u32[]{:S(2)}, u32[]{:S(2)}) collective-permute-start(bf16[256,512]{1,0:T(8,128)(2,1)S(1)} %fusion.12), channel_id=1, source_target_pairs={{0,2},{1,3},{2,0},{3,1},{4,6},{5,7},{6,4},{7,5},{8,10},{9,11},{10,... | collective-permute-start | bytes 786440 | tf_op jit(solution)/shard_map/ppermute | solution.py:346
  181.1 18.7 %collective-permute-start.39 = (bf16[1024,512]{1,0:T(8,128)(2,1)}, bf16[1024,512]{1,0:T(8,128)(2,1)}, u32[]{:S(2)}, u32[]{:S(2)}) collective-permute-start(bf16[1024,512]{1,0:T(8,128)(2,1)} %pad_maximum_fusion.2), channel_id=1, source_target_pairs={{0,1},{1,0},{2,3},{3,2},{4,5},{5,4},{6,7},{7,6},{8,9},{9,8},{10,11... | collective-permute-start | bytes 3145736 | tf_op jit(solution)/shard_map/ppermute | solution.py:333
  196.9 14.8 %collective-permute-start.28 = (bf16[512,512]{1,0:T(8,128)(2,1)S(1)}, bf16[512,512]{1,0:T(8,128)(2,1)S(1)}, u32[]{:S(2)}, u32[]{:S(2)}) collective-permute-start(bf16[512,512]{1,0:T(8,128)(2,1)S(1)} %fusion.4), channel_id=1, source_target_pairs={{0,2},{1,3},{2,0},{3,1},{4,6},{5,7},{6,4},{7,5},{8,10},{9,11},{10,... | collective-permute-start | bytes 1572872 | tf_op jit(solution)/shard_map/ppermute | solution.py:346
  198.1 24.4 %collective-permute-start.29 = (bf16[512,512]{1,0:T(8,128)(2,1)S(1)}, bf16[512,512]{1,0:T(8,128)(2,1)S(1)}, u32[]{:S(2)}, u32[]{:S(2)}) collective-permute-start(bf16[512,512]{1,0:T(8,128)(2,1)S(1)} %get-tuple-element.158), channel_id=1, source_target_pairs={{0,2},{1,3},{2,0},{3,1},{4,6},{5,7},{6,4},{7,5},{8,10},{9,11},{10,... | collective-permute-start | bytes 1572872 | tf_op jit(solution)/shard_map/ppermute | solution.py:346
  199.7 37.9 %collective-permute-start.38 = (bf16[512,512]{1,0:T(8,128)(2,1)S(1)}, bf16[512,512]{1,0:T(8,128)(2,1)S(1)}, u32[]{:S(2)}, u32[]{:S(2)}) collective-permute-start(bf16[512,512]{1,0:T(8,128)(2,1)S(1)} %pad_maximum_fusion.8), channel_id=1, source_target_pairs={{0,1},{1,0},{2,3},{3,2},{4,5},{5,4},{6,7},{7,6},{8,9},{9,8},{10,11... | collective-permute-start | bytes 1572872 | tf_op jit(solution)/shard_map/ppermute | solution.py:333
  226.4 14.9 %collective-permute-start.30 = (bf16[512,512]{1,0:T(8,128)(2,1)S(1)}, bf16[512,512]{1,0:T(8,128)(2,1)S(1)}, u32[]{:S(2)}, u32[]{:S(2)}) collective-permute-start(bf16[512,512]{1,0:T(8,128)(2,1)S(1)} %fusion.8), channel_id=1, source_target_pairs={{0,2},{1,3},{2,0},{3,1},{4,6},{5,7},{6,4},{7,5},{8,10},{9,11},{10,... | collective-permute-start | bytes 1572872 | tf_op jit(solution)/shard_map/ppermute | solution.py:346
  233.0 6.5 %collective-permute-start.31 = (bf16[512,512]{1,0:T(8,128)(2,1)S(1)}, bf16[512,512]{1,0:T(8,128)(2,1)S(1)}, u32[]{:S(2)}, u32[]{:S(2)}) collective-permute-start(bf16[512,512]{1,0:T(8,128)(2,1)S(1)} %get-tuple-element.167), channel_id=1, source_target_pairs={{0,1},{1,0},{2,3},{3,2},{4,5},{5,4},{6,7},{7,6},{8,9},{9,8},{10,11... | collective-permute-start | bytes 1572872 | tf_op jit(solution)/shard_map/ppermute | solution.py:333
  234.6 27.3 %collective-permute-start.36 = (bf16[1024,512]{1,0:T(8,128)(2,1)}, bf16[1024,512]{1,0:T(8,128)(2,1)}, u32[]{:S(2)}, u32[]{:S(2)}) collective-permute-start(bf16[1024,512]{1,0:T(8,128)(2,1)} %pad_maximum_fusion.1), channel_id=1, source_target_pairs={{0,1},{1,0},{2,3},{3,2},{4,5},{5,4},{6,7},{7,6},{8,9},{9,8},{10,11... | collective-permute-start | bytes 3145736 | tf_op jit(solution)/shard_map/ppermute | solution.py:333
  254.0 5.5 %collective-permute-start.32 = (bf16[512,512]{1,0:T(8,128)(2,1)}, bf16[512,512]{1,0:T(8,128)(2,1)}, u32[]{:S(2)}, u32[]{:S(2)}) collective-permute-start(bf16[512,512]{1,0:T(8,128)(2,1)} %get-tuple-element.175), channel_id=1, source_target_pairs={{0,1},{1,0},{2,3},{3,2},{4,5},{5,4},{6,7},{7,6},{8,9},{9,8},{10,11... | collective-permute-start | bytes 1572872 | tf_op jit(solution)/shard_map/ppermute | solution.py:333
  255.8 7.9 %collective-permute-start.37 = (bf16[512,512]{1,0:T(8,128)(2,1)}, bf16[512,512]{1,0:T(8,128)(2,1)}, u32[]{:S(2)}, u32[]{:S(2)}) collective-permute-start(bf16[512,512]{1,0:T(8,128)(2,1)} %pad_maximum_fusion.7), channel_id=1, source_target_pairs={{0,1},{1,0},{2,3},{3,2},{4,5},{5,4},{6,7},{7,6},{8,9},{9,8},{10,11... | collective-permute-start | bytes 1572872 | tf_op jit(solution)/shard_map/ppermute | solution.py:333
  267.4 14.8 %collective-permute-start.42 = (bf16[8,64,512]{2,1,0:T(8,128)(2,1)S(1)}, bf16[8,64,512]{2,1,0:T(8,128)(2,1)S(1)}, u32[]{:S(2)}, u32[]{:S(2)}) collective-permute-start(bf16[8,64,512]{2,1,0:T(8,128)(2,1)S(1)} %get-tuple-element.194), channel_id=1, source_target_pairs={{0,4},{4,0},{8,12},{12,8},{16,20},{20,16},{24,28},{28,24},{1,5},{5... | collective-permute-start | bytes 1572872 | tf_op jit(solution)/shard_map/ppermute | solution.py:404
  269.3 18.6 %collective-permute-start.51 = (f32[2,5,512]{2,1,0:T(8,128)S(1)}, f32[2,5,512]{2,1,0:T(8,128)S(1)}, u32[]{:S(2)}, u32[]{:S(2)}) collective-permute-start(f32[2,5,512]{2,1,0:T(8,128)S(1)} %fusion.128), channel_id=1, source_target_pairs={{0,4},{4,0},{8,12},{12,8},{16,20},{20,16},{24,28},{28,24},{1,5},{5... | collective-permute-start | bytes 61448 | tf_op jit(solution)/shard_map/ppermute | solution.py:398
  270.9 31.0 %collective-permute-start.41 = (bf16[8,64,512]{2,1,0:T(8,128)(2,1)S(1)}, bf16[8,64,512]{2,1,0:T(8,128)(2,1)S(1)}, u32[]{:S(2)}, u32[]{:S(2)}) collective-permute-start(bf16[8,64,512]{2,1,0:T(8,128)(2,1)S(1)} %get-tuple-element.192), channel_id=1, source_target_pairs={{0,4},{4,0},{8,12},{12,8},{16,20},{20,16},{24,28},{28,24},{1,5},{5... | collective-permute-start | bytes 1572872 | tf_op jit(solution)/shard_map/ppermute | solution.py:404
  282.4 20.1 %collective-permute-start.43 = (bf16[8,64,512]{2,1,0:T(8,128)(2,1)S(1)}, bf16[8,64,512]{2,1,0:T(8,128)(2,1)S(1)}, u32[]{:S(2)}, u32[]{:S(2)}) collective-permute-start(bf16[8,64,512]{2,1,0:T(8,128)(2,1)S(1)} %fusion.22), channel_id=1, source_target_pairs={{0,8},{4,12},{1,9},{5,13},{2,10},{6,14},{3,11},{7,15}} | collective-permute-start | bytes 1572872 | tf_op jit(solution)/shard_map/ppermute | solution.py:404
  287.1 15.3 %collective-permute-start.44 = (bf16[8,64,512]{2,1,0:T(8,128)(2,1)S(1)}, bf16[8,64,512]{2,1,0:T(8,128)(2,1)S(1)}, u32[]{:S(2)}, u32[]{:S(2)}) collective-permute-start(bf16[8,64,512]{2,1,0:T(8,128)(2,1)S(1)} %fusion.22), channel_id=1, source_target_pairs={{24,16},{28,20},{25,17},{29,21},{26,18},{30,22},{27,19},{31,23}} | collective-permute-start | bytes 1572872 | tf_op jit(solution)/shard_map/ppermute | solution.py:404
  287.9 10.5 %collective-permute-start.52 = (f32[2,5,512]{2,1,0:T(8,128)S(1)}, f32[2,5,512]{2,1,0:T(8,128)S(1)}, u32[]{:S(2)}, u32[]{:S(2)}) collective-permute-start(f32[2,5,512]{2,1,0:T(8,128)S(1)} %fusion.241), channel_id=1, source_target_pairs={{0,8},{4,12},{8,0},{12,4},{16,24},{20,28},{24,16},{28,20},{1,9},{5... | collective-permute-start | bytes 61448 | tf_op jit(solution)/shard_map/ppermute | solution.py:398
  288.0 36.8 %collective-permute-start.34 = (bf16[256,512]{1,0:T(8,128)(2,1)S(1)}, bf16[256,512]{1,0:T(8,128)(2,1)S(1)}, u32[]{:S(2)}, u32[]{:S(2)}) collective-permute-start(bf16[256,512]{1,0:T(8,128)(2,1)S(1)} %select_convert_fusion), channel_id=1, source_target_pairs={{0,2},{1,3},{2,0},{3,1},{4,6},{5,7},{6,4},{7,5},{8,10},{9,11},{10,... | collective-permute-start | bytes 786440 | tf_op jit(solution)/shard_map/ppermute | solution.py:346
  298.4 23.2 %collective-permute-start.53 = (f32[2,5,512]{2,1,0:T(8,128)S(1)}, f32[2,5,512]{2,1,0:T(8,128)S(1)}, u32[]{:S(2)}, u32[]{:S(2)}) collective-permute-start(f32[2,5,512]{2,1,0:T(8,128)S(1)} %add.793), channel_id=1, source_target_pairs={{0,16},{4,20},{8,24},{12,28},{16,0},{20,4},{24,8},{28,12},{1,17},{... | collective-permute-start | bytes 61448 | tf_op jit(solution)/shard_map/ppermute | solution.py:398
  301.9 11.9 %collective-permute-start.45 = (bf16[8,64,512]{2,1,0:T(8,128)(2,1)S(1)}, bf16[8,64,512]{2,1,0:T(8,128)(2,1)S(1)}, u32[]{:S(2)}, u32[]{:S(2)}) collective-permute-start(bf16[8,64,512]{2,1,0:T(8,128)(2,1)S(1)} %get-tuple-element.197), channel_id=1, source_target_pairs={{0,4},{4,0},{8,12},{12,8},{16,20},{20,16},{24,28},{28,24},{1,5},{5... | collective-permute-start | bytes 1572872 | tf_op jit(solution)/shard_map/ppermute | solution.py:404
  303.0 12.2 %collective-permute-start.46 = (bf16[8,64,512]{2,1,0:T(8,128)(2,1)S(1)}, bf16[8,64,512]{2,1,0:T(8,128)(2,1)S(1)}, u32[]{:S(2)}, u32[]{:S(2)}) collective-permute-start(bf16[8,64,512]{2,1,0:T(8,128)(2,1)S(1)} %get-tuple-element.335), channel_id=1, source_target_pairs={{0,8},{4,12},{8,16},{12,20},{1,9},{5,13},{9,17},{13,21},{2,10},{6,... | collective-permute-start | bytes 1572872 | tf_op jit(solution)/shard_map/ppermute | solution.py:404
  304.5 11.2 %collective-permute-start.47 = (bf16[8,64,512]{2,1,0:T(8,128)(2,1)S(1)}, bf16[8,64,512]{2,1,0:T(8,128)(2,1)S(1)}, u32[]{:S(2)}, u32[]{:S(2)}) collective-permute-start(bf16[8,64,512]{2,1,0:T(8,128)(2,1)S(1)} %get-tuple-element.334), channel_id=1, source_target_pairs={{16,8},{20,12},{24,16},{28,20},{17,9},{21,13},{25,17},{29,21},{18,... | collective-permute-start | bytes 1572872 | tf_op jit(solution)/shard_map/ppermute | solution.py:404
  313.8 12.1 %collective-permute-start.33 = (bf16[256,512]{1,0:T(8,128)(2,1)S(1)}, bf16[256,512]{1,0:T(8,128)(2,1)S(1)}, u32[]{:S(2)}, u32[]{:S(2)}) collective-permute-start(bf16[256,512]{1,0:T(8,128)(2,1)S(1)} %select_convert_fusion.1), channel_id=1, source_target_pairs={{0,2},{1,3},{2,0},{3,1},{4,6},{5,7},{6,4},{7,5},{8,10},{9,11},{10,... | collective-permute-start | bytes 786440 | tf_op jit(solution)/shard_map/ppermute | solution.py:346
  315.2 11.6 %collective-permute-start.40 = (bf16[8,64,512]{2,1,0:T(8,128)(2,1)S(1)}, bf16[8,64,512]{2,1,0:T(8,128)(2,1)S(1)}, u32[]{:S(2)}, u32[]{:S(2)}) collective-permute-start(bf16[8,64,512]{2,1,0:T(8,128)(2,1)S(1)} %get-tuple-element.190), channel_id=1, source_target_pairs={{0,4},{4,0},{8,12},{12,8},{16,20},{20,16},{24,28},{28,24},{1,5},{5... | collective-permute-start | bytes 1572872 | tf_op jit(solution)/shard_map/ppermute | solution.py:404
  316.3 13.4 %collective-permute-start.48 = (bf16[8,64,512]{2,1,0:T(8,128)(2,1)S(1)}, bf16[8,64,512]{2,1,0:T(8,128)(2,1)S(1)}, u32[]{:S(2)}, u32[]{:S(2)}) collective-permute-start(bf16[8,64,512]{2,1,0:T(8,128)(2,1)S(1)} %get-tuple-element.333), channel_id=1, source_target_pairs={{0,8},{4,12},{8,16},{12,20},{16,24},{20,28},{1,9},{5,13},{9,17},{1... | collective-permute-start | bytes 1572872 | tf_op jit(solution)/shard_map/ppermute | solution.py:404
  321.6 12.2 %collective-permute-start.49 = (bf16[8,64,512]{2,1,0:T(8,128)(2,1)S(1)}, bf16[8,64,512]{2,1,0:T(8,128)(2,1)S(1)}, u32[]{:S(2)}, u32[]{:S(2)}) collective-permute-start(bf16[8,64,512]{2,1,0:T(8,128)(2,1)S(1)} %get-tuple-element.332), channel_id=1, source_target_pairs={{8,0},{12,4},{16,8},{20,12},{24,16},{28,20},{9,1},{13,5},{17,9},{2... | collective-permute-start | bytes 1572872 | tf_op jit(solution)/shard_map/ppermute | solution.py:404
  (50 other events, 240.1 us)
